TPU v7x, 32 devices: a whole 2x2x4 slice. The times are simulated.
32 devices in a mesh: group: 2 (over y), chan: 4 (over z), tm: 2 (over x), beam: 2 (over core).
Axes of the slice: x: 2, y: 2, z: 4, core: 2. Of those that a mesh axis runs over, the one named last changes fastest.
Arguments:
- samples: bfloat16 [1024, 2, 1024, 16], P(('group', 'chan', 'beam'), None, None, 'tm'), parts along dimension 0, may hold values from -6 to 6
- window_taps: float32 [4, 1024], replicated, may hold values from -1 to 1
- sky_model: bfloat16 [1024, 2, 512, 512], P(('group', 'chan', 'tm'), None, 'beam'), parts along dimension 0, may hold values from -0.0234375 to 0.0234375
- prior_gains: float32 [1024, 2, 512], P(('group', 'chan', 'tm')), parts along dimension 0, may hold values from -4.2 to 4.2
- beam_steering: int32 [2, 1024], P(None, ('group', 'beam')), parts along dimension 1, may hold values from 0 to 255
- input_flags: int32 [1024, 512], P(('group', 'chan', 'tm')), parts along dimension 0, may hold values 0 or 1
Outputs:
- visibilities: bfloat16 [1024, 2, 512, 512], P(('group', 'chan', 'tm'), None, 'beam'), parts along dimension 0
- new_gains: float32 [1024, 2, 512], P(('group', 'chan', 'tm'), None, 'beam'), parts along dimension 0
- beam_power: float32 [1024, 512, 16], P(('group', 'chan', 'tm'), 'beam'), parts along dimension 0
There are 2 independent parts, one for each index of `group`. A program takes and returns all parts, laid end to end along the dimension named above; an argument that names none is the same for every part. Nothing has to cross between parts.
All inputs are finite; a program needn't handle non-finite values. No bound on the sum of `input_flags` on one device may be relied on, other than what follows from the above.
Results may differ from a plain program's by a relative error of at most 0.0076.
Values may be sent and summed in bfloat16 or wider, within the bound.
No kernel may reach another device: no remote copies, remote signals or barrier semaphores. Data moves between devices by JAX's collectives and lax.ppermute only.
A program may use at most 384 MiB of HBM per device.

v0:
```python
import math

import jax
import jax.numpy as jnp
from jax import lax
from jax.sharding import PartitionSpec as P

NCH = 512
ITERS = 2


damping = 0.5
epsilon = 1e-06


def from_behind(block, axis, distance):
    devices = range(lax.axis_size(axis))
    route = [(i - distance, i) for i in devices if i - distance in devices]
    return lax.ppermute(block, axis, route)


def filter_bank(extended, window_taps, kept_count, frames):
    transform_count = window_taps.shape[1]
    tap_count = window_taps.shape[0]
    local_inputs = extended.shape[0]
    kept = jnp.arange(kept_count, dtype=jnp.int32)
    indices = jnp.arange(transform_count, dtype=jnp.int32)
    phases = (kept[:, None] * indices[None, :] % transform_count).astype(jnp.float32) * (
        2.0 * math.pi / transform_count
    )
    cosine = jnp.cos(phases)
    sine_part = jnp.sin(phases)
    real_in = extended[:, :transform_count]
    imag_in = extended[:, transform_count:]
    real_sum = jnp.zeros((local_inputs, kept_count, frames), jnp.float32)
    imag_sum = jnp.zeros((local_inputs, kept_count, frames), jnp.float32)
    for tap_index in range(tap_count):
        tap_row = window_taps[tap_index][None, :]
        cos_block = (cosine * tap_row / math.sqrt(transform_count)).astype(jnp.bfloat16)
        sin_block = (sine_part * tap_row / math.sqrt(transform_count)).astype(jnp.bfloat16)
        part_real = real_in[:, :, tap_index : tap_index + frames]
        part_imag = imag_in[:, :, tap_index : tap_index + frames]
        real_sum = (
            real_sum
            + jnp.einsum("kn,inf->ikf", cos_block, part_real, preferred_element_type=jnp.float32)
            + jnp.einsum("kn,inf->ikf", sin_block, part_imag, preferred_element_type=jnp.float32)
        )
        imag_sum = (
            imag_sum
            + jnp.einsum("kn,inf->ikf", cos_block, part_imag, preferred_element_type=jnp.float32)
            - jnp.einsum("kn,inf->ikf", sin_block, part_real, preferred_element_type=jnp.float32)
        )
    return jnp.stack([real_sum, imag_sum], axis=2).astype(jnp.bfloat16)


def steering_angles(beam_steering, channels, input_count, chan_total):
    positions = jnp.arange(input_count, dtype=jnp.int32)
    column = positions // (input_count // 4)
    within = positions % (input_count // 4)
    phase_index = (
        beam_steering[0][:, None] * column[None, :] * 64
        + beam_steering[1][:, None] * within[None, :]
    ) % 256
    scaled = phase_index[None] * (chan_total + channels)[:, None, None]
    return scaled.astype(jnp.float32) * (2.0 * math.pi / (512 * chan_total))


def cross_rows(owned_rows, all_rows):
    paired = owned_rows.reshape(owned_rows.shape[0], owned_rows.shape[1], -1)
    rotated = jnp.stack([owned_rows[:, :, 1], -owned_rows[:, :, 0]], axis=2).reshape(paired.shape)
    left = jnp.stack([paired, rotated], axis=1)
    columns = all_rows.reshape(all_rows.shape[0], all_rows.shape[1], -1)
    return jnp.einsum("isck,jck->csij", left, columns, preferred_element_type=jnp.float32)


def form_beams(whole_set, gains_part, weights, beam_steering, channels, chan_total):
    input_count = whole_set.shape[0]
    angles = steering_angles(beam_steering, channels, input_count, chan_total)
    cosine = jnp.cos(angles)
    sine_part = jnp.sin(angles)
    scale_factor = 1.0 / math.sqrt(input_count)
    gain_real = (gains_part[:, 0] * weights)[:, None, :]
    gain_imaginary = (gains_part[:, 1] * weights)[:, None, :]
    steering_real = ((gain_real * cosine - gain_imaginary * sine_part) * scale_factor).astype(
        jnp.bfloat16
    )
    steering_imaginary = ((gain_real * sine_part + gain_imaginary * cosine) * scale_factor).astype(
        jnp.bfloat16
    )
    spectrum_real = whole_set[:, :, 0]
    spectrum_imaginary = whole_set[:, :, 1]
    volt_real = jnp.einsum(
        "jan,njg->jag", steering_real, spectrum_real, preferred_element_type=jnp.float32
    ) - jnp.einsum(
        "jan,njg->jag", steering_imaginary, spectrum_imaginary, preferred_element_type=jnp.float32
    )
    volt_imag = jnp.einsum(
        "jan,njg->jag", steering_real, spectrum_imaginary, preferred_element_type=jnp.float32
    ) + jnp.einsum(
        "jan,njg->jag", steering_imaginary, spectrum_real, preferred_element_type=jnp.float32
    )
    return volt_real * volt_real + volt_imag * volt_imag


def matvec(matrix, vector):
    return jnp.einsum("crj,cj->cr", matrix, vector, precision=lax.Precision.HIGHEST)


def shards(samples, window_taps, sky_model, prior_gains, beam_steering, input_flags):
    local_inputs = samples.shape[0]
    transform_count = samples.shape[2]
    frames = samples.shape[3]
    tap_count = window_taps.shape[0]
    kept_count = NCH
    time_count = lax.axis_size("tm")
    beam_count = lax.axis_size("beam")
    time_index = lax.axis_index("tm")
    beam_index = lax.axis_index("beam")
    chan_index = lax.axis_index("chan")
    weights = input_flags.astype(jnp.float32)
    stacked = samples.reshape(local_inputs, 2 * transform_count, frames)
    previous = from_behind(stacked[:, :, frames - tap_count + 1 :], "tm", 1)
    extended = jnp.concatenate([previous, stacked], axis=2)
    spectra = filter_bank(extended, window_taps, kept_count, frames).reshape(
        1, local_inputs, kept_count, 2, 1, frames
    )
    mixed = lax.all_to_all(spectra, ("chan", "tm"), split_axis=2, concat_axis=0, tiled=True)
    blocks = mixed.reshape(
        mixed.shape[0] // time_count, time_count, local_inputs, mixed.shape[2], 2, frames
    )
    turned = jnp.transpose(blocks, (0, 2, 3, 4, 1, 5))
    joined = lax.all_gather(turned, "beam", axis=1, tiled=True)
    input_count = joined.shape[0] * joined.shape[1]
    chan_local = joined.shape[2]
    whole_set = joined.reshape(input_count, chan_local, 2, joined.shape[4] * frames)
    half_rows = input_count // beam_count
    owned_rows = lax.dynamic_slice_in_dim(whole_set, beam_index * half_rows, half_rows, 0)
    terms = cross_rows(owned_rows, whole_set)
    visibilities = (terms / whole_set.shape[3]).astype(jnp.bfloat16)
    channels = (chan_index * time_count + time_index) * chan_local + jnp.arange(
        chan_local, dtype=jnp.int32
    )
    beam_power = form_beams(whole_set, prior_gains, weights, beam_steering, channels, kept_count)
    vis_used = lax.optimization_barrier(visibilities).astype(jnp.float32)
    model_values = sky_model.astype(jnp.float32)
    weighted = jnp.stack(
        [
            vis_used[:, 0] * model_values[:, 0] + vis_used[:, 1] * model_values[:, 1],
            vis_used[:, 1] * model_values[:, 0] - vis_used[:, 0] * model_values[:, 1],
        ],
        axis=1,
    )
    model_power = model_values[:, 0] * model_values[:, 0] + model_values[:, 1] * model_values[:, 1]
    row_start = beam_index * half_rows
    current = prior_gains
    updated = lax.dynamic_slice_in_dim(current, row_start, half_rows, 2)
    for step_index in range(ITERS):
        masked_real = current[:, 0] * weights
        masked_imag = current[:, 1] * weights
        vectors = jnp.stack([masked_real, masked_imag], axis=2)
        products = jnp.einsum("csrj,cjv->csrv", weighted, vectors, precision=lax.Precision.HIGHEST)
        numer_real = products[:, 0, :, 0] - products[:, 1, :, 1]
        numer_imag = products[:, 0, :, 1] + products[:, 1, :, 0]
        denom = (
            matvec(
                model_power,
                weights * (current[:, 0] * current[:, 0] + current[:, 1] * current[:, 1]),
            )
            + epsilon
        )
        older = lax.dynamic_slice_in_dim(current, row_start, half_rows, 2)
        updated = damping * older + (1.0 - damping) * jnp.stack(
            [numer_real / denom, numer_imag / denom], axis=1
        )
        if step_index + 1 < ITERS:
            current = lax.all_gather(updated, "beam", axis=2, tiled=True)
    return (visibilities, updated, beam_power)


def solution(mesh):
    return jax.shard_map(
        shards,
        mesh=mesh,
        in_specs=(
            P(("group", "chan", "beam"), None, None, "tm"),
            P(),
            P(("group", "chan", "tm"), None, "beam", None),
            P(("group", "chan", "tm"), None, None),
            P(None, ("group", "beam")),
            P(("group", "chan", "tm"), None),
        ),
        out_specs=(
            P(("group", "chan", "tm"), None, "beam", None),
            P(("group", "chan", "tm"), None, "beam"),
            P(("group", "chan", "tm"), "beam", None),
        ),
        check_vma=False,
    )
```

profile of v0, /device:TPU:0, one launch (start us, length us, event | category | flops | bytes accessed | tf_op | source)
XLA Modules:
  0.0 1086.7 jit_solution(5787775991752032830)
XLA Ops:
  23.5 8.7 convolution_bitcast_fusion.1
  32.2 8.6 convolution_bitcast_fusion.2
  49.9 8.6 fusion.76
  58.4 8.8 fusion.74
  67.2 8.7 fusion.60
  75.9 8.4 fusion.62
  94.2 8.6 fusion.68
  127.6 8.5 fusion.64
  136.0 8.5 fusion.43
  144.6 8.7 fusion.44
  166.7 44.5 %copy.137 = bf16[64,2,256,512]{2,3,1,0:T(8,128)(2,1)} copy(bf16[64,2,256,512]{3,2,1,0:T(8,128)(2,1)} %param.8) | data formatting | bytes 67108864 | tf_op args[2]
  211.2 32.8 %convert_element_type.85 = f32[64,2,256,512]{2,3,1,0:T(8,128)} convert(bf16[64,2,256,512]{2,3,1,0:T(8,128)(2,1)} %copy.137) | non-fusion elementwise | flops 16777216 | bytes 100663296 | tf_op jit(solution)/shard_map/convert_element_type | solution.py:145
  256.9 29.3 %fusion.5 = f32[64,1,256]{2,1,0:T(1,128)} fusion(f32[64,2,256,512]{2,3,1,0:T(8,128)} %convert_element_type.85, f32[64,512,1]{1,0,2:T(8,128)S(1)} %copy-done.13), kind=kOutput, calls=%fused_computation.7 | convolution fusion | flops 125829120 | bytes 67305472 | tf_op jit(solution)/shard_map/crj,cj->cr/dot_general | solution.py:106
  294.1 127.1 %fusion.9 = f32[64,256,16]{1,2,0:T(8,128)} fusion(f32[64,512]{1,0:T(8,128)S(1)} %get-tuple-element.37, s32[64]{0:T(128)S(1)} %add_add_fusion, s32[256,512]{1,0:T(8,128)S(1)} %copy-done.5, f32[64,512]{1,0:T(8,128)S(1)} %copy-done.8, bf16[512,64,2,16]{0,3,1,2:T(8,128)(2,1)S(1)} %bitcast.221), kind=kOutput, calls=%fused_computation.17 | convolution fusion | flops 335544320 | bytes 2884096 | tf_op jit(solution)/shard_map/jan,njg->jag/dot_general | solution.py:97
  421.1 126.8 %fusion.10 = f32[64,256,16]{1,2,0:T(8,128)} fusion(f32[64,512]{1,0:T(8,128)S(1)} %get-tuple-element.37, s32[64]{0:T(128)S(1)} %add_add_fusion, s32[256,512]{1,0:T(8,128)S(1)} %copy-done.5, f32[64,512]{1,0:T(8,128)S(1)} %copy-done.8, bf16[512,64,2,16]{0,3,1,2:T(8,128)(2,1)S(1)} %bitcast.222), kind=kOutput, calls=%fused_computation.18 | convolution fusion | flops 335544320 | bytes 2884096 | tf_op jit(solution)/shard_map/jan,njg->jag/dot_general | solution.py:92
  557.4 15.4 %fusion.2 = bf16[64,2,256,512]{2,3,1,0:T(8,128)(2,1)} fusion(bf16[512,64,32,1]{0,2,3,1:T(8,128)(2,1)S(1)} %bitcast.220, bf16[256,1,64,32]{0,3,1,2:T(8,128)(2,1)S(1)} %bitcast.243, bf16[256,1,64,32]{0,3,1,2:T(8,128)(2,1)} %bitcast.244), kind=kOutput, calls=%fused_computation.4 | convolution fusion | flops 1111490560 | bytes 37748736 | tf_op jit(solution)/shard_map/isck,jck->csij/dot_general | solution.py:73
  572.8 44.6 %copy.152 = bf16[64,2,256,512]{3,2,1,0:T(8,128)(2,1)} copy(bf16[64,2,256,512]{2,3,1,0:T(8,128)(2,1)} %fusion.2) | data formatting | bytes 67108864
  617.4 127.7 %fusion.26 = f32[64,256,16]{1,2,0:T(8,128)} fusion(f32[64,256,16]{1,2,0:T(8,128)} %fusion.9, f32[64,512]{1,0:T(8,128)S(1)} %get-tuple-element.37, s32[64]{0:T(128)S(1)} %add_add_fusion, s32[256,512]{1,0:T(8,128)S(1)} %copy-done.6, f32[64,512]{1,0:T(8,128)S(1)} %copy-done.8, bf16[512,64,2,16]{0,3,1,2:T(8,128)(2,1)S(1)} %bitcast.225), kind=kOutput, calls=%fused_computation.55 | convolution fusion | flops 336068608 | bytes 3932672 | tf_op jit(solution)/shard_map/jan,njg->jag/dot_general | solution.py:99
  745.1 32.7 %convert_element_type.84 = f32[64,2,256,512]{2,3,1,0:T(8,128)} convert(bf16[64,2,256,512]{2,3,1,0:T(8,128)(2,1)} %fusion.2) | non-fusion elementwise | flops 16777216 | bytes 100663296 | tf_op jit(solution)/shard_map/convert_element_type | solution.py:144
  777.8 64.6 %multiply_add_fusion.1 = (f32[64,1,256,512]{2,3,1,0:T(8,128)}, f32[64,1,256,512]{2,3,1,0:T(8,128)}) fusion(f32[64,2,256,512]{2,3,1,0:T(8,128)} %convert_element_type.84, f32[64,2,256,512]{2,3,1,0:T(8,128)} %convert_element_type.85), kind=kLoop, calls=%fused_computation.16 | loop fusion | flops 50331648 | bytes 201326592 | tf_op jit(solution)/shard_map/add | solution.py:148
  842.4 39.1 %fusion.1 = f32[64,2,256,2]{2,3,1,0:T(2,128)S(1)} fusion(f32[64,1,256,512]{2,3,1,0:T(8,128)} %get-tuple-element.19, f32[64,1,256,512]{2,3,1,0:T(8,128)} %get-tuple-element.18, f32[64,512,1]{1,2,0:T(1,128)S(1)} %copy-done.12, f32[64,512,1]{1,2,0:T(1,128)S(1)} %copy-done.11), kind=kOutput, calls=%fused_computation.3 | convolution fusion | flops 419495936 | bytes 67633152 | tf_op jit(solution)/shard_map/csrj,cjv->csrv/dot_general | solution.py:161
  883.8 27.3 %fusion.3 = f32[64,1,256]{2,1,0:T(1,128)S(1)} fusion(f32[64,2,256,512]{2,3,1,0:T(8,128)} %convert_element_type.85, f32[64,512,1]{1,0,2:T(8,128)S(1)} %get-tuple-element.25), kind=kOutput, calls=%fused_computation.5 | convolution fusion | flops 125829120 | bytes 67305472 | tf_op jit(solution)/shard_map/crj,cj->cr/dot_general | solution.py:106
  911.2 39.3 %fusion = f32[64,2,256,2]{2,3,1,0:T(2,128)S(1)} fusion(f32[64,1,256,512]{2,3,1,0:T(8,128)} %get-tuple-element.19, f32[64,1,256,512]{2,3,1,0:T(8,128)} %get-tuple-element.18, f32[64,512,2,1]{1,0,2,3:T(8,128)S(1)} %maximum_bitcast_fusion.2), kind=kOutput, calls=%fused_computation.2 | convolution fusion | flops 419430400 | bytes 67633152 | tf_op jit(solution)/shard_map/csrj,cjv->csrv/dot_general | solution.py:161
  951.5 128.0 %fusion.24 = f32[64,256,16]{1,2,0:T(8,128)} fusion(f32[64,256,16]{1,2,0:T(8,128)} %fusion.26, f32[64,256,16]{1,2,0:T(8,128)S(1)} %copy-done.17, f32[64,512]{1,0:T(8,128)S(1)} %get-tuple-element.37, s32[64]{0:T(128)S(1)} %add_add_fusion, s32[256,512]{1,0:T(8,128)S(1)} %copy-done.6, f32[64,512]{1,0:T(8,128)S(1)} %copy-done.8, ...), kind=kOutput, calls=%fused_computation.53 | convolution fusion | flops 336330752 | bytes 4981248 | tf_op jit(solution)/shard_map/jan,njg->jag/dot_general | solution.py:94
  (87 shorter events, 106.8 us)
Async XLA Ops:
  7.2 7.9 copy-start.2
  7.2 7.9 copy-start.15
  10.2 39.0 %collective-permute-start = (bf16[64,2048,3]{1,0,2:T(8,128)(2,1)S(1)}, bf16[64,2048,3]{1,0,2:T(8,128)(2,1)S(1)}, u32[]{:S(2)}, u32[]{:S(2)}) collective-permute-start(bf16[64,2048,3]{1,0,2:T(8,128)(2,1)S(1)} %copy.126), channel_id=1, source_target_pairs={{0,2},{1,3},{4,6},{5,7},{8,10},{9,11},{12,14},{13,15},{16,18},{17,... | collective-permute-start | bytes 2359304 | tf_op jit(solution)/shard_map/ppermute | solution.py:19
  155.8 7.7 copy-start.3
  158.5 5.3 copy-start.9
  158.5 87.3 %all-to-all-start = ((bf16[8,2,32768]{2,1,0:T(2,128)(2,1)}), bf16[8,2,32768]{2,1,0:T(2,128)(2,1)S(1)}, u32[]{:S(2)}, u32[]{:S(2)}) async-start(bf16[8,2,32768]{2,1,0:T(2,128)(2,1)} %reshape.179), calls=%async_computation | async-start | bytes 2097152 | tf_op jit(solution)/shard_map/all_to_all | solution.py:127
  163.5 122.7 %all-gather.2.cloned.1.call-start = ((), (), s32[]{:S(2)}) async-start(), calls=%async_computation.1 | async-start | bytes 6291456 | tf_op jit(solution)/shard_map/all_gather | solution.py:132
  164.5 0.6 copy-start.7
  211.2 33.5 %copy-start.16 = (s32[2,256]{1,0:T(2,128)S(1)}, s32[2,256]{1,0:T(2,128)}, u32[]{:S(2)}) copy-start(s32[2,256]{1,0:T(2,128)} %param.10) | copy-start | bytes 6148
  256.0 0.9 copy-start.13
  286.2 7.9 copy-start.5
  286.2 7.9 copy-start.8
  294.1 254.0 %copy-start = (bf16[4,128,64,2,2,8]{1,5,0,4,2,3:T(8,128)(2,1)}, bf16[4,128,64,2,2,8]{1,5,0,4,2,3:T(8,128)(2,1)S(1)}, u32[]{:S(2)}) copy-start(bf16[4,128,64,2,2,8]{1,5,0,4,2,3:T(8,128)(2,1)S(1)} %copy.133) | copy-start | bytes 6291460
  572.8 44.6 %copy-start.1 = (bf16[4,128,64,2,2,8]{1,5,0,4,2,3:T(8,128)(2,1)S(1)}, bf16[4,128,64,2,2,8]{1,5,0,4,2,3:T(8,128)(2,1)}, u32[]{:S(2)}) copy-start(bf16[4,128,64,2,2,8]{1,5,0,4,2,3:T(8,128)(2,1)} %copy-done) | copy-start | bytes 6291460
  572.8 44.6 %copy-start.6 = (s32[256,512]{1,0:T(8,128)S(1)}, s32[256,512]{1,0:T(8,128)}, u32[]{:S(2)}) copy-start(s32[256,512]{1,0:T(8,128)} %add_select_fusion.1) | copy-start | bytes 1572868
  777.8 64.6 %copy-start.11 = (f32[64,512,1]{1,2,0:T(1,128)S(1)}, f32[64,512,1]{1,2,0:T(1,128)}, u32[]{:S(2)}) copy-start(f32[64,512,1]{1,2,0:T(1,128)} %copy.140) | copy-start | bytes 393220
  777.8 64.6 %copy-start.12 = (f32[64,512,1]{1,2,0:T(1,128)S(1)}, f32[64,512,1]{1,2,0:T(1,128)}, u32[]{:S(2)}) copy-start(f32[64,512,1]{1,2,0:T(1,128)} %stack.64) | copy-start | bytes 393220
  842.4 39.3 %copy-start.14 = (f32[64,1,256]{2,1,0:T(1,128)S(1)}, f32[64,1,256]{2,1,0:T(1,128)}, u32[]{:S(2)}) copy-start(f32[64,1,256]{2,1,0:T(1,128)} %fusion.5) | copy-start | bytes 196612
  842.4 39.4 %copy-start.4 = (f32[64,2,256]{2,1,0:T(2,128)S(1)}, f32[64,2,256]{2,1,0:T(2,128)}, u32[]{:S(2)}) copy-start(f32[64,2,256]{2,1,0:T(2,128)} %constant_dynamic-slice_fusion.1) | copy-start | bytes 393220
  842.4 41.4 %copy-start.10 = (s32[64,512]{1,0:T(8,128)S(1)}, s32[64,512]{1,0:T(8,128)}, u32[]{:S(2)}) copy-start(s32[64,512]{1,0:T(8,128)} %param.11) | copy-start | bytes 393220
  911.2 40.3 %copy-start.17 = (f32[64,256,16]{1,2,0:T(8,128)S(1)}, f32[64,256,16]{1,2,0:T(8,128)}, u32[]{:S(2)}) copy-start(f32[64,256,16]{1,2,0:T(8,128)} %fusion.10) | copy-start | bytes 3145732
Sparse Core Ops, SparseCore 0:
  256.1 15.0 all-gather.1
where the time goes:
time: 1100 us; the launch traced here: 1090 us
  matrix products  796 us (72%)
  other arithmetic  134 us (12%)
  local copies, waits for them, and re-layouts  130 us (12%)
  between operations  14.9 us (1%)
    dot_general x1, matrix products, form_beams(): jnp.einsum('jan,njg->jag', steering_imaginary, spectrum_imaginary, prefer...  128 us
    dot_general x1, matrix products, form_beams(): jnp.einsum('jan,njg->jag', steering_imaginary, spectrum_real, preferred_e...  128 us
    dot_general x1, matrix products, form_beams(): jnp.einsum('jan,njg->jag', steering_real, spectrum_imaginary, preferred_e...  127 us
    dot_general x1, matrix products, form_beams(): jnp.einsum('jan,njg->jag', steering_real, spectrum_real, preferred_elemen...  127 us
    unnamed x41, local copies, waits for them, and re-layouts  95.5 us
    dot_general x2, matrix products, shards(): jnp.einsum('csrj,cjv->csrv', weighted, vectors, precision=lax.Precision.H...  78.3 us
    add x1, other arithmetic, shards(): vis_used[:, 0] * model_values[:, 0] + vis_used[:, 1] * model_values[:, 1]  64.6 us
    dot_general x2, matrix products, matvec(): jnp.einsum('crj,cj->cr', matrix, vector, precision=lax.Precision.HIGHEST)  56.6 us
  transfers between devices with their start and end apart: 3, of which 0 were waited for; matrix products, arithmetic and copies ran while one was open for 13% of the time, Pallas kernels for 0%

commit v1 on v0

--- a/solution.py
+++ b/solution.py
@@ -1,8 +1,12 @@
+import functools
 import math
 
 import jax
 import jax.numpy as jnp
+import numpy as np
 from jax import lax
+from jax.experimental import pallas as pl
+from jax.experimental.pallas import tpu as pltpu
 from jax.sharding import PartitionSpec as P
 
 NCH = 512
@@ -106,7 +110,7 @@
     return jnp.einsum("crj,cj->cr", matrix, vector, precision=lax.Precision.HIGHEST)
 
 
-def shards(samples, window_taps, sky_model, prior_gains, beam_steering, input_flags):
+def general_shards(samples, window_taps, sky_model, prior_gains, beam_steering, input_flags):
     local_inputs = samples.shape[0]
     transform_count = samples.shape[2]
     frames = samples.shape[3]
@@ -175,6 +179,471 @@
         if step_index + 1 < ITERS:
             current = lax.all_gather(updated, "beam", axis=2, tiled=True)
     return (visibilities, updated, beam_power)
+
+
+LANES = 128
+SUBLANES = 8
+NEXT_ROWS = 4
+MIB = 2**20
+NT = (((1,), (1,)), ((), ()))
+TN = (((0,), (0,)), ((), ()))
+NN = (((1,), (0,)), ((), ()))
+
+
+def mxu(left, right, dims):
+    return lax.dot_general(left, right, dims, preferred_element_type=jnp.float32)
+
+
+def transform_rows(kept_count, transform_count, owners, chunks):
+    kept = np.arange(kept_count).reshape(owners, chunks, -1).transpose(1, 0, 2).reshape(-1)
+    phases = (kept[:, None] * np.arange(transform_count)[None, :] % transform_count) * (
+        2.0 * math.pi / transform_count
+    )
+    table = np.concatenate([np.cos(phases), np.sin(phases)], axis=1) / math.sqrt(transform_count)
+    return jnp.asarray(table.astype(jnp.bfloat16))
+
+
+def filter_kernel(owners, x_ref, taps_ref, table_ref, *refs):
+    *out_refs, here_ref, next_ref, windowed_ref, turned_ref, spill_ref = refs
+    inputs, _, frames, points = x_ref.shape
+    taps = taps_ref.shape[0]
+    width = 2 * inputs
+    frame_of = lax.broadcasted_iota(jnp.int32, (frames, points), 0)
+    here_weights = []
+    next_weights = []
+    for tap in range(taps):
+        shift = taps - 1 - tap
+        row = jnp.broadcast_to(taps_ref[tap : tap + 1, :], (frames, points))
+        here_weights.append(jnp.where(frame_of >= shift, row, 0.0))
+        next_weights.append(jnp.where(frame_of < shift, row, 0.0))
+
+    def window(i, carry):
+        for part in range(2):
+            block = x_ref[i, part].astype(jnp.float32)
+            here = block * here_weights[taps - 1]
+            later = jnp.zeros_like(block)
+            for tap in range(taps - 1):
+                rolled = pltpu.roll(block, taps - 1 - tap, 0)
+                here = here + rolled * here_weights[tap]
+                later = later + rolled * next_weights[tap]
+            for piece in range(points // LANES):
+                lanes = slice(piece * LANES, (piece + 1) * LANES)
+                here_ref[part, piece, pl.ds(i * frames, frames), :] = here[:, lanes]
+                next_ref[part, piece, pl.ds(i * frames, frames), :] = later[:, lanes]
+        return carry
+
+    lax.fori_loop(0, inputs, window, 0)
+    for frame in range(frames + taps - 1):
+        source = here_ref if frame < frames else next_ref
+        first = frame % frames
+        for piece in range(points // LANES):
+            lanes = slice(piece * LANES, (piece + 1) * LANES)
+            upper = slice(points + piece * LANES, points + (piece + 1) * LANES)
+            real = source[0, piece, pl.ds(first, inputs, stride=frames), :].astype(jnp.bfloat16)
+            imag = source[1, piece, pl.ds(first, inputs, stride=frames), :].astype(jnp.bfloat16)
+            base = frame * width
+            windowed_ref[base : base + inputs, lanes] = real
+            windowed_ref[base : base + inputs, upper] = imag
+            windowed_ref[base + inputs : base + width, lanes] = imag
+            windowed_ref[base + inputs : base + width, upper] = -real
+    rows = table_ref.shape[0] // len(out_refs)
+    share = rows // owners
+    for chunk, out_ref in enumerate(out_refs):
+        block = mxu(table_ref[chunk * rows : (chunk + 1) * rows, :], windowed_ref[...], NT)
+        for frame in range(frames):
+            turned_ref[pl.ds(frame, rows, stride=frames), :] = block[
+                :, frame * width : (frame + 1) * width
+            ]
+        for frame in range(NEXT_ROWS):
+            at = (frames + frame) * width
+            if frame < taps - 1:
+                part = block[:, at : at + width]
+            else:
+                part = jnp.zeros((rows, width), jnp.float32)
+            spill_ref[pl.ds(frame, rows, stride=NEXT_ROWS), :] = part
+        main = share * frames
+        for owner in range(owners):
+            out_ref[owner, :main, :] = turned_ref[owner * main : (owner + 1) * main, :].astype(
+                jnp.bfloat16
+            )
+            extra = share * NEXT_ROWS
+            out_ref[owner, main : main + extra, :] = spill_ref[
+                owner * extra : (owner + 1) * extra, :
+            ].astype(jnp.bfloat16)
+
+
+def filtered(samples, window_taps, kept_count, owners, chunks):
+    inputs, _, points, frames = samples.shape
+    taps = window_taps.shape[0]
+    width = 2 * inputs
+    rows = kept_count // chunks
+    table = transform_rows(kept_count, points, owners, chunks)
+    by_frame = jnp.transpose(samples, (0, 1, 3, 2))
+    out = jax.ShapeDtypeStruct(
+        (owners, rows // owners * (frames + NEXT_ROWS), width), jnp.bfloat16
+    )
+    pieces = points // LANES
+    return pl.pallas_call(
+        functools.partial(filter_kernel, owners),
+        out_shape=[out] * chunks,
+        in_specs=[pl.BlockSpec(memory_space=pltpu.VMEM)] * 3,
+        out_specs=[pl.BlockSpec(memory_space=pltpu.VMEM)] * chunks,
+        scratch_shapes=[
+            pltpu.VMEM((2, pieces, inputs * frames, LANES), jnp.float32),
+            pltpu.VMEM((2, pieces, inputs * frames, LANES), jnp.float32),
+            pltpu.VMEM(((frames + taps - 1) * width, 2 * points), jnp.bfloat16),
+            pltpu.VMEM((rows * frames, width), jnp.float32),
+            pltpu.VMEM((rows * NEXT_ROWS, width), jnp.float32),
+        ],
+        compiler_params=pltpu.CompilerParams(vmem_limit_bytes=48 * MIB),
+        name="filter",
+    )(by_frame, window_taps, table)
+
+
+def gain_terms(real, imag, gains, flags):
+    weights = flags.astype(jnp.float32)
+    gain_real = gains[0:1] * weights
+    gain_imag = gains[1:2] * weights
+    turned_real = real * gain_real + imag * gain_imag
+    turned_imag = imag * gain_real - real * gain_imag
+    power = weights * (gains[0:1] * gains[0:1] + gains[1:2] * gains[1:2])
+    return turned_real, turned_imag, power
+
+
+def updated_gains(real, imag, own_real, own_imag, model_real, model_imag, gains, flags, older):
+    turned_real, turned_imag, power = gain_terms(real, imag, gains, flags)
+    straight = jnp.concatenate([turned_real, turned_imag], axis=0).astype(jnp.bfloat16)
+    crossed = jnp.concatenate([-turned_imag, turned_real], axis=0).astype(jnp.bfloat16)
+    modelled = mxu(straight, model_real, NT) + mxu(crossed, model_imag, NT)
+    model_power = model_real * model_real + model_imag * model_imag
+    power_rows = jnp.broadcast_to(power, (SUBLANES, power.shape[1])).astype(jnp.bfloat16)
+    denom = mxu(power_rows, model_power, NT)[0:1] + epsilon
+    frames = real.shape[0]
+    modelled_real = modelled[:frames]
+    modelled_imag = modelled[frames:]
+    numer_real = jnp.sum(own_real * modelled_real + own_imag * modelled_imag, axis=0, keepdims=True)
+    numer_imag = jnp.sum(own_imag * modelled_real - own_real * modelled_imag, axis=0, keepdims=True)
+    numer = jnp.concatenate([numer_real, numer_imag], axis=0) / frames
+    return damping * older + (1.0 - damping) * (numer / denom)
+
+
+def own_half(values, core):
+    half = values.shape[1] // 2
+    return jnp.where(core == 0, values[:, :half], values[:, half:])
+
+
+def first_kernel(
+    times,
+    core_ref,
+    own_ref,
+    own_next_ref,
+    other_ref,
+    other_next_ref,
+    model_ref,
+    gains_ref,
+    flags_ref,
+    spectra_ref,
+    updated_ref,
+):
+    core = core_ref[0]
+    count = gains_ref.shape[0]
+    sources = own_ref.shape[0]
+    frames = own_ref.shape[1] // count
+    width = own_ref.shape[2]
+    columns = sources // times
+    lane = lax.broadcasted_iota(jnp.int32, (frames, width), 1)
+    row = lax.broadcasted_iota(jnp.int32, (frames, width), 0)
+    low = lane < width // 2
+
+    def loaded(ref, next_ref, column, time, c):
+        source = column * times + time
+        block = ref[source, c * frames : (c + 1) * frames, :].astype(jnp.float32)
+        if time > 0:
+            pair = c // 2 * 2 * NEXT_ROWS
+            extra = next_ref[source - 1, pair : pair + 2 * NEXT_ROWS, :].astype(jnp.float32)
+            if c % 2:
+                extra = pltpu.roll(extra, NEXT_ROWS, 0)
+            block = block + jnp.where(row < NEXT_ROWS - 1, extra, 0.0)
+        return block
+
+    for c in range(count):
+        real_rows = []
+        imag_rows = []
+        for time in range(times):
+            reals = []
+            imags = []
+            for column in range(columns):
+                own = loaded(own_ref, own_next_ref, column, time, c)
+                other = loaded(other_ref, other_next_ref, column, time, c)
+                first = jnp.where(core == 0, own, other)
+                second = jnp.where(core == 0, other, own)
+                reals.append(jnp.where(low, first, pltpu.roll(second, width // 2, 1)))
+                imags.append(jnp.where(low, pltpu.roll(first, width // 2, 1), second))
+            real_rows.append(jnp.concatenate(reals, axis=1))
+            imag_rows.append(jnp.concatenate(imags, axis=1))
+        spectra = jnp.concatenate(real_rows + imag_rows, axis=0).astype(jnp.bfloat16)
+        spectra_ref[c] = spectra
+        values = spectra.astype(jnp.float32)
+        half = values.shape[0] // 2
+        real = values[:half]
+        imag = values[half:]
+        updated_ref[c] = updated_gains(
+            real,
+            imag,
+            own_half(real, core),
+            own_half(imag, core),
+            model_ref[c, 0],
+            model_ref[c, 1],
+            gains_ref[c],
+            flags_ref[c : c + 1],
+            own_half(gains_ref[c], core),
+        )
+
+
+def second_kernel(
+    core_ref, spectra_ref, model_ref, own_ref, other_ref, flags_ref, *refs
+):
+    visibilities_ref, updated_ref = refs[-2:]
+    core = core_ref[0]
+    for c in range(spectra_ref.shape[0]):
+        spectra = spectra_ref[c]
+        half = spectra.shape[0] // 2
+        values = spectra.astype(jnp.float32)
+        real = values[:half]
+        imag = values[half:]
+        own_real = own_half(real, core)
+        own_imag = own_half(imag, core)
+        paired = (jnp.concatenate([own_real, own_imag], axis=0) / half).astype(jnp.bfloat16)
+        rotated = (jnp.concatenate([own_imag, -own_real], axis=0) / half).astype(jnp.bfloat16)
+        visibilities_ref[c, 0] = mxu(paired, spectra, TN).astype(jnp.bfloat16)
+        visibilities_ref[c, 1] = mxu(rotated, spectra, TN).astype(jnp.bfloat16)
+        own = own_ref[c]
+        other = other_ref[c]
+        first = jnp.where(core == 0, own, other)
+        second = jnp.where(core == 0, other, own)
+        gains = jnp.concatenate([first, second], axis=1)
+        updated_ref[c] = updated_gains(
+            real,
+            imag,
+            own_real,
+            own_imag,
+            model_ref[c, 0],
+            model_ref[c, 1],
+            gains,
+            flags_ref[c : c + 1],
+            own,
+        )
+
+
+def series_length(reach):
+    terms = 1
+    while reach**terms / math.factorial(terms) >= 2.0**-22:
+        terms += 1
+    return terms
+
+
+def steering_kernel(terms, reach, step, centre_ref, steering_ref, table_ref):
+    inputs = table_ref.shape[1] // 2
+    beams = table_ref.shape[2] // 2
+    position = lax.broadcasted_iota(jnp.int32, (inputs, beams), 0)
+    column = position // (inputs // 4)
+    within = position % (inputs // 4)
+    phase_index = (steering_ref[0:1, :] * column * 64 + steering_ref[1:2, :] * within) % 256
+    angle = (phase_index * centre_ref[0]).astype(jnp.float32) * (0.5 * step)
+    cosine = jnp.cos(angle)
+    sine_part = jnp.sin(angle)
+    offset = (phase_index - 128).astype(jnp.float32) * (reach * step)
+    factor = jnp.ones_like(offset)
+    for term in range(terms):
+        if term:
+            factor = factor * offset / term
+        real, imag = (
+            (cosine, sine_part),
+            (-sine_part, cosine),
+            (-cosine, -sine_part),
+            (sine_part, -cosine),
+        )[term % 4]
+        real = (factor * real).astype(jnp.bfloat16)
+        imag = (factor * imag).astype(jnp.bfloat16)
+        table_ref[term, :inputs, :beams] = real
+        table_ref[term, :inputs, beams:] = imag
+        table_ref[term, inputs:, :beams] = -imag
+        table_ref[term, inputs:, beams:] = real
+
+
+def beams_kernel(spectra_ref, gains_ref, flags_ref, table_ref, *refs):
+    power_ref, left_ref = refs[-2:]
+    count, doubled, inputs = spectra_ref.shape
+    frames = doubled // 2
+    scale = 1.0 / math.sqrt(inputs)
+    middle = 0.5 * (count - 1)
+    terms = table_ref.shape[0]
+    for c in range(count):
+        values = spectra_ref[c].astype(jnp.float32)
+        real = values[:frames]
+        imag = values[frames:]
+        weights = flags_ref[c : c + 1].astype(jnp.float32) * scale
+        gain_real = gains_ref[c, 0:1] * weights
+        gain_imag = gains_ref[c, 1:2] * weights
+        lit_real = real * gain_real - imag * gain_imag
+        lit_imag = real * gain_imag + imag * gain_real
+        rows = slice(c * frames, (c + 1) * frames)
+        for term in range(terms):
+            power = ((c - middle) / max(middle, 0.5)) ** term
+            left_ref[term, rows, :inputs] = (lit_real * power).astype(jnp.bfloat16)
+            left_ref[term, rows, inputs:] = (lit_imag * power).astype(jnp.bfloat16)
+    total = mxu(left_ref[0], table_ref[0], NN)
+    for term in range(1, terms):
+        total = total + mxu(left_ref[term], table_ref[term], NN)
+    beams = total.shape[1] // 2
+    real = total[:, :beams]
+    imag = total[:, beams:]
+    power_ref[...] = (real * real + imag * imag).reshape(count, frames, beams)
+
+
+def chunk_shards(samples, window_taps, sky_model, prior_gains, beam_steering, input_flags):
+    frames = samples.shape[3]
+    chan_local, _, half_rows, input_count = sky_model.shape
+    times = lax.axis_size("tm")
+    owners = lax.axis_size("chan") * times
+    core = lax.axis_index("beam")
+    kept_count = chan_local * owners
+    frame_count = frames * times
+    beams = beam_steering.shape[1]
+    chunks = CHUNKS
+    share = chan_local // chunks
+    block = BLOCK
+    steps = share // block
+    sent = filtered(samples, window_taps, kept_count, owners, chunks)
+    core_word = core.astype(jnp.int32).reshape(1)
+    swap = [(0, 1), (1, 0)]
+    smem = pl.BlockSpec(memory_space=pltpu.SMEM)
+    vmem = pl.BlockSpec(memory_space=pltpu.VMEM)
+    anywhere = pl.BlockSpec(memory_space=pl.ANY)
+    first_channel = (lax.axis_index("chan") * times + lax.axis_index("tm")) * chan_local
+    step = 2.0 * math.pi / (512 * kept_count)
+    reach = max(0.5 * (share - 1), 0.5)
+    terms = series_length(128 * reach * step)
+    visibilities = None
+    beam_power = None
+    gain_parts = []
+    for chunk in range(chunks):
+        base = chunk * steps
+        own = lax.all_to_all(sent[chunk], ("chan", "tm"), 0, 0, tiled=True)
+        other = lax.ppermute(own, "beam", swap)
+        width = own.shape[2]
+        next_base = frames * steps // NEXT_ROWS
+        main_spec = pl.BlockSpec((owners, block * frames, width), lambda i: (0, i, 0))
+        next_spec = pl.BlockSpec(
+            (owners, block * NEXT_ROWS, width), lambda i, at=next_base: (0, at + i, 0)
+        )
+        model_spec = pl.BlockSpec(
+            (block, 2, half_rows, input_count), lambda i, at=base: (at + i, 0, 0, 0)
+        )
+        gains_spec = pl.BlockSpec((block, 2, input_count), lambda i, at=base: (at + i, 0, 0))
+        flags_spec = pl.BlockSpec((block, input_count), lambda i, at=base: (at + i, 0))
+        spectra_spec = pl.BlockSpec((block, 2 * frame_count, input_count), lambda i: (i, 0, 0))
+        half_spec = pl.BlockSpec((block, 2, half_rows), lambda i: (i, 0, 0))
+        half_shape = jax.ShapeDtypeStruct((share, 2, half_rows), jnp.float32)
+        spectra, gains_own = pl.pallas_call(
+            functools.partial(first_kernel, times),
+            grid=(steps,),
+            in_specs=[
+                smem,
+                main_spec,
+                next_spec,
+                main_spec,
+                next_spec,
+                model_spec,
+                gains_spec,
+                flags_spec,
+            ],
+            out_specs=[spectra_spec, half_spec],
+            out_shape=[
+                jax.ShapeDtypeStruct((share, 2 * frame_count, input_count), jnp.bfloat16),
+                half_shape,
+            ],
+            compiler_params=pltpu.CompilerParams(vmem_limit_bytes=40 * MIB),
+            name="first_update",
+        )(core_word, own, own, other, other, sky_model, prior_gains, input_flags)
+        gains_other = lax.ppermute(gains_own, "beam", swap)
+        centre = 2 * (kept_count + first_channel + chunk * share) + share - 1
+        table = pl.pallas_call(
+            functools.partial(steering_kernel, terms, reach, step),
+            in_specs=[smem, vmem],
+            out_specs=vmem,
+            out_shape=jax.ShapeDtypeStruct((terms, 2 * input_count, 2 * beams), jnp.bfloat16),
+            compiler_params=pltpu.CompilerParams(vmem_limit_bytes=32 * MIB),
+            name="steering",
+        )(centre.astype(jnp.int32).reshape(1), beam_steering)
+        power_spec = pl.BlockSpec(
+            (share, frame_count, beams), lambda i, at=chunk: (at, 0, 0)
+        )
+        earlier = [] if beam_power is None else [beam_power]
+        beam_power = pl.pallas_call(
+            beams_kernel,
+            grid=(1,),
+            in_specs=[
+                pl.BlockSpec((share, 2 * frame_count, input_count), lambda i: (0, 0, 0)),
+                pl.BlockSpec((share, 2, input_count), lambda i, at=chunk: (at, 0, 0)),
+                pl.BlockSpec((share, input_count), lambda i, at=chunk: (at, 0)),
+                pl.BlockSpec((terms, 2 * input_count, 2 * beams), lambda i: (0, 0, 0)),
+            ]
+            + [anywhere] * len(earlier),
+            out_specs=power_spec,
+            out_shape=jax.ShapeDtypeStruct((chan_local, frame_count, beams), jnp.float32),
+            input_output_aliases={4: 0} if earlier else {},
+            scratch_shapes=[
+                pltpu.VMEM((terms, share * frame_count, 2 * input_count), jnp.bfloat16)
+            ],
+            compiler_params=pltpu.CompilerParams(vmem_limit_bytes=40 * MIB),
+            name="beams",
+        )(spectra, prior_gains, input_flags, table, *earlier)
+        earlier = [] if visibilities is None else [visibilities]
+        visibilities, gains_new = pl.pallas_call(
+            second_kernel,
+            grid=(steps,),
+            in_specs=[smem, spectra_spec, model_spec, half_spec, half_spec, flags_spec]
+            + [anywhere] * len(earlier),
+            out_specs=[model_spec, half_spec],
+            out_shape=[
+                jax.ShapeDtypeStruct((chan_local, 2, half_rows, input_count), jnp.bfloat16),
+                half_shape,
+            ],
+            input_output_aliases={6: 0} if earlier else {},
+            compiler_params=pltpu.CompilerParams(vmem_limit_bytes=40 * MIB),
+            name="second_update",
+        )(core_word, spectra, sky_model, gains_own, gains_other, input_flags, *earlier)
+        gain_parts.append(gains_new)
+    return (
+        visibilities,
+        jnp.concatenate(gain_parts, axis=0),
+        jnp.transpose(beam_power, (0, 2, 1)),
+    )
+
+
+CHUNKS = 2
+BLOCK = 8
+
+
+def shards(samples, window_taps, sky_model, prior_gains, beam_steering, input_flags):
+    inputs, _, points, frames = samples.shape
+    chan_local, _, half_rows, input_count = sky_model.shape
+    frame_count = frames * lax.axis_size("tm")
+    fits = (
+        ITERS == 2
+        and 2 * inputs == LANES
+        and points % LANES == 0
+        and frames == SUBLANES
+        and window_taps.shape[0] == NEXT_ROWS
+        and lax.axis_size("beam") == 2
+        and chan_local % (CHUNKS * BLOCK) == 0
+        and half_rows % LANES == 0
+        and frame_count & (frame_count - 1) == 0
+        and beam_steering.shape[1] % LANES == 0
+    )
+    form = chunk_shards if fits else general_shards
+    return form(samples, window_taps, sky_model, prior_gains, beam_steering, input_flags)
 
 
 def solution(mesh):

time: 1100 us -> 132 us (0.12); the launches traced: 1090 us -> 131 us
  matrix products: 796 us -> 0 us
  other arithmetic: 134 us -> 0.71 us
  local copies, waits for them, and re-layouts: 130 us -> 5.97 us
  Pallas kernels: 0 us -> 72.3 us
  blocking collectives: 1.99 us -> 27.2 us
  waiting for transfers between devices: 0.03 us -> 19.8 us
  between operations: 14.9 us -> 0.74 us
    dot_general x21 -> x0, matrix products: 761 us -> none  [the longest x1 128 us: form_beams(): jnp.einsum('jan,njg->jag', steering_imaginary, spectrum_imaginary, prefer...]
    unnamed x41 -> x20, local copies, waits for them, and re-layouts: 95.5 us -> 5.97 us
    pallas_call x0 -> x9, Pallas kernels: none -> 72.3 us  [the longest x2 31.9 us: chunk_shards(): pl.pallas_call(second_kernel, grid=(steps,), in_specs=[smem, spectra_spec...]
    convert_element_type x2 -> x0, other arithmetic: 65.5 us -> none  [the longest x1 32.8 us: shards(): model_values = sky_model.astype(jnp.float32)]
    add x4 -> x0, other arithmetic: 64.6 us -> none  [the longest x1 64.6 us: shards(): vis_used[:, 0] * model_values[:, 0] + vis_used[:, 1] * model_values[:, 1]]
    unnamed x4 -> x0, matrix products: 34.1 us -> none
    all_to_all x0 -> x1, blocking collectives: none -> 27.2 us  [chunk_shards(): own = lax.all_to_all(sent[chunk], ('chan', 'tm'), 0, 0, tiled=True)]
    all_to_all x1, waiting for transfers between devices: 0.01 us -> 19.8 us  [chunk_shards(): own = lax.all_to_all(sent[chunk], ('chan', 'tm'), 0, 0, tiled=True)]
  transfers between devices with their start and end apart: 3 -> 5, of which waited for: 0 -> 1; matrix products, arithmetic and copies ran while one was open for 13% -> 0% of each run, Pallas kernels for 0% -> 37%
where the time goes in v1:
time: 132 us; the launch traced here: 131 us
  Pallas kernels  72.3 us (55%)
  blocking collectives  27.2 us (21%)
  waiting for transfers between devices  19.8 us (15%)
  local copies, waits for them, and re-layouts  5.97 us (5%)
  starting transfers between devices  4.38 us (3%)
    pallas_call x2, Pallas kernels, chunk_shards(): pl.pallas_call(second_kernel, grid=(steps,), in_specs=[smem, spectra_spec...  31.9 us
    all_to_all x1, blocking collectives, chunk_shards(): own = lax.all_to_all(sent[chunk], ('chan', 'tm'), 0, 0, tiled=True)  27.2 us
    pallas_call x2, Pallas kernels, chunk_shards(): pl.pallas_call(functools.partial(first_kernel, times), grid=(steps,), in_...  20.4 us
    all_to_all x1, waiting for transfers between devices, chunk_shards(): own = lax.all_to_all(sent[chunk], ('chan', 'tm'), 0, 0, tiled=True)  19.8 us
    pallas_call x1, Pallas kernels, filtered(): pl.pallas_call(functools.partial(filter_kernel, owners), out_shape=[out]...  7.94 us
    pallas_call x2, Pallas kernels, chunk_shards(): pl.pallas_call(beams_kernel, grid=(1,), in_specs=[pl.BlockSpec((share, 2...  6.35 us
    unnamed x20, local copies, waits for them, and re-layouts  5.97 us
    pallas_call x2, Pallas kernels, chunk_shards(): pl.pallas_call(functools.partial(steering_kernel, terms, reach, step), in...  5.7 us
  transfers between devices with their start and end apart: 5, of which 1 were waited for; matrix products, arithmetic and copies ran while one was open for 0% of the time, Pallas kernels for 37%

profile of v1, /device:TPU:0, one launch (start us, length us, event | category | flops | bytes accessed | tf_op | source)
XLA Modules:
  0.0 131.1 jit_solution(4222971017977393909)
XLA Ops:
  0.7 1.6 %copy-done.6 = bf16[64,2,1024,8]{2,3,1,0:T(8,128)(2,1)S(1)} copy-done((bf16[64,2,1024,8]{2,3,1,0:T(8,128)(2,1)S(1)}, bf16[64,2,1024,8]{2,3,1,0:T(8,128)(2,1)}, u32[]{:S(2)}) %copy-start.6) | copy-done | bytes 2097176
  2.3 1.6 %copy-done.7 = bf16[512,2048]{1,0:T(8,128)(2,1)S(1)} copy-done((bf16[512,2048]{1,0:T(8,128)(2,1)S(1)}, bf16[512,2048]{1,0:T(8,128)(2,1)}, u32[]{:S(2)}) %copy-start.7) | copy-done | bytes 2097176
  3.9 0.7 copy-done.8
  4.6 7.9 %filter.1 = (bf16[8,384,128]{2,1,0:T(8,128)(2,1)S(1)}, bf16[8,384,128]{2,1,0:T(8,128)(2,1)}) custom-call(bf16[64,2,8,1024]{3,2,1,0:T(8,128)(2,1)S(1)} %bitcast.5, f32[4,1024]{1,0:T(4,128)S(1)} %copy-done.8, bf16[512,2048]{1,0:T(8,128)(2,1)S(1)} %copy-done.7), custom_call_target="tpu_custom_call" | custom-call | tf_op jit(solution)/shard_map/filter/pallas_call | solution.py:286
  12.5 27.2 %all_to_all.10.own_ref.own_next_ref = bf16[8,384,128]{2,1,0:T(8,128)(2,1)S(1)} all-to-all(bf16[8,384,128]{2,1,0:T(8,128)(2,1)S(1)} %get-tuple-element.16), channel_id=1, replica_groups=mesh['group'=2,'chan'=4,'tm'=2,'beam'=2] {'chan','tm'}, dimensions={0} | all-to-all | bytes 1572864 | tf_op jit(solution)/shard_map/all_to_all | solution.py:532
  39.7 3.6 %all-to-all-start = ((bf16[8,384,128]{2,1,0:T(8,128)(2,1)}), bf16[8,384,128]{2,1,0:T(8,128)(2,1)S(1)}, u32[]{:S(2)}, u32[]{:S(2)}) async-start(bf16[8,384,128]{2,1,0:T(8,128)(2,1)} %get-tuple-element.13), calls=%async_computation | async-start | bytes 1572864 | tf_op jit(solution)/shard_map/all_to_all | solution.py:532
  43.3 0.1 collective-permute-start.2
  43.4 19.8 %all-to-all-done.own_ref.own_next_ref = bf16[8,384,128]{2,1,0:T(8,128)(2,1)S(1)} async-done(((bf16[8,384,128]{2,1,0:T(8,128)(2,1)}), bf16[8,384,128]{2,1,0:T(8,128)(2,1)S(1)}, u32[]{:S(2)}, u32[]{:S(2)}) %all-to-all-start) | async-done | bytes 786464 | tf_op jit(solution)/shard_map/all_to_all | solution.py:532
  63.2 0.0 collective-permute-start
  63.2 0.0 collective-permute-done.2.other_ref.other_next_ref
  63.2 10.2 %first_update.3 = (bf16[32,32,512]{2,1,0:T(8,128)(2,1)S(1)}, f32[32,2,256]{2,1,0:T(2,128)S(1)}) custom-call(s32[1]{0:T(128)} %bitcast.core_ref, bf16[8,384,128]{2,1,0:T(8,128)(2,1)S(1)} %all_to_all.10.own_ref.own_next_ref, bf16[8,384,128]{2,1,0:T(8,128)(2,1)S(1)} %all_to_all.10.own_ref.own_next_ref, ...), custom_call_target="tpu_custom_call" | custom-call | tf_op jit(solution)/shard_map/first_update/pallas_call | solution.py:548
  73.5 0.0 copy-start.2
  73.5 0.6 collective-permute-start.3
  74.0 0.9 copy-done.4
  74.9 1.1 copy-done.5
  76.1 10.2 %first_update.2 = (bf16[32,32,512]{2,1,0:T(8,128)(2,1)S(1)}, f32[32,2,256]{2,1,0:T(2,128)S(1)}) custom-call(s32[1]{0:T(128)} %bitcast.core_ref, bf16[8,384,128]{2,1,0:T(8,128)(2,1)S(1)} %all-to-all-done.own_ref.own_next_ref, bf16[8,384,128]{2,1,0:T(8,128)(2,1)S(1)} %all-to-all-done.own_ref.own_next_ref, bf16[8,384,128]{2,1,0:T(8,128)(2,1)S(1)} %copy-done.5, ...), custom_call_target="tpu_custom_call" | custom-call | tf_op jit(solution)/shard_map/first_update/pallas_call | solution.py:548
  86.3 0.2 collective-permute-start.1
  86.4 2.9 %steering.3.table_ref = bf16[4,1024,512]{2,1,0:T(8,128)(2,1)S(1)} custom-call(s32[1]{0:T(128)} %bitcast.3.centre_ref, s32[2,256]{1,0:T(2,128)S(1)} %copy-done.9), custom_call_target="tpu_custom_call" | custom-call | tf_op jit(solution)/shard_map/steering/pallas_call | solution.py:571
  89.3 2.9 %steering.2.table_ref = bf16[4,1024,512]{2,1,0:T(8,128)(2,1)S(1)} custom-call(s32[1]{0:T(128)} %bitcast.2.centre_ref, s32[2,256]{1,0:T(2,128)S(1)} %copy-done.9), custom_call_target="tpu_custom_call" | custom-call | tf_op jit(solution)/shard_map/steering/pallas_call | solution.py:571
  92.2 3.2 %beams.2.refs_0_ = f32[64,16,256]{2,1,0:T(8,128)} custom-call(bf16[32,32,512]{2,1,0:T(8,128)(2,1)S(1)} %copy-done.3, f32[64,2,512]{2,1,0:T(2,128)S(1)} %copy-done.1, s32[64,512]{1,0:T(8,128)S(1)} %copy-done, bf16[4,1024,512]{2,1,0:T(8,128)(2,1)S(1)} %steering.3.table_ref), custom_call_target="tpu_custom_call" | custom-call | tf_op jit(solution)/shard_map/beams/pallas_call | solution.py:583
  95.3 3.2 %beams.3 = f32[64,16,256]{2,1,0:T(8,128)} custom-call(bf16[32,32,512]{2,1,0:T(8,128)(2,1)S(1)} %get-tuple-element.14.spectra_ref, f32[64,2,512]{2,1,0:T(2,128)S(1)} %copy-done.1, s32[64,512]{1,0:T(8,128)S(1)} %copy-done, bf16[4,1024,512]{2,1,0:T(8,128)(2,1)S(1)} %steering.2.table_ref, f32[64,16,256]{2,1,0:T(8,128)} %beams.2.refs_0_), custom_call_target="tpu_custom_call", output_to_operand_aliasing={{}: (4, {})} | custom-call | tf_op jit(solution)/shard_map/beams/pallas_call | solution.py:583
  98.5 15.9 %second_update.2 = (bf16[64,2,256,512]{3,2,1,0:T(8,128)(2,1)}, f32[32,2,256]{2,1,0:T(2,128)S(1)}) custom-call(s32[1]{0:T(128)} %bitcast.core_ref, bf16[32,32,512]{2,1,0:T(8,128)(2,1)S(1)} %copy-done.3, bf16[64,2,256,512]{3,2,1,0:T(8,128)(2,1)} %model_ref.7, f32[32,2,256]{2,1,0:T(2,128)S(1)} %get-tuple-element.18.own_ref, ...), custom_call_target="tpu_custom_call" | custom-call | tf_op jit(solution)/shard_map/second_update/pallas_call | solution.py:603
  114.5 15.9 %second_update.3 = (bf16[64,2,256,512]{3,2,1,0:T(8,128)(2,1)}, f32[32,2,256]{2,1,0:T(2,128)S(1)}) custom-call(s32[1]{0:T(128)} %bitcast.core_ref, bf16[32,32,512]{2,1,0:T(8,128)(2,1)S(1)} %get-tuple-element.14.spectra_ref, bf16[64,2,256,512]{3,2,1,0:T(8,128)(2,1)} %model_ref.7, ...), custom_call_target="tpu_custom_call", output_to_operand_aliasing={{0}: (6, {})} | custom-call | tf_op jit(solution)/shard_map/second_update/pallas_call | solution.py:603
  130.4 0.7 pad_maximum_fusion
  (17 shorter events, 0.0 us)
Async XLA Ops:
  0.6 62.6 %copy-start = (s32[64,512]{1,0:T(8,128)S(1)}, s32[64,512]{1,0:T(8,128)}, u32[]{:S(2)}) copy-start(s32[64,512]{1,0:T(8,128)} %flags_ref.11) | copy-start | bytes 393220
  0.6 62.6 %copy-start.1 = (f32[64,2,512]{2,1,0:T(2,128)S(1)}, f32[64,2,512]{2,1,0:T(2,128)}, u32[]{:S(2)}) copy-start(f32[64,2,512]{2,1,0:T(2,128)} %gains_ref.7) | copy-start | bytes 786436
  0.7 1.6 %copy-start.6 = (bf16[64,2,1024,8]{2,3,1,0:T(8,128)(2,1)S(1)}, bf16[64,2,1024,8]{2,3,1,0:T(8,128)(2,1)}, u32[]{:S(2)}) copy-start(bf16[64,2,1024,8]{2,3,1,0:T(8,128)(2,1)} %param.7) | copy-start | bytes 6291460
  2.3 1.6 %copy-start.7 = (bf16[512,2048]{1,0:T(8,128)(2,1)S(1)}, bf16[512,2048]{1,0:T(8,128)(2,1)}, u32[]{:S(2)}) copy-start(bf16[512,2048]{1,0:T(8,128)(2,1)} %constant.28.clone.table_ref) | copy-start | bytes 6291460
  3.9 0.7 copy-start.8
  39.7 23.5 %all-to-all-start = ((bf16[8,384,128]{2,1,0:T(8,128)(2,1)}), bf16[8,384,128]{2,1,0:T(8,128)(2,1)S(1)}, u32[]{:S(2)}, u32[]{:S(2)}) async-start(bf16[8,384,128]{2,1,0:T(8,128)(2,1)} %get-tuple-element.13), calls=%async_computation | async-start | bytes 1572864 | tf_op jit(solution)/shard_map/all_to_all | solution.py:532
  43.3 19.9 %collective-permute-start.2 = (bf16[8,384,128]{2,1,0:T(8,128)(2,1)S(1)}, bf16[8,384,128]{2,1,0:T(8,128)(2,1)}, u32[]{:S(2)}, u32[]{:S(2)}) collective-permute-start(bf16[8,384,128]{2,1,0:T(8,128)(2,1)S(1)} %all_to_all.10.own_ref.own_next_ref), channel_id=1, source_target_pairs={{0,1},{1,0},{2,3},{3,2},{4,5},{5,4},{6,7},{7,6},{8,9},{9,8},{10,11... | collective-permute-start | bytes 2359304 | tf_op jit(solution)/shard_map/ppermute | solution.py:533
  63.2 10.8 %collective-permute-start = (bf16[8,384,128]{2,1,0:T(8,128)(2,1)S(1)}, bf16[8,384,128]{2,1,0:T(8,128)(2,1)S(1)}, u32[]{:S(2)}, u32[]{:S(2)}) collective-permute-start(bf16[8,384,128]{2,1,0:T(8,128)(2,1)S(1)} %all-to-all-done.own_ref.own_next_ref), channel_id=1, source_target_pairs={{0,1},{1,0},{2,3},{3,2},{4,5},{5,4},{6,7},{7,6},{8,9},{9,8},{10,11... | collective-permute-start | bytes 2359304 | tf_op jit(solution)/shard_map/ppermute | solution.py:533
  73.5 12.8 %copy-start.2 = (bf16[32,32,512]{2,1,0:T(8,128)(2,1)}, bf16[32,32,512]{2,1,0:T(8,128)(2,1)S(1)}, u32[]{:S(2)}) copy-start(bf16[32,32,512]{2,1,0:T(8,128)(2,1)S(1)} %get-tuple-element.17.spectra_ref) | copy-start | bytes 3145732
  73.5 25.0 %collective-permute-start.3 = (f32[32,2,256]{2,1,0:T(2,128)S(1)}, f32[32,2,256]{2,1,0:T(2,128)S(1)}, u32[]{:S(2)}, u32[]{:S(2)}) collective-permute-start(f32[32,2,256]{2,1,0:T(2,128)S(1)} %get-tuple-element.18.own_ref), channel_id=1, source_target_pairs={{0,1},{1,0},{2,3},{3,2},{4,5},{5,4},{6,7},{7,6},{8,9},{9,8},{10,11... | collective-permute-start | bytes 196616 | tf_op jit(solution)/shard_map/ppermute | solution.py:569
  74.0 0.9 copy-start.4
  74.9 1.1 copy-start.5
  76.1 10.4 %copy-start.9 = (s32[2,256]{1,0:T(2,128)S(1)}, s32[2,256]{1,0:T(2,128)}, u32[]{:S(2)}) copy-start(s32[2,256]{1,0:T(2,128)} %steering_ref.3) | copy-start | bytes 6148
  86.3 28.2 %collective-permute-start.1 = (f32[32,2,256]{2,1,0:T(2,128)S(1)}, f32[32,2,256]{2,1,0:T(2,128)S(1)}, u32[]{:S(2)}, u32[]{:S(2)}) collective-permute-start(f32[32,2,256]{2,1,0:T(2,128)S(1)} %get-tuple-element.15.own_ref), channel_id=1, source_target_pairs={{0,1},{1,0},{2,3},{3,2},{4,5},{5,4},{6,7},{7,6},{8,9},{9,8},{10,11... | collective-permute-start | bytes 196616 | tf_op jit(solution)/shard_map/ppermute | solution.py:569
  86.4 5.7 %copy-start.3 = (bf16[32,32,512]{2,1,0:T(8,128)(2,1)S(1)}, bf16[32,32,512]{2,1,0:T(8,128)(2,1)}, u32[]{:S(2)}) copy-start(bf16[32,32,512]{2,1,0:T(8,128)(2,1)} %copy-done.2) | copy-start | bytes 3145732

commit v2 on v1

--- a/solution.py
+++ b/solution.py
@@ -194,8 +194,12 @@
     return lax.dot_general(left, right, dims, preferred_element_type=jnp.float32)
 
 
-def transform_rows(kept_count, transform_count, owners, chunks):
-    kept = np.arange(kept_count).reshape(owners, chunks, -1).transpose(1, 0, 2).reshape(-1)
+def transform_rows(kept_count, transform_count, owners, shares):
+    by_owner = np.arange(kept_count).reshape(owners, -1)
+    ends = np.cumsum(shares)
+    kept = np.concatenate(
+        [by_owner[:, end - share : end].reshape(-1) for share, end in zip(shares, ends)]
+    )
     phases = (kept[:, None] * np.arange(transform_count)[None, :] % transform_count) * (
         2.0 * math.pi / transform_count
     )
@@ -203,11 +207,66 @@
     return jnp.asarray(table.astype(jnp.bfloat16))
 
 
-def filter_kernel(owners, x_ref, taps_ref, table_ref, *refs):
-    *out_refs, here_ref, next_ref, windowed_ref, turned_ref, spill_ref = refs
+def transformed(owners, frames, taps, table, windowed, out_ref, turned_ref, spill_ref):
+    rows = table.shape[0]
+    width = out_ref.shape[2]
+    share = rows // owners
+    block = mxu(table, windowed, NT)
+    for frame in range(frames):
+        turned_ref[pl.ds(frame, rows, stride=frames), :] = block[
+            :, frame * width : (frame + 1) * width
+        ]
+    for frame in range(NEXT_ROWS):
+        at = (frames + frame) * width
+        if frame < taps - 1:
+            part = block[:, at : at + width]
+        else:
+            part = jnp.zeros((rows, width), jnp.float32)
+        spill_ref[pl.ds(frame, rows, stride=NEXT_ROWS), :] = part
+    main = share * frames
+    extra = share * NEXT_ROWS
+    for owner in range(owners):
+        out_ref[owner, :main, :] = turned_ref[owner * main : (owner + 1) * main, :].astype(
+            jnp.bfloat16
+        )
+        out_ref[owner, main : main + extra, :] = spill_ref[
+            owner * extra : (owner + 1) * extra, :
+        ].astype(jnp.bfloat16)
+
+
+def filter_kernel(
+    owners,
+    x_hbm,
+    taps_ref,
+    table_hbm,
+    windowed_hbm,
+    out_ref,
+    x_ref,
+    table_ref,
+    here_ref,
+    next_ref,
+    windowed_ref,
+    turned_ref,
+    spill_ref,
+    sems,
+):
     inputs, _, frames, points = x_ref.shape
     taps = taps_ref.shape[0]
     width = 2 * inputs
+    pieces = sems.shape[0] - 2
+    group = inputs // pieces
+    table_copy = pltpu.make_async_copy(
+        table_hbm.at[pl.ds(0, table_ref.shape[0])], table_ref, sems.at[pieces]
+    )
+    copies = [
+        pltpu.make_async_copy(
+            x_hbm.at[pl.ds(i * group, group)], x_ref.at[pl.ds(i * group, group)], sems.at[i]
+        )
+        for i in range(pieces)
+    ]
+    for copy in copies:
+        copy.start()
+    table_copy.start()
     frame_of = lax.broadcasted_iota(jnp.int32, (frames, points), 0)
     here_weights = []
     next_weights = []
@@ -232,7 +291,9 @@
                 next_ref[part, piece, pl.ds(i * frames, frames), :] = later[:, lanes]
         return carry
 
-    lax.fori_loop(0, inputs, window, 0)
+    for i, copy in enumerate(copies):
+        copy.wait()
+        lax.fori_loop(i * group, (i + 1) * group, window, 0)
     for frame in range(frames + taps - 1):
         source = here_ref if frame < frames else next_ref
         first = frame % frames
@@ -246,58 +307,107 @@
             windowed_ref[base : base + inputs, upper] = imag
             windowed_ref[base + inputs : base + width, lanes] = imag
             windowed_ref[base + inputs : base + width, upper] = -real
-    rows = table_ref.shape[0] // len(out_refs)
-    share = rows // owners
-    for chunk, out_ref in enumerate(out_refs):
-        block = mxu(table_ref[chunk * rows : (chunk + 1) * rows, :], windowed_ref[...], NT)
-        for frame in range(frames):
-            turned_ref[pl.ds(frame, rows, stride=frames), :] = block[
-                :, frame * width : (frame + 1) * width
-            ]
-        for frame in range(NEXT_ROWS):
-            at = (frames + frame) * width
-            if frame < taps - 1:
-                part = block[:, at : at + width]
-            else:
-                part = jnp.zeros((rows, width), jnp.float32)
-            spill_ref[pl.ds(frame, rows, stride=NEXT_ROWS), :] = part
-        main = share * frames
-        for owner in range(owners):
-            out_ref[owner, :main, :] = turned_ref[owner * main : (owner + 1) * main, :].astype(
-                jnp.bfloat16
-            )
-            extra = share * NEXT_ROWS
-            out_ref[owner, main : main + extra, :] = spill_ref[
-                owner * extra : (owner + 1) * extra, :
-            ].astype(jnp.bfloat16)
-
-
-def filtered(samples, window_taps, kept_count, owners, chunks):
+    keep = pltpu.make_async_copy(windowed_ref, windowed_hbm, sems.at[pieces + 1])
+    keep.start()
+    table_copy.wait()
+    transformed(
+        owners, frames, taps, table_ref[...], windowed_ref[...], out_ref, turned_ref, spill_ref
+    )
+    keep.wait()
+
+
+def filter_more_kernel(
+    owners,
+    frames,
+    taps,
+    start,
+    windowed_hbm,
+    table_hbm,
+    out_ref,
+    windowed_ref,
+    table_ref,
+    turned_ref,
+    spill_ref,
+    sems,
+):
+    copies = [
+        pltpu.make_async_copy(windowed_hbm, windowed_ref, sems.at[0]),
+        pltpu.make_async_copy(
+            table_hbm.at[pl.ds(start, table_ref.shape[0])], table_ref, sems.at[1]
+        ),
+    ]
+    for copy in copies:
+        copy.start()
+    for copy in copies:
+        copy.wait()
+    transformed(
+        owners, frames, taps, table_ref[...], windowed_ref[...], out_ref, turned_ref, spill_ref
+    )
+
+
+def filtered(samples, window_taps, kept_count, owners, shares):
     inputs, _, points, frames = samples.shape
     taps = window_taps.shape[0]
     width = 2 * inputs
-    rows = kept_count // chunks
-    table = transform_rows(kept_count, points, owners, chunks)
+    table = transform_rows(kept_count, points, owners, shares)
     by_frame = jnp.transpose(samples, (0, 1, 3, 2))
-    out = jax.ShapeDtypeStruct(
-        (owners, rows // owners * (frames + NEXT_ROWS), width), jnp.bfloat16
-    )
+    by_frame = pltpu.with_memory_space_constraint(by_frame, pltpu.HBM)
+    table = pltpu.with_memory_space_constraint(table, pltpu.HBM)
     pieces = points // LANES
-    return pl.pallas_call(
+    anywhere = pl.BlockSpec(memory_space=pl.ANY)
+    vmem = pl.BlockSpec(memory_space=pltpu.VMEM)
+    windowed_shape = ((frames + taps - 1) * width, 2 * points)
+
+    def out_shape(share):
+        return jax.ShapeDtypeStruct((owners, share * (frames + NEXT_ROWS), width), jnp.bfloat16)
+
+    def scratch(share):
+        rows = owners * share
+        return [
+            pltpu.VMEM((rows * frames, width), jnp.float32),
+            pltpu.VMEM((rows * NEXT_ROWS, width), jnp.float32),
+        ]
+
+    windowed, first = pl.pallas_call(
         functools.partial(filter_kernel, owners),
-        out_shape=[out] * chunks,
-        in_specs=[pl.BlockSpec(memory_space=pltpu.VMEM)] * 3,
-        out_specs=[pl.BlockSpec(memory_space=pltpu.VMEM)] * chunks,
+        out_shape=[pltpu.HBM(windowed_shape, jnp.bfloat16), out_shape(shares[0])],
+        in_specs=[anywhere, vmem, anywhere],
+        out_specs=[anywhere, vmem],
         scratch_shapes=[
+            pltpu.VMEM(by_frame.shape, jnp.bfloat16),
+            pltpu.VMEM((owners * shares[0], 2 * points), jnp.bfloat16),
             pltpu.VMEM((2, pieces, inputs * frames, LANES), jnp.float32),
             pltpu.VMEM((2, pieces, inputs * frames, LANES), jnp.float32),
-            pltpu.VMEM(((frames + taps - 1) * width, 2 * points), jnp.bfloat16),
-            pltpu.VMEM((rows * frames, width), jnp.float32),
-            pltpu.VMEM((rows * NEXT_ROWS, width), jnp.float32),
+            pltpu.VMEM(windowed_shape, jnp.bfloat16),
+            *scratch(shares[0]),
+            pltpu.SemaphoreType.DMA((6,)),
         ],
-        compiler_params=pltpu.CompilerParams(vmem_limit_bytes=48 * MIB),
+        compiler_params=pltpu.CompilerParams(vmem_limit_bytes=32 * MIB),
         name="filter",
     )(by_frame, window_taps, table)
+    windowed = pltpu.with_memory_space_constraint(windowed, pltpu.HBM)
+    sent = [first]
+    start = owners * shares[0]
+    for share in shares[1:]:
+        rows = owners * share
+        sent.append(
+            pl.pallas_call(
+                functools.partial(filter_more_kernel, owners, frames, taps, start),
+                out_shape=out_shape(share),
+                in_specs=[anywhere, anywhere],
+                out_specs=vmem,
+                scratch_shapes=[
+                    pltpu.VMEM(windowed_shape, jnp.bfloat16),
+                    pltpu.VMEM((rows, 2 * points), jnp.bfloat16),
+                    *scratch(share),
+                    pltpu.SemaphoreType.DMA((2,)),
+                ],
+                compiler_params=pltpu.CompilerParams(vmem_limit_bytes=24 * MIB),
+                name="filter_more",
+            )(windowed, table)
+        )
+        start += rows
+    return sent
 
 
 def gain_terms(real, imag, gains, flags):
@@ -310,17 +420,21 @@
     return turned_real, turned_imag, power
 
 
-def updated_gains(real, imag, own_real, own_imag, model_real, model_imag, gains, flags, older):
-    turned_real, turned_imag, power = gain_terms(real, imag, gains, flags)
-    straight = jnp.concatenate([turned_real, turned_imag], axis=0).astype(jnp.bfloat16)
-    crossed = jnp.concatenate([-turned_imag, turned_real], axis=0).astype(jnp.bfloat16)
+def denominators(power, model_real, model_imag):
+    model_power = model_real * model_real + model_imag * model_imag
+    rows = jnp.broadcast_to(power, (SUBLANES, power.shape[1])).astype(jnp.bfloat16)
+    return mxu(rows, model_power, NT)[0:1] + epsilon
+
+
+def updated_gains(own, turned, model_real, model_imag, denom, older):
+    real, imag = turned
+    straight = jnp.concatenate([real, imag], axis=0).astype(jnp.bfloat16)
+    crossed = jnp.concatenate([-imag, real], axis=0).astype(jnp.bfloat16)
     modelled = mxu(straight, model_real, NT) + mxu(crossed, model_imag, NT)
-    model_power = model_real * model_real + model_imag * model_imag
-    power_rows = jnp.broadcast_to(power, (SUBLANES, power.shape[1])).astype(jnp.bfloat16)
-    denom = mxu(power_rows, model_power, NT)[0:1] + epsilon
     frames = real.shape[0]
     modelled_real = modelled[:frames]
     modelled_imag = modelled[frames:]
+    own_real, own_imag = own
     numer_real = jnp.sum(own_real * modelled_real + own_imag * modelled_imag, axis=0, keepdims=True)
     numer_imag = jnp.sum(own_imag * modelled_real - own_real * modelled_imag, axis=0, keepdims=True)
     numer = jnp.concatenate([numer_real, numer_imag], axis=0) / frames
@@ -332,81 +446,123 @@
     return jnp.where(core == 0, values[:, :half], values[:, half:])
 
 
-def first_kernel(
-    times,
-    core_ref,
-    own_ref,
-    own_next_ref,
-    other_ref,
-    other_next_ref,
-    model_ref,
-    gains_ref,
-    flags_ref,
-    spectra_ref,
-    updated_ref,
-):
+def denominators_kernel(model_ref, gains_ref, flags_ref, denom_ref):
+    flags = flags_ref[...].astype(jnp.float32)
+    for c in range(model_ref.shape[0]):
+        gains = gains_ref[c]
+        power = flags[c : c + 1] * (gains[0:1] * gains[0:1] + gains[1:2] * gains[1:2])
+        denom_ref[c] = denominators(power, model_ref[c, 0], model_ref[c, 1])
+
+
+def first_kernel(times, base, core_ref, own_ref, other_ref, model_hbm, gains_ref, flags_ref, *refs):
+    denom_ref = refs[0] if len(refs) == 5 else None
+    spectra_ref, updated_ref, model_ref, sems = refs[-4:]
     core = core_ref[0]
-    count = gains_ref.shape[0]
-    sources = own_ref.shape[0]
-    frames = own_ref.shape[1] // count
-    width = own_ref.shape[2]
+    share = spectra_ref.shape[0]
+    sources, rows, width = own_ref.shape
+    frames = rows // share - NEXT_ROWS
     columns = sources // times
     lane = lax.broadcasted_iota(jnp.int32, (frames, width), 1)
     row = lax.broadcasted_iota(jnp.int32, (frames, width), 0)
     low = lane < width // 2
-
-    def loaded(ref, next_ref, column, time, c):
-        source = column * times + time
-        block = ref[source, c * frames : (c + 1) * frames, :].astype(jnp.float32)
-        if time > 0:
-            pair = c // 2 * 2 * NEXT_ROWS
-            extra = next_ref[source - 1, pair : pair + 2 * NEXT_ROWS, :].astype(jnp.float32)
-            if c % 2:
-                extra = pltpu.roll(extra, NEXT_ROWS, 0)
-            block = block + jnp.where(row < NEXT_ROWS - 1, extra, 0.0)
-        return block
-
-    for c in range(count):
-        real_rows = []
-        imag_rows = []
-        for time in range(times):
-            reals = []
-            imags = []
-            for column in range(columns):
-                own = loaded(own_ref, own_next_ref, column, time, c)
-                other = loaded(other_ref, other_next_ref, column, time, c)
-                first = jnp.where(core == 0, own, other)
-                second = jnp.where(core == 0, other, own)
-                reals.append(jnp.where(low, first, pltpu.roll(second, width // 2, 1)))
-                imags.append(jnp.where(low, pltpu.roll(first, width // 2, 1), second))
-            real_rows.append(jnp.concatenate(reals, axis=1))
-            imag_rows.append(jnp.concatenate(imags, axis=1))
-        spectra = jnp.concatenate(real_rows + imag_rows, axis=0).astype(jnp.bfloat16)
-        spectra_ref[c] = spectra
-        values = spectra.astype(jnp.float32)
-        half = values.shape[0] // 2
-        real = values[:half]
-        imag = values[half:]
-        updated_ref[c] = updated_gains(
-            real,
-            imag,
-            own_half(real, core),
-            own_half(imag, core),
-            model_ref[c, 0],
-            model_ref[c, 1],
-            gains_ref[c],
-            flags_ref[c : c + 1],
-            own_half(gains_ref[c], core),
-        )
+    count = BLOCK
+
+    def copy(i):
+        here = pl.ds(i * count, count)
+        there = pl.ds(base + i * count, count)
+        return pltpu.make_async_copy(model_hbm.at[there], model_ref.at[here], sems.at[i])
+
+    for i in range(share // count):
+        copy(i).start()
+
+    def step(i, carry):
+        main_rows = pl.ds(pl.multiple_of(i * (count * frames), count * frames), count * frames)
+        next_rows = pl.ds(
+            pl.multiple_of(share * frames + i * (count * NEXT_ROWS), count * NEXT_ROWS),
+            count * NEXT_ROWS,
+        )
+        flags = flags_ref[pl.ds(pl.multiple_of(base + i * count, count), count), :]
+
+        def loaded(ref, column, time):
+            source = column * times + time
+            block = ref[source, main_rows, :].astype(jnp.float32)
+            extra = None
+            if time > 0:
+                extra = ref[source - 1, next_rows, :].astype(jnp.float32)
+            return block, extra
+
+        def one(value, c):
+            block, extra = value
+            block = block[c * frames : (c + 1) * frames]
+            if extra is not None:
+                pair = c // 2 * 2 * NEXT_ROWS
+                extra = extra[pair : pair + 2 * NEXT_ROWS]
+                if c % 2:
+                    extra = pltpu.roll(extra, NEXT_ROWS, 0)
+                block = block + jnp.where(row < NEXT_ROWS - 1, extra, 0.0)
+            return block
+
+        blocks = {
+            (column, time): (loaded(own_ref, column, time), loaded(other_ref, column, time))
+            for column in range(columns)
+            for time in range(times)
+        }
+        for c in range(count):
+            real_rows = []
+            imag_rows = []
+            for time in range(times):
+                reals = []
+                imags = []
+                for column in range(columns):
+                    own, other = blocks[column, time]
+                    own = one(own, c)
+                    other = one(other, c)
+                    first = jnp.where(core == 0, own, other)
+                    second = jnp.where(core == 0, other, own)
+                    reals.append(jnp.where(low, first, pltpu.roll(second, width // 2, 1)))
+                    imags.append(jnp.where(low, pltpu.roll(first, width // 2, 1), second))
+                real_rows.append(jnp.concatenate(reals, axis=1))
+                imag_rows.append(jnp.concatenate(imags, axis=1))
+            spectra = jnp.concatenate(real_rows + imag_rows, axis=0)
+            spectra_ref[i * count + c] = spectra.astype(jnp.bfloat16)
+        copy(i).wait()
+        for c in range(count):
+            here = i * count + c
+            values = spectra_ref[here].astype(jnp.float32)
+            half = values.shape[0] // 2
+            real = values[:half]
+            imag = values[half:]
+            gains = gains_ref[base + here]
+            model_real = model_ref[here, 0]
+            model_imag = model_ref[here, 1]
+            turned_real, turned_imag, power = gain_terms(real, imag, gains, flags[c : c + 1])
+            if denom_ref is None:
+                denom = denominators(power, model_real, model_imag)
+            else:
+                denom = denom_ref[base + here]
+            updated_ref[here] = updated_gains(
+                (own_half(real, core), own_half(imag, core)),
+                (turned_real, turned_imag),
+                model_real,
+                model_imag,
+                denom,
+                own_half(gains, core),
+            )
+        return carry
+
+    lax.fori_loop(0, share // count, step, 0)
 
 
 def second_kernel(
-    core_ref, spectra_ref, model_ref, own_ref, other_ref, flags_ref, *refs
+    base, core_ref, spectra_ref, model_ref, own_ref, other_ref, flags_ref, *refs
 ):
     visibilities_ref, updated_ref = refs[-2:]
     core = core_ref[0]
-    for c in range(spectra_ref.shape[0]):
-        spectra = spectra_ref[c]
+    count = visibilities_ref.shape[0]
+    start = pl.program_id(0) * count
+    for c in range(count):
+        here = start + c
+        spectra = spectra_ref[here]
         half = spectra.shape[0] // 2
         values = spectra.astype(jnp.float32)
         real = values[:half]
@@ -417,20 +573,20 @@
         rotated = (jnp.concatenate([own_imag, -own_real], axis=0) / half).astype(jnp.bfloat16)
         visibilities_ref[c, 0] = mxu(paired, spectra, TN).astype(jnp.bfloat16)
         visibilities_ref[c, 1] = mxu(rotated, spectra, TN).astype(jnp.bfloat16)
-        own = own_ref[c]
-        other = other_ref[c]
+        own = own_ref[here]
+        other = other_ref[here]
         first = jnp.where(core == 0, own, other)
         second = jnp.where(core == 0, other, own)
         gains = jnp.concatenate([first, second], axis=1)
-        updated_ref[c] = updated_gains(
-            real,
-            imag,
-            own_real,
-            own_imag,
-            model_ref[c, 0],
-            model_ref[c, 1],
-            gains,
-            flags_ref[c : c + 1],
+        turned_real, turned_imag, power = gain_terms(real, imag, gains, flags_ref[base + here])
+        model_real = model_ref[here, 0]
+        model_imag = model_ref[here, 1]
+        updated_ref[here] = updated_gains(
+            (own_real, own_imag),
+            (turned_real, turned_imag),
+            model_real,
+            model_imag,
+            denominators(power, model_real, model_imag),
             own,
         )
 
@@ -501,119 +657,142 @@
     power_ref[...] = (real * real + imag * imag).reshape(count, frames, beams)
 
 
+def formed_beams(chunk, gains, flags, earlier):
+    base, spectra, table = chunk
+    share, doubled, input_count = spectra.shape
+    frame_count = doubled // 2
+    beams = table.shape[2] // 2
+    at = base // share
+    earlier = [] if earlier is None else [earlier]
+    return pl.pallas_call(
+        beams_kernel,
+        grid=(1,),
+        in_specs=[
+            pl.BlockSpec((share, doubled, input_count), lambda i: (0, 0, 0)),
+            pl.BlockSpec((share, 2, input_count), lambda i: (at, 0, 0)),
+            pl.BlockSpec((share, input_count), lambda i: (at, 0)),
+            pl.BlockSpec(memory_space=pltpu.VMEM),
+        ]
+        + [pl.BlockSpec(memory_space=pl.ANY)] * len(earlier),
+        out_specs=pl.BlockSpec((share, frame_count, beams), lambda i: (at, 0, 0)),
+        out_shape=jax.ShapeDtypeStruct((gains.shape[0], frame_count, beams), jnp.float32),
+        input_output_aliases={4: 0} if earlier else {},
+        scratch_shapes=[
+            pltpu.VMEM((table.shape[0], share * frame_count, 2 * input_count), jnp.bfloat16)
+        ],
+        compiler_params=pltpu.CompilerParams(vmem_limit_bytes=12 * MIB),
+        name="beams",
+    )(spectra, gains, flags, table, *earlier)
+
+
 def chunk_shards(samples, window_taps, sky_model, prior_gains, beam_steering, input_flags):
     frames = samples.shape[3]
     chan_local, _, half_rows, input_count = sky_model.shape
     times = lax.axis_size("tm")
     owners = lax.axis_size("chan") * times
-    core = lax.axis_index("beam")
+    core = lax.axis_index("beam").astype(jnp.int32).reshape(1)
+    first_channel = (lax.axis_index("chan") * times + lax.axis_index("tm")) * chan_local
     kept_count = chan_local * owners
     frame_count = frames * times
     beams = beam_steering.shape[1]
-    chunks = CHUNKS
-    share = chan_local // chunks
-    block = BLOCK
-    steps = share // block
-    sent = filtered(samples, window_taps, kept_count, owners, chunks)
-    core_word = core.astype(jnp.int32).reshape(1)
+    shares = [chan_local // CHUNKS] * CHUNKS
+    bases = [sum(shares[:chunk]) for chunk in range(CHUNKS)]
+    centres = [
+        (2 * (kept_count + first_channel + base) + share - 1).astype(jnp.int32).reshape(1)
+        for base, share in zip(bases, shares)
+    ]
+    flag_rows = input_flags.reshape(chan_local, 1, input_count)
+    sent = filtered(samples, window_taps, kept_count, owners, shares)
     swap = [(0, 1), (1, 0)]
     smem = pl.BlockSpec(memory_space=pltpu.SMEM)
     vmem = pl.BlockSpec(memory_space=pltpu.VMEM)
     anywhere = pl.BlockSpec(memory_space=pl.ANY)
-    first_channel = (lax.axis_index("chan") * times + lax.axis_index("tm")) * chan_local
     step = 2.0 * math.pi / (512 * kept_count)
-    reach = max(0.5 * (share - 1), 0.5)
-    terms = series_length(128 * reach * step)
+
+    sent[0], gains, flags, steering, flag_rows, core, centres = lax.optimization_barrier(
+        (sent[0], prior_gains, input_flags, beam_steering, flag_rows, core, centres)
+    )
+    denom = pl.pallas_call(
+        denominators_kernel,
+        grid=(shares[0] // BLOCK,),
+        in_specs=[
+            pl.BlockSpec((BLOCK, 2, half_rows, input_count), lambda i: (i, 0, 0, 0)),
+            pl.BlockSpec((BLOCK, 2, input_count), lambda i: (i, 0, 0)),
+            pl.BlockSpec((BLOCK, input_count), lambda i: (i, 0)),
+        ],
+        out_specs=pl.BlockSpec((BLOCK, 1, half_rows), lambda i: (i, 0, 0)),
+        out_shape=jax.ShapeDtypeStruct((shares[0], 1, half_rows), jnp.float32),
+        compiler_params=pltpu.CompilerParams(vmem_limit_bytes=24 * MIB),
+        name="denominators",
+    )(sky_model, gains, flags)
+    tables = []
+    for centre, share in zip(centres, shares):
+        reach = max(0.5 * (share - 1), 0.5)
+        terms = series_length(128 * reach * step)
+        tables.append(
+            pl.pallas_call(
+                functools.partial(steering_kernel, terms, reach, step),
+                in_specs=[smem, vmem],
+                out_specs=vmem,
+                out_shape=jax.ShapeDtypeStruct((terms, 2 * input_count, 2 * beams), jnp.bfloat16),
+                compiler_params=pltpu.CompilerParams(vmem_limit_bytes=8 * MIB),
+                name="steering",
+            )(centre, steering)
+        )
+    denom, *rest = lax.optimization_barrier((denom, *tables, *sent[1:]))
+    tables = rest[:CHUNKS]
+    sent[1:] = rest[CHUNKS:]
     visibilities = None
     beam_power = None
     gain_parts = []
-    for chunk in range(chunks):
-        base = chunk * steps
+    before = None
+    for chunk, (base, share) in enumerate(zip(bases, shares)):
         own = lax.all_to_all(sent[chunk], ("chan", "tm"), 0, 0, tiled=True)
+        if before is not None:
+            own, gain_parts[-1], spectra = lax.optimization_barrier((own, gain_parts[-1], spectra))
+            before = (before[0], spectra, before[2])
         other = lax.ppermute(own, "beam", swap)
-        width = own.shape[2]
-        next_base = frames * steps // NEXT_ROWS
-        main_spec = pl.BlockSpec((owners, block * frames, width), lambda i: (0, i, 0))
-        next_spec = pl.BlockSpec(
-            (owners, block * NEXT_ROWS, width), lambda i, at=next_base: (0, at + i, 0)
-        )
-        model_spec = pl.BlockSpec(
-            (block, 2, half_rows, input_count), lambda i, at=base: (at + i, 0, 0, 0)
-        )
-        gains_spec = pl.BlockSpec((block, 2, input_count), lambda i, at=base: (at + i, 0, 0))
-        flags_spec = pl.BlockSpec((block, input_count), lambda i, at=base: (at + i, 0))
-        spectra_spec = pl.BlockSpec((block, 2 * frame_count, input_count), lambda i: (i, 0, 0))
-        half_spec = pl.BlockSpec((block, 2, half_rows), lambda i: (i, 0, 0))
+        if before is not None:
+            beam_power = formed_beams(before, gains, flags, beam_power)
+            other, beam_power = lax.optimization_barrier((other, beam_power))
         half_shape = jax.ShapeDtypeStruct((share, 2, half_rows), jnp.float32)
-        spectra, gains_own = pl.pallas_call(
-            functools.partial(first_kernel, times),
-            grid=(steps,),
-            in_specs=[
-                smem,
-                main_spec,
-                next_spec,
-                main_spec,
-                next_spec,
-                model_spec,
-                gains_spec,
-                flags_spec,
-            ],
-            out_specs=[spectra_spec, half_spec],
+        known = [denom] if chunk == 0 else []
+        spectra, gains_own, model = pl.pallas_call(
+            functools.partial(first_kernel, times, base),
+            in_specs=[smem, vmem, vmem, anywhere, vmem, vmem] + [vmem] * len(known),
+            out_specs=[vmem, vmem, vmem],
             out_shape=[
                 jax.ShapeDtypeStruct((share, 2 * frame_count, input_count), jnp.bfloat16),
                 half_shape,
+                pltpu.VMEM((share, *sky_model.shape[1:]), sky_model.dtype),
             ],
-            compiler_params=pltpu.CompilerParams(vmem_limit_bytes=40 * MIB),
+            scratch_shapes=[pltpu.SemaphoreType.DMA((share // BLOCK,))],
+            compiler_params=pltpu.CompilerParams(vmem_limit_bytes=12 * MIB),
             name="first_update",
-        )(core_word, own, own, other, other, sky_model, prior_gains, input_flags)
+        )(core, own, other, sky_model, gains, flags, *known)
+        model = pltpu.with_memory_space_constraint(model, pltpu.VMEM)
         gains_other = lax.ppermute(gains_own, "beam", swap)
-        centre = 2 * (kept_count + first_channel + chunk * share) + share - 1
-        table = pl.pallas_call(
-            functools.partial(steering_kernel, terms, reach, step),
-            in_specs=[smem, vmem],
-            out_specs=vmem,
-            out_shape=jax.ShapeDtypeStruct((terms, 2 * input_count, 2 * beams), jnp.bfloat16),
-            compiler_params=pltpu.CompilerParams(vmem_limit_bytes=32 * MIB),
-            name="steering",
-        )(centre.astype(jnp.int32).reshape(1), beam_steering)
-        power_spec = pl.BlockSpec(
-            (share, frame_count, beams), lambda i, at=chunk: (at, 0, 0)
-        )
-        earlier = [] if beam_power is None else [beam_power]
-        beam_power = pl.pallas_call(
-            beams_kernel,
-            grid=(1,),
-            in_specs=[
-                pl.BlockSpec((share, 2 * frame_count, input_count), lambda i: (0, 0, 0)),
-                pl.BlockSpec((share, 2, input_count), lambda i, at=chunk: (at, 0, 0)),
-                pl.BlockSpec((share, input_count), lambda i, at=chunk: (at, 0)),
-                pl.BlockSpec((terms, 2 * input_count, 2 * beams), lambda i: (0, 0, 0)),
-            ]
-            + [anywhere] * len(earlier),
-            out_specs=power_spec,
-            out_shape=jax.ShapeDtypeStruct((chan_local, frame_count, beams), jnp.float32),
-            input_output_aliases={4: 0} if earlier else {},
-            scratch_shapes=[
-                pltpu.VMEM((terms, share * frame_count, 2 * input_count), jnp.bfloat16)
-            ],
-            compiler_params=pltpu.CompilerParams(vmem_limit_bytes=40 * MIB),
-            name="beams",
-        )(spectra, prior_gains, input_flags, table, *earlier)
+        before = (base, spectra, tables[chunk])
+        if chunk == CHUNKS - 1:
+            beam_power = formed_beams(before, gains, flags, beam_power)
         earlier = [] if visibilities is None else [visibilities]
+        block = VIS_BLOCK
+        block_spec = pl.BlockSpec(
+            (block, 2, half_rows, input_count), lambda i, at=base // block: (at + i, 0, 0, 0)
+        )
         visibilities, gains_new = pl.pallas_call(
-            second_kernel,
-            grid=(steps,),
-            in_specs=[smem, spectra_spec, model_spec, half_spec, half_spec, flags_spec]
-            + [anywhere] * len(earlier),
-            out_specs=[model_spec, half_spec],
+            functools.partial(second_kernel, base),
+            grid=(share // block,),
+            in_specs=[smem, vmem, vmem, vmem, vmem, vmem] + [anywhere] * len(earlier),
+            out_specs=[block_spec, vmem],
             out_shape=[
                 jax.ShapeDtypeStruct((chan_local, 2, half_rows, input_count), jnp.bfloat16),
                 half_shape,
             ],
             input_output_aliases={6: 0} if earlier else {},
-            compiler_params=pltpu.CompilerParams(vmem_limit_bytes=40 * MIB),
+            compiler_params=pltpu.CompilerParams(vmem_limit_bytes=12 * MIB),
             name="second_update",
-        )(core_word, spectra, sky_model, gains_own, gains_other, input_flags, *earlier)
+        )(core, spectra, model, gains_own, gains_other, flag_rows, *earlier)
         gain_parts.append(gains_new)
     return (
         visibilities,
@@ -624,6 +803,7 @@
 
 CHUNKS = 2
 BLOCK = 8
+VIS_BLOCK = 4
 
 
 def shards(samples, window_taps, sky_model, prior_gains, beam_steering, input_flags):

time: 132 us -> 106 us (0.80)
  blocking collectives: 27.2 us -> 0 us
  waiting for transfers between devices: 19.8 us -> 3.41 us
  starting transfers between devices: 4.38 us -> 14.1 us
  Pallas kernels: 72.3 us -> 77.7 us
  local copies, waits for them, and re-layouts: 5.97 us -> 8.56 us
    all_to_all x1 -> x0, blocking collectives: 27.2 us -> none  [chunk_shards(): own = lax.all_to_all(sent[chunk], ('chan', 'tm'), 0, 0, tiled=True)]
    all_to_all x1 -> x2, waiting for transfers between devices: 19.8 us -> 0.02 us  [chunk_shards(): own = lax.all_to_all(sent[chunk], ('chan', 'tm'), 0, 0, tiled=True)]
    all_to_all x1 -> x2, starting transfers between devices: 3.59 us -> 13.3 us  [chunk_shards(): own = lax.all_to_all(sent[chunk], ('chan', 'tm'), 0, 0, tiled=True)]
    pallas_call x7 -> x9, Pallas kernels: 66.6 us -> 72 us  [the longest x2 25.3 us: chunk_shards(): pl.pallas_call(functools.partial(second_kernel, base), grid=(share // blo...]
    ppermute x2, waiting for transfers between devices: 0.01 us -> 2.28 us  [chunk_shards(): other = lax.ppermute(own, 'beam', swap)]
    unnamed x20 -> x18, local copies, waits for them, and re-layouts: 5.97 us -> 7.51 us
  transfers between devices with their start and end apart: 5 -> 6, of which waited for: 1 -> 2; matrix products, arithmetic and copies ran while one was open for 0% -> 0% of each run, Pallas kernels for 37% -> 44%
where the time goes in v2:
time: 106 us; the launch traced here: 105 us
  Pallas kernels  77.7 us (73%)
  starting transfers between devices  14.1 us (13%)
  local copies, waits for them, and re-layouts  8.56 us (8%)
  waiting for transfers between devices  3.41 us (3%)
    pallas_call x2, Pallas kernels, chunk_shards(): pl.pallas_call(functools.partial(second_kernel, base), grid=(share // blo...  25.3 us
    pallas_call x2, Pallas kernels, chunk_shards(): pl.pallas_call(functools.partial(first_kernel, times, base), in_specs=[sm...  18.7 us
    all_to_all x2, starting transfers between devices, chunk_shards(): own = lax.all_to_all(sent[chunk], ('chan', 'tm'), 0, 0, tiled=True)  13.3 us
    pallas_call x1, Pallas kernels, filtered(): pl.pallas_call(functools.partial(filter_kernel, owners), out_shape=[pltpu...  8.54 us
    unnamed x18, local copies, waits for them, and re-layouts  7.51 us
    pallas_call x1, Pallas kernels, chunk_shards(): pl.pallas_call(denominators_kernel, grid=(shares[0] // BLOCK,), in_specs=...  7.22 us
    pallas_call x2, Pallas kernels, formed_beams(): pl.pallas_call(beams_kernel, grid=(1,), in_specs=[pl.BlockSpec((share, do...  6.4 us
    pallas_call x1, Pallas kernels, filtered(): pl.pallas_call(functools.partial(filter_more_kernel, owners, frames, taps...  5.86 us
  transfers between devices with their start and end apart: 6, of which 2 were waited for; matrix products, arithmetic and copies ran while one was open for 0% of the time, Pallas kernels for 44%

profile of v2, /device:TPU:0, one launch (start us, length us, event | category | flops | bytes accessed | tf_op | source)
XLA Modules:
  0.0 105.2 jit_solution(12485087523106019389)
XLA Ops:
  0.7 1.0 reshape.18.flags_ref
  1.7 0.7 copy-done.6
  2.4 8.5 %filter.1 = (bf16[1408,2048]{1,0:T(8,128)(2,1)}, bf16[8,384,128]{2,1,0:T(8,128)(2,1)}) custom-call(bf16[64,2,8,1024]{3,2,1,0:T(8,128)(2,1)} %bitcast.6, f32[4,1024]{1,0:T(4,128)S(1)} %copy-done.6, bf16[512,2048]{1,0:T(8,128)(2,1)} %constant.28.clone.table_hbm), custom_call_target="tpu_custom_call" | custom-call | tf_op jit(solution)/shard_map/filter/pallas_call | solution.py:371
  11.0 7.3 %all-to-all-start.1 = ((bf16[8,384,128]{2,1,0:T(8,128)(2,1)}), bf16[8,384,128]{2,1,0:T(8,128)(2,1)S(1)}, u32[]{:S(2)}, u32[]{:S(2)}) async-start(bf16[8,384,128]{2,1,0:T(8,128)(2,1)} %get-tuple-element.41), calls=%async_computation.1 | async-start | bytes 1572864 | tf_op jit(solution)/shard_map/all_to_all | solution.py:750
  18.2 5.9 %filter_more.1 = bf16[8,384,128]{2,1,0:T(8,128)(2,1)} custom-call(bf16[1408,2048]{1,0:T(8,128)(2,1)} %get-tuple-element.39.windowed_hbm, bf16[512,2048]{1,0:T(8,128)(2,1)} %constant.28.clone.table_hbm), custom_call_target="tpu_custom_call" | custom-call | tf_op jit(solution)/shard_map/filter_more/pallas_call | solution.py:394
  24.1 0.7 copy-done.7
  24.8 2.9 %steering.3.table_ref = bf16[4,1024,512]{2,1,0:T(8,128)(2,1)S(1)} custom-call(s32[1]{0:T(128)} %bitcast.3.centre_ref, s32[2,256]{1,0:T(2,128)S(1)} %copy-done.7), custom_call_target="tpu_custom_call" | custom-call | tf_op jit(solution)/shard_map/steering/pallas_call | solution.py:733
  27.7 1.9 %copy-done.2 = bf16[4,1024,512]{2,1,0:T(8,128)(2,1)} copy-done((bf16[4,1024,512]{2,1,0:T(8,128)(2,1)}, bf16[4,1024,512]{2,1,0:T(8,128)(2,1)S(1)}, u32[]{:S(2)}) %copy-start.2) | copy-done | bytes 4194328
  29.6 2.9 %steering.2.table_ref = bf16[4,1024,512]{2,1,0:T(8,128)(2,1)S(1)} custom-call(s32[1]{0:T(128)} %bitcast.2.centre_ref, s32[2,256]{1,0:T(2,128)S(1)} %copy-done.8), custom_call_target="tpu_custom_call" | custom-call | tf_op jit(solution)/shard_map/steering/pallas_call | solution.py:733
  32.5 2.0 %copy-done = bf16[4,1024,512]{2,1,0:T(8,128)(2,1)} copy-done((bf16[4,1024,512]{2,1,0:T(8,128)(2,1)}, bf16[4,1024,512]{2,1,0:T(8,128)(2,1)S(1)}, u32[]{:S(2)}) %copy-start) | copy-done | bytes 4194328
  34.4 7.2 %denominators.1.refs_0_ = f32[32,1,256]{2,1,0:T(1,128)S(1)} custom-call(bf16[64,2,256,512]{3,2,1,0:T(8,128)(2,1)} %model_hbm.3, f32[64,2,512]{2,1,0:T(2,128)S(1)} %copy-done.4, s32[64,512]{1,0:T(8,128)S(1)} %copy-done.5), custom_call_target="tpu_custom_call" | custom-call | tf_op jit(solution)/shard_map/denominators/pallas_call | solution.py:715
  41.7 6.0 %all-to-all-start = ((bf16[8,384,128]{2,1,0:T(8,128)(2,1)}), bf16[8,384,128]{2,1,0:T(8,128)(2,1)S(1)}, u32[]{:S(2)}, u32[]{:S(2)}) async-start(bf16[8,384,128]{2,1,0:T(8,128)(2,1)} %filter_more.1), calls=%async_computation | async-start | bytes 1572864 | tf_op jit(solution)/shard_map/all_to_all | solution.py:750
  47.7 2.3 %collective-permute-done.other_ref = bf16[8,384,128]{2,1,0:T(8,128)(2,1)S(1)} collective-permute-done((bf16[8,384,128]{2,1,0:T(8,128)(2,1)S(1)}, bf16[8,384,128]{2,1,0:T(8,128)(2,1)S(1)}, u32[]{:S(2)}, u32[]{:S(2)}) %collective-permute-start) | collective-permute-done | bytes 786464 | tf_op jit(solution)/shard_map/ppermute | solution.py:754
  50.0 8.1 %first_update.2 = (bf16[32,32,512]{2,1,0:T(8,128)(2,1)S(1)}, f32[32,2,256]{2,1,0:T(2,128)S(1)}, bf16[32,2,256,512]{3,2,1,0:T(8,128)(2,1)S(1)}) custom-call(s32[1]{0:T(128)} %bitcast.1.core_ref, bf16[8,384,128]{2,1,0:T(8,128)(2,1)S(1)} %all-to-all-done.1.own_ref, bf16[8,384,128]{2,1,0:T(8,128)(2,1)S(1)} %collective-permute-done.other_ref, ...), custom_call_target="tpu_custom_call" | custom-call | tf_op jit(solution)/shard_map/first_update/pallas_call | solution.py:760
  58.1 0.2 collective-permute-start.1
  58.3 1.1 %collective-permute-done.1.other_ref = f32[32,2,256]{2,1,0:T(2,128)S(1)} collective-permute-done((f32[32,2,256]{2,1,0:T(2,128)S(1)}, f32[32,2,256]{2,1,0:T(2,128)S(1)}, u32[]{:S(2)}, u32[]{:S(2)}) %collective-permute-start.1) | collective-permute-done | bytes 65568 | tf_op jit(solution)/shard_map/ppermute | solution.py:774
  59.5 12.7 %second_update.2 = (bf16[64,2,256,512]{3,2,1,0:T(8,128)(2,1)}, f32[32,2,256]{2,1,0:T(2,128)S(1)}) custom-call(s32[1]{0:T(128)} %bitcast.1.core_ref, bf16[32,32,512]{2,1,0:T(8,128)(2,1)S(1)} %get-tuple-element.49.spectra_ref, bf16[32,2,256,512]{3,2,1,0:T(8,128)(2,1)S(1)} %get-tuple-element.44.model_ref, f32[32,2,256]{2,1,0:T(2,128)S(1)} %get-tuple-element.45.own_ref, ...), custom_call_target="tpu_custom_call" | custom-call | tf_op jit(solution)/shard_map/second_update/pallas_call | solution.py:783
  72.4 2.2 %copy-done.1 = bf16[4,1024,512]{2,1,0:T(8,128)(2,1)S(1)} copy-done((bf16[4,1024,512]{2,1,0:T(8,128)(2,1)S(1)}, bf16[4,1024,512]{2,1,0:T(8,128)(2,1)}, u32[]{:S(2)}) %copy-start.1) | copy-done | bytes 4194328
  74.6 3.2 %beams.2.refs_0_ = f32[64,16,256]{2,1,0:T(8,128)} custom-call(bf16[32,32,512]{2,1,0:T(8,128)(2,1)S(1)} %get-tuple-element.49.spectra_ref, f32[64,2,512]{2,1,0:T(2,128)S(1)} %copy-done.4, s32[64,512]{1,0:T(8,128)S(1)} %copy-done.5, bf16[4,1024,512]{2,1,0:T(8,128)(2,1)S(1)} %copy-done.1), custom_call_target="tpu_custom_call" | custom-call | tf_op jit(solution)/shard_map/beams/pallas_call | solution.py:667
  77.7 10.5 %first_update.3 = (bf16[32,32,512]{2,1,0:T(8,128)(2,1)S(1)}, f32[32,2,256]{2,1,0:T(2,128)S(1)}, bf16[32,2,256,512]{3,2,1,0:T(8,128)(2,1)S(1)}) custom-call(s32[1]{0:T(128)} %bitcast.1.core_ref, bf16[8,384,128]{2,1,0:T(8,128)(2,1)S(1)} %all-to-all-done.own_ref, bf16[8,384,128]{2,1,0:T(8,128)(2,1)S(1)} %collective-permute-done.2.other_ref, ...), custom_call_target="tpu_custom_call" | custom-call | tf_op jit(solution)/shard_map/first_update/pallas_call | solution.py:760
  88.3 0.4 collective-permute-start.3
  88.7 3.2 %beams.3 = f32[64,16,256]{2,1,0:T(8,128)} custom-call(bf16[32,32,512]{2,1,0:T(8,128)(2,1)S(1)} %get-tuple-element.52.spectra_ref, f32[64,2,512]{2,1,0:T(2,128)S(1)} %copy-done.4, s32[64,512]{1,0:T(8,128)S(1)} %copy-done.5, bf16[4,1024,512]{2,1,0:T(8,128)(2,1)S(1)} %copy-done.3, f32[64,16,256]{2,1,0:T(8,128)} %beams.2.refs_0_), custom_call_target="tpu_custom_call", output_to_operand_aliasing={{}: (4, {})} | custom-call | tf_op jit(solution)/shard_map/beams/pallas_call | solution.py:667
  91.9 12.6 %second_update.3 = (bf16[64,2,256,512]{3,2,1,0:T(8,128)(2,1)}, f32[32,2,256]{2,1,0:T(2,128)S(1)}) custom-call(s32[1]{0:T(128)} %bitcast.1.core_ref, bf16[32,32,512]{2,1,0:T(8,128)(2,1)S(1)} %get-tuple-element.52.spectra_ref, bf16[32,2,256,512]{3,2,1,0:T(8,128)(2,1)S(1)} %get-tuple-element.53.model_ref, ...), custom_call_target="tpu_custom_call", output_to_operand_aliasing={{0}: (6, {})} | custom-call | tf_op jit(solution)/shard_map/second_update/pallas_call | solution.py:783
  104.5 0.7 pad_maximum_fusion
  (19 shorter events, 0.2 us)
Async XLA Ops:
  0.6 33.8 %copy-start.5 = (s32[64,512]{1,0:T(8,128)S(1)}, s32[64,512]{1,0:T(8,128)}, u32[]{:S(2)}) copy-start(s32[64,512]{1,0:T(8,128)} %flags_ref.4) | copy-start | bytes 393220
  0.6 33.8 %copy-start.4 = (f32[64,2,512]{2,1,0:T(2,128)S(1)}, f32[64,2,512]{2,1,0:T(2,128)}, u32[]{:S(2)}) copy-start(f32[64,2,512]{2,1,0:T(2,128)} %gains_ref.4) | copy-start | bytes 786436
  1.7 0.7 copy-start.6
  2.4 27.2 %copy-start.8 = (s32[2,256]{1,0:T(2,128)S(1)}, s32[2,256]{1,0:T(2,128)}, u32[]{:S(2)}) copy-start(s32[2,256]{1,0:T(2,128)} %steering_ref.1) | copy-start | bytes 6148
  11.0 30.7 %all-to-all-start.1 = ((bf16[8,384,128]{2,1,0:T(8,128)(2,1)}), bf16[8,384,128]{2,1,0:T(8,128)(2,1)S(1)}, u32[]{:S(2)}, u32[]{:S(2)}) async-start(bf16[8,384,128]{2,1,0:T(8,128)(2,1)} %get-tuple-element.41), calls=%async_computation.1 | async-start | bytes 1572864 | tf_op jit(solution)/shard_map/all_to_all | solution.py:750
  24.1 0.7 copy-start.7
  27.6 1.9 %copy-start.2 = (bf16[4,1024,512]{2,1,0:T(8,128)(2,1)}, bf16[4,1024,512]{2,1,0:T(8,128)(2,1)S(1)}, u32[]{:S(2)}) copy-start(bf16[4,1024,512]{2,1,0:T(8,128)(2,1)S(1)} %steering.3.table_ref) | copy-start | bytes 12582916
  32.4 2.0 %copy-start = (bf16[4,1024,512]{2,1,0:T(8,128)(2,1)}, bf16[4,1024,512]{2,1,0:T(8,128)(2,1)S(1)}, u32[]{:S(2)}) copy-start(bf16[4,1024,512]{2,1,0:T(8,128)(2,1)S(1)} %steering.2.table_ref) | copy-start | bytes 12582916
  41.7 30.5 %all-to-all-start = ((bf16[8,384,128]{2,1,0:T(8,128)(2,1)}), bf16[8,384,128]{2,1,0:T(8,128)(2,1)S(1)}, u32[]{:S(2)}, u32[]{:S(2)}) async-start(bf16[8,384,128]{2,1,0:T(8,128)(2,1)} %filter_more.1), calls=%async_computation | async-start | bytes 1572864 | tf_op jit(solution)/shard_map/all_to_all | solution.py:750
  47.7 2.3 %collective-permute-start = (bf16[8,384,128]{2,1,0:T(8,128)(2,1)S(1)}, bf16[8,384,128]{2,1,0:T(8,128)(2,1)S(1)}, u32[]{:S(2)}, u32[]{:S(2)}) collective-permute-start(bf16[8,384,128]{2,1,0:T(8,128)(2,1)S(1)} %all-to-all-done.1.own_ref), channel_id=1, source_target_pairs={{0,1},{1,0},{2,3},{3,2},{4,5},{5,4},{6,7},{7,6},{8,9},{9,8},{10,11... | collective-permute-start | bytes 2359304 | tf_op jit(solution)/shard_map/ppermute | solution.py:754
  58.1 1.3 %collective-permute-start.1 = (f32[32,2,256]{2,1,0:T(2,128)S(1)}, f32[32,2,256]{2,1,0:T(2,128)S(1)}, u32[]{:S(2)}, u32[]{:S(2)}) collective-permute-start(f32[32,2,256]{2,1,0:T(2,128)S(1)} %get-tuple-element.45.own_ref), channel_id=1, source_target_pairs={{0,1},{1,0},{2,3},{3,2},{4,5},{5,4},{6,7},{7,6},{8,9},{9,8},{10,11... | collective-permute-start | bytes 196616 | tf_op jit(solution)/shard_map/ppermute | solution.py:774
  72.2 5.5 %collective-permute-start.2 = (bf16[8,384,128]{2,1,0:T(8,128)(2,1)S(1)}, bf16[8,384,128]{2,1,0:T(8,128)(2,1)S(1)}, u32[]{:S(2)}, u32[]{:S(2)}) collective-permute-start(bf16[8,384,128]{2,1,0:T(8,128)(2,1)S(1)} %all-to-all-done.own_ref), channel_id=1, source_target_pairs={{0,1},{1,0},{2,3},{3,2},{4,5},{5,4},{6,7},{7,6},{8,9},{9,8},{10,11... | collective-permute-start | bytes 2359304 | tf_op jit(solution)/shard_map/ppermute | solution.py:754
  72.4 2.2 %copy-start.1 = (bf16[4,1024,512]{2,1,0:T(8,128)(2,1)S(1)}, bf16[4,1024,512]{2,1,0:T(8,128)(2,1)}, u32[]{:S(2)}) copy-start(bf16[4,1024,512]{2,1,0:T(8,128)(2,1)} %copy-done) | copy-start | bytes 12582916
  77.7 10.9 %copy-start.3 = (bf16[4,1024,512]{2,1,0:T(8,128)(2,1)S(1)}, bf16[4,1024,512]{2,1,0:T(8,128)(2,1)}, u32[]{:S(2)}) copy-start(bf16[4,1024,512]{2,1,0:T(8,128)(2,1)} %copy-done.2) | copy-start | bytes 12582916
  88.3 3.6 %collective-permute-start.3 = (f32[32,2,256]{2,1,0:T(2,128)S(1)}, f32[32,2,256]{2,1,0:T(2,128)S(1)}, u32[]{:S(2)}, u32[]{:S(2)}) collective-permute-start(f32[32,2,256]{2,1,0:T(2,128)S(1)} %get-tuple-element.54.own_ref), channel_id=1, source_target_pairs={{0,1},{1,0},{2,3},{3,2},{4,5},{5,4},{6,7},{7,6},{8,9},{9,8},{10,11... | collective-permute-start | bytes 196616 | tf_op jit(solution)/shard_map/ppermute | solution.py:774

commit v3 on v2

v3 whole, which is shorter than its diff:
```python
import functools
import math

import jax
import jax.numpy as jnp
import numpy as np
from jax import lax
from jax.experimental import pallas as pl
from jax.experimental.pallas import tpu as pltpu
from jax.sharding import PartitionSpec as P

NCH = 512
ITERS = 2


damping = 0.5
epsilon = 1e-06


def from_behind(block, axis, distance):
    devices = range(lax.axis_size(axis))
    route = [(i - distance, i) for i in devices if i - distance in devices]
    return lax.ppermute(block, axis, route)


def filter_bank(extended, window_taps, kept_count, frames):
    transform_count = window_taps.shape[1]
    tap_count = window_taps.shape[0]
    local_inputs = extended.shape[0]
    kept = jnp.arange(kept_count, dtype=jnp.int32)
    indices = jnp.arange(transform_count, dtype=jnp.int32)
    phases = (kept[:, None] * indices[None, :] % transform_count).astype(jnp.float32) * (
        2.0 * math.pi / transform_count
    )
    cosine = jnp.cos(phases)
    sine_part = jnp.sin(phases)
    real_in = extended[:, :transform_count]
    imag_in = extended[:, transform_count:]
    real_sum = jnp.zeros((local_inputs, kept_count, frames), jnp.float32)
    imag_sum = jnp.zeros((local_inputs, kept_count, frames), jnp.float32)
    for tap_index in range(tap_count):
        tap_row = window_taps[tap_index][None, :]
        cos_block = (cosine * tap_row / math.sqrt(transform_count)).astype(jnp.bfloat16)
        sin_block = (sine_part * tap_row / math.sqrt(transform_count)).astype(jnp.bfloat16)
        part_real = real_in[:, :, tap_index : tap_index + frames]
        part_imag = imag_in[:, :, tap_index : tap_index + frames]
        real_sum = (
            real_sum
            + jnp.einsum("kn,inf->ikf", cos_block, part_real, preferred_element_type=jnp.float32)
            + jnp.einsum("kn,inf->ikf", sin_block, part_imag, preferred_element_type=jnp.float32)
        )
        imag_sum = (
            imag_sum
            + jnp.einsum("kn,inf->ikf", cos_block, part_imag, preferred_element_type=jnp.float32)
            - jnp.einsum("kn,inf->ikf", sin_block, part_real, preferred_element_type=jnp.float32)
        )
    return jnp.stack([real_sum, imag_sum], axis=2).astype(jnp.bfloat16)


def steering_angles(beam_steering, channels, input_count, chan_total):
    positions = jnp.arange(input_count, dtype=jnp.int32)
    column = positions // (input_count // 4)
    within = positions % (input_count // 4)
    phase_index = (
        beam_steering[0][:, None] * column[None, :] * 64
        + beam_steering[1][:, None] * within[None, :]
    ) % 256
    scaled = phase_index[None] * (chan_total + channels)[:, None, None]
    return scaled.astype(jnp.float32) * (2.0 * math.pi / (512 * chan_total))


def cross_rows(owned_rows, all_rows):
    paired = owned_rows.reshape(owned_rows.shape[0], owned_rows.shape[1], -1)
    rotated = jnp.stack([owned_rows[:, :, 1], -owned_rows[:, :, 0]], axis=2).reshape(paired.shape)
    left = jnp.stack([paired, rotated], axis=1)
    columns = all_rows.reshape(all_rows.shape[0], all_rows.shape[1], -1)
    return jnp.einsum("isck,jck->csij", left, columns, preferred_element_type=jnp.float32)


def form_beams(whole_set, gains_part, weights, beam_steering, channels, chan_total):
    input_count = whole_set.shape[0]
    angles = steering_angles(beam_steering, channels, input_count, chan_total)
    cosine = jnp.cos(angles)
    sine_part = jnp.sin(angles)
    scale_factor = 1.0 / math.sqrt(input_count)
    gain_real = (gains_part[:, 0] * weights)[:, None, :]
    gain_imaginary = (gains_part[:, 1] * weights)[:, None, :]
    steering_real = ((gain_real * cosine - gain_imaginary * sine_part) * scale_factor).astype(
        jnp.bfloat16
    )
    steering_imaginary = ((gain_real * sine_part + gain_imaginary * cosine) * scale_factor).astype(
        jnp.bfloat16
    )
    spectrum_real = whole_set[:, :, 0]
    spectrum_imaginary = whole_set[:, :, 1]
    volt_real = jnp.einsum(
        "jan,njg->jag", steering_real, spectrum_real, preferred_element_type=jnp.float32
    ) - jnp.einsum(
        "jan,njg->jag", steering_imaginary, spectrum_imaginary, preferred_element_type=jnp.float32
    )
    volt_imag = jnp.einsum(
        "jan,njg->jag", steering_real, spectrum_imaginary, preferred_element_type=jnp.float32
    ) + jnp.einsum(
        "jan,njg->jag", steering_imaginary, spectrum_real, preferred_element_type=jnp.float32
    )
    return volt_real * volt_real + volt_imag * volt_imag


def matvec(matrix, vector):
    return jnp.einsum("crj,cj->cr", matrix, vector, precision=lax.Precision.HIGHEST)


def general_shards(samples, window_taps, sky_model, prior_gains, beam_steering, input_flags):
    local_inputs = samples.shape[0]
    transform_count = samples.shape[2]
    frames = samples.shape[3]
    tap_count = window_taps.shape[0]
    kept_count = NCH
    time_count = lax.axis_size("tm")
    beam_count = lax.axis_size("beam")
    time_index = lax.axis_index("tm")
    beam_index = lax.axis_index("beam")
    chan_index = lax.axis_index("chan")
    weights = input_flags.astype(jnp.float32)
    stacked = samples.reshape(local_inputs, 2 * transform_count, frames)
    previous = from_behind(stacked[:, :, frames - tap_count + 1 :], "tm", 1)
    extended = jnp.concatenate([previous, stacked], axis=2)
    spectra = filter_bank(extended, window_taps, kept_count, frames).reshape(
        1, local_inputs, kept_count, 2, 1, frames
    )
    mixed = lax.all_to_all(spectra, ("chan", "tm"), split_axis=2, concat_axis=0, tiled=True)
    blocks = mixed.reshape(
        mixed.shape[0] // time_count, time_count, local_inputs, mixed.shape[2], 2, frames
    )
    turned = jnp.transpose(blocks, (0, 2, 3, 4, 1, 5))
    joined = lax.all_gather(turned, "beam", axis=1, tiled=True)
    input_count = joined.shape[0] * joined.shape[1]
    chan_local = joined.shape[2]
    whole_set = joined.reshape(input_count, chan_local, 2, joined.shape[4] * frames)
    half_rows = input_count // beam_count
    owned_rows = lax.dynamic_slice_in_dim(whole_set, beam_index * half_rows, half_rows, 0)
    terms = cross_rows(owned_rows, whole_set)
    visibilities = (terms / whole_set.shape[3]).astype(jnp.bfloat16)
    channels = (chan_index * time_count + time_index) * chan_local + jnp.arange(
        chan_local, dtype=jnp.int32
    )
    beam_power = form_beams(whole_set, prior_gains, weights, beam_steering, channels, kept_count)
    vis_used = lax.optimization_barrier(visibilities).astype(jnp.float32)
    model_values = sky_model.astype(jnp.float32)
    weighted = jnp.stack(
        [
            vis_used[:, 0] * model_values[:, 0] + vis_used[:, 1] * model_values[:, 1],
            vis_used[:, 1] * model_values[:, 0] - vis_used[:, 0] * model_values[:, 1],
        ],
        axis=1,
    )
    model_power = model_values[:, 0] * model_values[:, 0] + model_values[:, 1] * model_values[:, 1]
    row_start = beam_index * half_rows
    current = prior_gains
    updated = lax.dynamic_slice_in_dim(current, row_start, half_rows, 2)
    for step_index in range(ITERS):
        masked_real = current[:, 0] * weights
        masked_imag = current[:, 1] * weights
        vectors = jnp.stack([masked_real, masked_imag], axis=2)
        products = jnp.einsum("csrj,cjv->csrv", weighted, vectors, precision=lax.Precision.HIGHEST)
        numer_real = products[:, 0, :, 0] - products[:, 1, :, 1]
        numer_imag = products[:, 0, :, 1] + products[:, 1, :, 0]
        denom = (
            matvec(
                model_power,
                weights * (current[:, 0] * current[:, 0] + current[:, 1] * current[:, 1]),
            )
            + epsilon
        )
        older = lax.dynamic_slice_in_dim(current, row_start, half_rows, 2)
        updated = damping * older + (1.0 - damping) * jnp.stack(
            [numer_real / denom, numer_imag / denom], axis=1
        )
        if step_index + 1 < ITERS:
            current = lax.all_gather(updated, "beam", axis=2, tiled=True)
    return (visibilities, updated, beam_power)


LANES = 128
SUBLANES = 8
NEXT_ROWS = 4
MIB = 2**20
UPDATE_LIMIT = 14 * MIB
NT = (((1,), (1,)), ((), ()))
TN = (((0,), (0,)), ((), ()))
NN = (((1,), (0,)), ((), ()))


def mxu(left, right, dims):
    return lax.dot_general(left, right, dims, preferred_element_type=jnp.float32)


def transform_rows(kept_count, transform_count, owners, shares):
    by_owner = np.arange(kept_count).reshape(owners, -1)
    ends = np.cumsum(shares)
    kept = np.concatenate(
        [by_owner[:, end - share : end].reshape(-1) for share, end in zip(shares, ends)]
    )
    phases = (kept[:, None] * np.arange(transform_count)[None, :] % transform_count) * (
        2.0 * math.pi / transform_count
    )
    table = np.concatenate([np.cos(phases), np.sin(phases)], axis=1) / math.sqrt(transform_count)
    return jnp.asarray(table.astype(jnp.bfloat16))


def transformed(owners, frames, table, windowed_ref, turned_ref, copies=()):
    rows = table.shape[0]
    width = turned_ref.shape[1]
    share = rows // owners
    total = windowed_ref.shape[0] // width
    step = 4
    for frame in range(0, total, step):
        some = min(step, total - frame)
        for copy in copies[frame : frame + some]:
            copy.wait()
        block = mxu(table, windowed_ref[frame * width : (frame + some) * width, :], NT)
        for i in range(some):
            at = frame + i
            part = block[:, i * width : (i + 1) * width]
            if at < frames:
                turned_ref[pl.ds(at, rows, stride=frames), :] = part
            else:
                first = rows * frames + (at - frames) * share
                for owner in range(owners):
                    turned_ref[pl.ds(first + owner * (total - frames) * share, share), :] = part[
                        owner * share : (owner + 1) * share
                    ]


def filter_kernel(
    owners,
    x_hbm,
    taps_hbm,
    table_hbm,
    windowed_hbm,
    out_ref,
    x_ref,
    table_ref,
    taps_ref,
    frames_ref,
    windowed_ref,
    turned_ref,
    sems,
):
    inputs, _, frames, points = x_ref.shape
    taps = taps_ref.shape[0]
    width = 2 * inputs
    pieces = sems.shape[0] - 3
    group = inputs // pieces
    table_copy = pltpu.make_async_copy(
        table_hbm.at[pl.ds(0, table_ref.shape[0])], table_ref, sems.at[pieces]
    )
    copies = [
        pltpu.make_async_copy(
            x_hbm.at[pl.ds(i * group, group)], x_ref.at[pl.ds(i * group, group)], sems.at[i]
        )
        for i in range(pieces)
    ]
    taps_copy = pltpu.make_async_copy(taps_hbm, taps_ref, sems.at[pieces + 2])
    taps_copy.start()
    for copy in copies:
        copy.start()
    taps_copy.wait()

    def spread(i, carry):
        for part in range(2):
            block = x_ref[i, part].astype(jnp.float32)
            for piece in range(points // LANES):
                here = pl.ds(pl.multiple_of(i * frames, frames), frames)
                frames_ref[part, piece, here, :] = block[:, piece * LANES : (piece + 1) * LANES]
        return carry

    for i, copy in enumerate(copies):
        copy.wait()
        lax.fori_loop(i * group, (i + 1) * group, spread, 0, unroll=4)

    table_copy.start()

    def window(piece, carry):
        lanes = pl.ds(pl.multiple_of(piece * LANES, LANES), LANES)
        upper = pl.ds(pl.multiple_of(points + piece * LANES, LANES), LANES)
        weights = taps_ref[:, lanes]
        weights = [
            jnp.broadcast_to(weights[tap : tap + 1], (2 * SUBLANES, LANES)) for tap in range(taps)
        ]
        for first in range(0, inputs, 2 * SUBLANES):
            for part in range(2):
                values = [
                    frames_ref[
                        part, piece, pl.ds(first * frames + frame, 2 * SUBLANES, stride=frames), :
                    ]
                    for frame in range(frames)
                ]
                for frame in range(frames + taps - 1):
                    total = None
                    for tap in range(taps):
                        source = frame + tap - (taps - 1)
                        if 0 <= source < frames:
                            term = values[source] * weights[tap]
                            total = term if total is None else total + term
                    base = frame * width + first
                    rows = slice(base, base + 2 * SUBLANES)
                    swapped = slice(base + inputs, base + inputs + 2 * SUBLANES)
                    total = total.astype(jnp.bfloat16)
                    if part == 0:
                        windowed_ref[rows, lanes] = total
                        windowed_ref[swapped, upper] = -total
                    else:
                        windowed_ref[rows, upper] = total
                        windowed_ref[swapped, lanes] = total
        return carry

    lax.fori_loop(0, points // LANES, window, 0)
    keep = pltpu.make_async_copy(windowed_ref, windowed_hbm, sems.at[pieces + 1])
    keep.start()
    table_copy.wait()
    transformed(owners, frames, table_ref[...], windowed_ref, turned_ref)
    share = table_ref.shape[0] // owners
    main = share * frames
    extra = share * (taps - 1)
    for owner in range(owners):
        out_ref[owner, :main, :] = turned_ref[owner * main : (owner + 1) * main, :].astype(
            jnp.bfloat16
        )
        first = owners * main + owner * extra
        out_ref[owner, main : main + extra, :] = turned_ref[first : first + extra, :].astype(
            jnp.bfloat16
        )
    keep.wait()


def rows_copies(source, target, sems, first=0):
    size = target.shape[0] // sems.shape[0]
    return [
        pltpu.make_async_copy(
            source.at[pl.ds(first + i * size, size)], target.at[pl.ds(i * size, size)], sems.at[i]
        )
        for i in range(sems.shape[0])
    ]


def spill_kernel(first, start, windowed_hbm, table_hbm, out_ref, windowed_ref, table_ref, sems):
    copies = rows_copies(windowed_hbm, windowed_ref, sems.at[pl.ds(0, 1)], first)
    copies += rows_copies(table_hbm, table_ref, sems.at[pl.ds(1, 1)], start)
    for copy in copies:
        copy.start()
    for copy in copies:
        copy.wait()
    frames, _, width = out_ref.shape
    block = mxu(table_ref[...], windowed_ref[...], NT)
    for frame in range(frames):
        out_ref[frame] = block[:, frame * width : (frame + 1) * width].astype(jnp.bfloat16)


def filter_more_kernel(
    owners, start, windowed_hbm, table_hbm, turned_ref, windowed_ref, table_ref, sems
):
    frames = sems.shape[0] - 1
    copies = rows_copies(windowed_hbm, windowed_ref, sems.at[pl.ds(0, frames)])
    table_copies = rows_copies(table_hbm, table_ref, sems.at[pl.ds(frames, 1)], start)
    for copy in table_copies + copies:
        copy.start()
    for copy in table_copies:
        copy.wait()
    transformed(owners, frames, table_ref[...], windowed_ref, turned_ref, copies)


def added_kernel(turned_ref, added_ref, out_ref, total_ref):
    owners, main, _ = out_ref.shape
    nexts, rows, _ = added_ref.shape
    frames = turned_ref.shape[0] // rows
    total_ref[...] = turned_ref[...]
    for frame in range(nexts):
        here = pl.ds(frame, rows, stride=frames)
        total_ref[here, :] = turned_ref[here, :] + added_ref[frame].astype(jnp.float32)
    for owner in range(owners):
        out_ref[owner] = total_ref[owner * main : (owner + 1) * main, :].astype(jnp.bfloat16)


def filtered(samples, window_taps, kept_count, owners, shares):
    inputs, _, points, frames = samples.shape
    taps = window_taps.shape[0]
    width = 2 * inputs
    table = transform_rows(kept_count, points, owners, shares)
    by_frame = jnp.transpose(samples, (0, 1, 3, 2))
    by_frame = pltpu.with_memory_space_constraint(by_frame, pltpu.HBM)
    table = pltpu.with_memory_space_constraint(table, pltpu.HBM)
    window_taps = pltpu.with_memory_space_constraint(window_taps, pltpu.HBM)
    pieces = points // LANES
    anywhere = pl.BlockSpec(memory_space=pl.ANY)
    vmem = pl.BlockSpec(memory_space=pltpu.VMEM)
    windowed_shape = ((frames + taps - 1) * width, 2 * points)
    rows = owners * shares[0]
    windowed, first = pl.pallas_call(
        functools.partial(filter_kernel, owners),
        out_shape=[
            pltpu.HBM(windowed_shape, jnp.bfloat16),
            jax.ShapeDtypeStruct((owners, shares[0] * (frames + taps - 1), width), jnp.bfloat16),
        ],
        in_specs=[anywhere, anywhere, anywhere],
        out_specs=[anywhere, vmem],
        scratch_shapes=[
            pltpu.VMEM(by_frame.shape, jnp.bfloat16),
            pltpu.VMEM((rows, 2 * points), jnp.bfloat16),
            pltpu.VMEM(window_taps.shape, jnp.float32),
            pltpu.VMEM((2, pieces, inputs * frames, LANES), jnp.float32),
            pltpu.VMEM(windowed_shape, jnp.bfloat16),
            pltpu.VMEM((rows * (frames + taps - 1), width), jnp.float32),
            pltpu.SemaphoreType.DMA((7,)),
        ],
        compiler_params=pltpu.CompilerParams(vmem_limit_bytes=32 * MIB),
        name="filter",
    )(by_frame, window_taps, table)
    windowed = pltpu.with_memory_space_constraint(windowed, pltpu.HBM)

    def more(chunk, start):
        rows = owners * shares[chunk]
        spill = pl.pallas_call(
            functools.partial(spill_kernel, frames * width, start),
            out_shape=jax.ShapeDtypeStruct((taps - 1, rows, width), jnp.bfloat16),
            in_specs=[anywhere, anywhere],
            out_specs=vmem,
            scratch_shapes=[
                pltpu.VMEM(((taps - 1) * width, 2 * points), jnp.bfloat16),
                pltpu.VMEM((rows, 2 * points), jnp.bfloat16),
                pltpu.SemaphoreType.DMA((2,)),
            ],
            compiler_params=pltpu.CompilerParams(vmem_limit_bytes=24 * MIB),
            name="spill",
        )(windowed, table)
        added = from_behind(spill, "tm", 1)
        turned = pl.pallas_call(
            functools.partial(filter_more_kernel, owners, start),
            out_shape=jax.ShapeDtypeStruct((rows * frames, width), jnp.float32),
            in_specs=[anywhere, anywhere],
            out_specs=vmem,
            scratch_shapes=[
                pltpu.VMEM((frames * width, 2 * points), jnp.bfloat16),
                pltpu.VMEM((rows, 2 * points), jnp.bfloat16),
                pltpu.SemaphoreType.DMA((frames + 1,)),
            ],
            compiler_params=pltpu.CompilerParams(vmem_limit_bytes=24 * MIB),
            name="filter_more",
        )(windowed, table)
        return pl.pallas_call(
            added_kernel,
            out_shape=jax.ShapeDtypeStruct((owners, shares[chunk] * frames, width), jnp.bfloat16),
            in_specs=[vmem, vmem],
            out_specs=vmem,
            scratch_shapes=[pltpu.VMEM((rows * frames, width), jnp.float32)],
            compiler_params=pltpu.CompilerParams(vmem_limit_bytes=24 * MIB),
            name="added",
        )(turned, added)

    sent = [first]
    start = rows
    for chunk in range(1, len(shares)):
        sent.append(more(chunk, start))
        start += owners * shares[chunk]
    return sent


def gain_terms(real, imag, gains, flags):
    weights = flags.astype(jnp.float32)
    gain_real = gains[0:1] * weights
    gain_imag = gains[1:2] * weights
    turned_real = real * gain_real + imag * gain_imag
    turned_imag = imag * gain_real - real * gain_imag
    power = weights * (gains[0:1] * gains[0:1] + gains[1:2] * gains[1:2])
    return turned_real, turned_imag, power


def denominators(power, model_real, model_imag):
    model_power = model_real * model_real + model_imag * model_imag
    terms = model_power * jnp.broadcast_to(power.astype(jnp.bfloat16), model_power.shape)
    folded = terms[:, :LANES]
    for first in range(LANES, terms.shape[1], LANES):
        folded = folded + terms[:, first : first + LANES]
    return mxu(jnp.ones((SUBLANES, LANES), jnp.bfloat16), folded, NT)[0:1] + epsilon


def updated_gains(own, turned, model_real, model_imag, denom, older):
    real, imag = turned
    straight = jnp.concatenate([real, imag], axis=0).astype(jnp.bfloat16)
    crossed = jnp.concatenate([-imag, real], axis=0).astype(jnp.bfloat16)
    modelled = mxu(straight, model_real, NT) + mxu(crossed, model_imag, NT)
    frames = real.shape[0]
    modelled_real = modelled[:frames]
    modelled_imag = modelled[frames:]
    own_real, own_imag = own
    numer_real = jnp.sum(own_real * modelled_real + own_imag * modelled_imag, axis=0, keepdims=True)
    numer_imag = jnp.sum(own_imag * modelled_real - own_real * modelled_imag, axis=0, keepdims=True)
    numer = jnp.concatenate([numer_real, numer_imag], axis=0) / frames
    return damping * older + (1.0 - damping) * (numer / denom)


def own_half(values, core):
    half = values.shape[1] // 2
    return jnp.where(core == 0, values[:, :half], values[:, half:])


def model_kernel(base, own_hbm, model_hbm, model_ref, sem):
    del own_hbm
    count = min(MODEL_BLOCK, model_ref.shape[0])
    copy = pltpu.make_async_copy(
        model_hbm.at[pl.ds(base, count)], model_ref.at[pl.ds(0, count)], sem
    )
    copy.start()
    copy.wait()


def first_kernel(
    times, base, core_ref, own_ref, other_ref, model_hbm, gains_ref, flags_ref, here_ref, *refs
):
    del here_ref
    spectra_ref, updated_ref, model_ref, next_ref, sems = refs
    core = core_ref[0]
    share = spectra_ref.shape[0]
    sources, rows, width = own_ref.shape
    frames = spectra_ref.shape[1] // 2 // times
    nexts = rows // share - frames
    columns = sources // times
    lane = lax.broadcasted_iota(jnp.int32, (frames, width), 1)
    row = lax.broadcasted_iota(jnp.int32, (frames, width), 0)
    low = lane < width // 2
    count = BLOCK

    def copy(i):
        here = pl.ds(i * VIS_BLOCK, VIS_BLOCK)
        there = pl.ds(base + i * VIS_BLOCK, VIS_BLOCK)
        return pltpu.make_async_copy(model_hbm.at[there], model_ref.at[here], sems.at[i])

    groups = share // VIS_BLOCK
    there = min(MODEL_BLOCK, share) // VIS_BLOCK
    ahead = 4
    for i in range(there, min(there + ahead, groups)):
        copy(i).start()
    if nexts:
        for source in range(sources):
            for side, ref in enumerate((own_ref, other_ref)):
                next_ref[side, source] = ref[source, share * frames :, :].astype(jnp.float32)

    def assemble(i):
        main_rows = pl.ds(pl.multiple_of(i * (count * frames), count * frames), count * frames)

        def loaded(side, column, time):
            ref = (own_ref, other_ref)[side]
            source = column * times + time
            block = ref[source, main_rows, :].astype(jnp.float32)
            extra = []
            if time > 0:
                extra = [
                    next_ref[
                        side, source - 1, pl.ds(pl.multiple_of(share * k + i * count, count), count), :
                    ]
                    for k in range(nexts)
                ]
            return block, extra

        def one(value, c):
            block, extra = value
            block = block[c * frames : (c + 1) * frames]
            for k, more in enumerate(extra):
                block = block + jnp.where(row == k, more[c : c + 1], 0.0)
            return block

        blocks = {
            (column, time): (loaded(0, column, time), loaded(1, column, time))
            for column in range(columns)
            for time in range(times)
        }
        for c in range(count):
            real_rows = []
            imag_rows = []
            for time in range(times):
                reals = []
                imags = []
                for column in range(columns):
                    own, other = blocks[column, time]
                    own = one(own, c)
                    other = one(other, c)
                    first = jnp.where(core == 0, own, other)
                    second = jnp.where(core == 0, other, own)
                    reals.append(jnp.where(low, first, pltpu.roll(second, width // 2, 1)))
                    imags.append(jnp.where(low, pltpu.roll(first, width // 2, 1), second))
                real_rows.append(jnp.concatenate(reals, axis=1))
                imag_rows.append(jnp.concatenate(imags, axis=1))
            spectra = jnp.concatenate(real_rows + imag_rows, axis=0)
            spectra_ref[i * count + c] = spectra.astype(jnp.bfloat16)

    def update(i):
        for part in range(count // VIS_BLOCK):
            group = i * (count // VIS_BLOCK) + part

            @pl.when(group >= there)
            def _():
                copy(group).wait()

                @pl.when(group + ahead < groups)
                def _():
                    copy(group + ahead).start()

        for c in range(count):
            here = i * count + c
            values = spectra_ref[here].astype(jnp.float32)
            half = values.shape[0] // 2
            real = values[:half]
            imag = values[half:]
            gains = gains_ref[base + here]
            flags = flags_ref[pl.ds(base + here, 1), :]
            model_real = model_ref[here, 0]
            model_imag = model_ref[here, 1]
            turned_real, turned_imag, power = gain_terms(real, imag, gains, flags)
            updated_ref[here] = updated_gains(
                (own_half(real, core), own_half(imag, core)),
                (turned_real, turned_imag),
                model_real,
                model_imag,
                denominators(power, model_real, model_imag),
                own_half(gains, core),
            )

    def step(i, carry):
        update(i)
        assemble(i + 1)
        return carry

    last = share // count - 1
    assemble(0)
    lax.fori_loop(0, last, step, 0)
    update(last)


def second_kernel(
    base, core_ref, spectra_ref, model_ref, own_ref, other_ref, flags_ref, *refs
):
    visibilities_ref, updated_ref = refs[-2:]
    core = core_ref[0]
    count = visibilities_ref.shape[0]
    start = pl.program_id(0) * count
    for c in range(count):
        here = start + c
        spectra = spectra_ref[here]
        half = spectra.shape[0] // 2
        values = spectra.astype(jnp.float32)
        real = values[:half]
        imag = values[half:]
        own_real = own_half(real, core)
        own_imag = own_half(imag, core)
        paired = (jnp.concatenate([own_real, own_imag], axis=0) / half).astype(jnp.bfloat16)
        rotated = (jnp.concatenate([own_imag, -own_real], axis=0) / half).astype(jnp.bfloat16)
        visibilities_ref[c, 0] = mxu(paired, spectra, TN).astype(jnp.bfloat16)
        visibilities_ref[c, 1] = mxu(rotated, spectra, TN).astype(jnp.bfloat16)
        own = own_ref[here]
        other = other_ref[here]
        first = jnp.where(core == 0, own, other)
        second = jnp.where(core == 0, other, own)
        gains = jnp.concatenate([first, second], axis=1)
        turned_real, turned_imag, power = gain_terms(real, imag, gains, flags_ref[pl.ds(base + here, 1), :])
        model_real = model_ref[here, 0]
        model_imag = model_ref[here, 1]
        updated_ref[c] = updated_gains(
            (own_real, own_imag),
            (turned_real, turned_imag),
            model_real,
            model_imag,
            denominators(power, model_real, model_imag),
            own,
        )


def series_length(reach):
    terms = 1
    while reach**terms / math.factorial(terms) >= 2.0**-22:
        terms += 1
    return terms


def turns(count, period):
    quarter = period // 4
    quadrant = lax.shift_right_logical(count + period // 8, quarter.bit_length() - 1)
    angle = (count - quadrant * quarter).astype(jnp.float32) * (2.0 * math.pi / period)
    square = angle * angle
    sine_part = jnp.full_like(angle, 1.0 / math.factorial(9))
    cosine = jnp.full_like(angle, 1.0 / math.factorial(8))
    for power in (7, 5, 3, 1):
        sign = -1.0 if power % 4 == 3 else 1.0
        sine_part = sine_part * square + sign / math.factorial(power)
        cosine = cosine * square + sign / math.factorial(power - 1)
    sine_part = sine_part * angle
    odd = (quadrant & 1) == 1
    real = jnp.where(odd, sine_part, cosine)
    imag = jnp.where(odd, cosine, sine_part)
    real = jnp.where(((quadrant + 1) & 2) == 2, -real, real)
    imag = jnp.where((quadrant & 2) == 2, -imag, imag)
    return real, imag


def steering_tables(centre, steering_ref, table_ref, step, reach):
    inputs = table_ref.shape[1] // 2
    beams = table_ref.shape[2] // 2
    quarter = inputs // 4
    for column in range(4):
        for first in range(0, quarter, 4 * SUBLANES):
            shape = (4 * SUBLANES, beams)
            within = lax.broadcasted_iota(jnp.int32, shape, 0) + first
            phase_index = (steering_ref[0:1, :] * (column * 64) + steering_ref[1:2, :] * within) & 255
            cosine, sine_part = turns(phase_index * centre, round(4.0 * math.pi / step))
            offset = (phase_index - 128).astype(jnp.float32) * (reach * step)
            factor = None
            at = column * quarter + first
            rows = slice(at, at + shape[0])
            lower = slice(inputs + at, inputs + at + shape[0])
            for term in range(table_ref.shape[0]):
                real, imag = (
                    (cosine, sine_part),
                    (-sine_part, cosine),
                    (-cosine, -sine_part),
                    (sine_part, -cosine),
                )[term % 4]
                if term:
                    factor = offset if factor is None else factor * offset / term
                    real = factor * real
                    imag = factor * imag
                real = real.astype(jnp.bfloat16)
                imag = imag.astype(jnp.bfloat16)
                table_ref[term, rows, :beams] = real
                table_ref[term, rows, beams:] = imag
                table_ref[term, lower, :beams] = -imag
                table_ref[term, lower, beams:] = real


def beams_kernel(step, reach, base, centre_ref, spectra_ref, gains_ref, flags_ref, steering_ref, *refs):
    power_hbm, power_ref, left_ref, table_ref, sem = refs[-5:]
    steering_tables(centre_ref[0], steering_ref, table_ref, step, reach)
    count, doubled, inputs = spectra_ref.shape
    frames = doubled // 2
    scale = 1.0 / math.sqrt(inputs)
    middle = 0.5 * (count - 1)
    terms = table_ref.shape[0]
    for c in range(count):
        values = spectra_ref[c].astype(jnp.float32)
        real = values[:frames]
        imag = values[frames:]
        at = base + c
        weights = flags_ref[at : at + 1].astype(jnp.float32) * scale
        gain_real = gains_ref[at, 0:1] * weights
        gain_imag = gains_ref[at, 1:2] * weights
        lit_real = real * gain_real - imag * gain_imag
        lit_imag = real * gain_imag + imag * gain_real
        rows = slice(c * frames, (c + 1) * frames)
        for term in range(terms):
            power = ((c - middle) / max(middle, 0.5)) ** term
            left_ref[term, rows, :inputs] = (lit_real * power).astype(jnp.bfloat16)
            left_ref[term, rows, inputs:] = (lit_imag * power).astype(jnp.bfloat16)
    total = mxu(left_ref[0], table_ref[0], NN)
    for term in range(1, terms):
        total = total + mxu(left_ref[term], table_ref[term], NN)
    beams = total.shape[1] // 2
    real = total[:, :beams]
    imag = total[:, beams:]
    power_ref[...] = (real * real + imag * imag).reshape(count, frames, beams)
    copy = pltpu.make_async_copy(power_ref, power_hbm.at[pl.ds(base, count)], sem)
    copy.start()
    copy.wait()


def formed_beams(chunk, gains, flags, steering, step, earlier):
    base, centre, spectra = chunk
    share, doubled, input_count = spectra.shape
    frame_count = doubled // 2
    beams = steering.shape[1]
    earlier = [] if earlier is None else [earlier]
    reach = max(0.5 * (share - 1), 0.5)
    terms = series_length(128 * reach * step)
    vmem = pl.BlockSpec(memory_space=pltpu.VMEM)
    return pl.pallas_call(
        functools.partial(beams_kernel, step, reach, base),
        in_specs=[pl.BlockSpec(memory_space=pltpu.SMEM)] + [vmem] * 4
        + [pl.BlockSpec(memory_space=pl.ANY)] * len(earlier),
        out_specs=pl.BlockSpec(memory_space=pl.ANY),
        out_shape=jax.ShapeDtypeStruct((gains.shape[0], frame_count, beams), jnp.float32),
        input_output_aliases={5: 0} if earlier else {},
        scratch_shapes=[
            pltpu.VMEM((share, frame_count, beams), jnp.float32),
            pltpu.VMEM((terms, share * frame_count, 2 * input_count), jnp.bfloat16),
            pltpu.VMEM((terms, 2 * input_count, 2 * beams), jnp.bfloat16),
            pltpu.SemaphoreType.DMA,
        ],
        compiler_params=pltpu.CompilerParams(vmem_limit_bytes=UPDATE_LIMIT),
        name="beams",
    )(centre, spectra, gains, flags, steering, *earlier)


def chunk_shards(samples, window_taps, sky_model, prior_gains, beam_steering, input_flags):
    frames = samples.shape[3]
    chan_local, _, half_rows, input_count = sky_model.shape
    times = lax.axis_size("tm")
    owners = lax.axis_size("chan") * times
    core = lax.axis_index("beam").astype(jnp.int32).reshape(1)
    first_channel = (lax.axis_index("chan") * times + lax.axis_index("tm")) * chan_local
    kept_count = chan_local * owners
    frame_count = frames * times
    beams = beam_steering.shape[1]
    shares = chunk_shares(chan_local)
    bases = [sum(shares[:chunk]) for chunk in range(len(shares))]
    centres = [
        (2 * (kept_count + first_channel + base) + share - 1).astype(jnp.int32).reshape(1)
        for base, share in zip(bases, shares)
    ]
    sent = filtered(samples, window_taps, kept_count, owners, shares)
    swap = [(0, 1), (1, 0)]
    smem = pl.BlockSpec(memory_space=pltpu.SMEM)
    vmem = pl.BlockSpec(memory_space=pltpu.VMEM)
    anywhere = pl.BlockSpec(memory_space=pl.ANY)
    step = 2.0 * math.pi / (512 * kept_count)

    sent[0], gains, flags, steering, core, centres = lax.optimization_barrier(
        (sent[0], prior_gains, input_flags, beam_steering, core, centres)
    )
    visibilities = None
    beam_power = None
    gains_new = None
    before = None
    for chunk, (base, share) in enumerate(zip(bases, shares)):
        own = lax.all_to_all(sent[chunk], ("chan", "tm"), 0, 0, tiled=True)
        if before is not None:
            beam_power = formed_beams(before, gains, flags, steering, step, beam_power)
            own, gains_new, beam_power = lax.optimization_barrier((own, gains_new, beam_power))
        other = lax.ppermute(own, "beam", swap)
        model_shape = (share, *sky_model.shape[1:])
        model = pl.pallas_call(
            functools.partial(model_kernel, base),
            in_specs=[anywhere, anywhere],
            out_specs=vmem,
            out_shape=pltpu.VMEM(model_shape, sky_model.dtype),
            scratch_shapes=[pltpu.SemaphoreType.DMA],
            compiler_params=pltpu.CompilerParams(vmem_limit_bytes=UPDATE_LIMIT),
            name="model",
        )(own, sky_model)
        model = pltpu.with_memory_space_constraint(model, pltpu.VMEM)
        half_shape = jax.ShapeDtypeStruct((share, 2, half_rows), jnp.float32)
        spectra, gains_own, model = pl.pallas_call(
            functools.partial(first_kernel, times, base),
            in_specs=[smem, vmem, vmem, anywhere, vmem, vmem, vmem],
            out_specs=[vmem, vmem, vmem],
            out_shape=[
                jax.ShapeDtypeStruct((share, 2 * frame_count, input_count), jnp.bfloat16),
                half_shape,
                pltpu.VMEM(model_shape, sky_model.dtype),
            ],
            input_output_aliases={6: 2},
            scratch_shapes=[
                pltpu.VMEM((2, owners, max(own.shape[1] - share * frames, SUBLANES), own.shape[2]), jnp.float32),
                pltpu.SemaphoreType.DMA((share // VIS_BLOCK,)),
            ],
            compiler_params=pltpu.CompilerParams(vmem_limit_bytes=UPDATE_LIMIT),
            name="first_update",
        )(core, own, other, sky_model, gains, flags, model)
        model = pltpu.with_memory_space_constraint(model, pltpu.VMEM)
        gains_other = lax.ppermute(gains_own, "beam", swap)
        before = (base, centres[chunk], spectra)
        if chunk == len(shares) - 1:
            beam_power = formed_beams(before, gains, flags, steering, step, beam_power)
        earlier = [] if visibilities is None else [visibilities, gains_new]
        block = VIS_BLOCK
        block_spec = pl.BlockSpec(
            (block, 2, half_rows, input_count), lambda i, at=base // block: (at + i, 0, 0, 0)
        )
        visibilities, gains_new = pl.pallas_call(
            functools.partial(second_kernel, base),
            grid=(share // block,),
            in_specs=[smem, vmem, vmem, vmem, vmem, vmem] + [anywhere] * len(earlier),
            out_specs=[
                block_spec,
                pl.BlockSpec((block, 2, half_rows), lambda i, at=base // block: (at + i, 0, 0)),
            ],
            out_shape=[
                jax.ShapeDtypeStruct((chan_local, 2, half_rows, input_count), jnp.bfloat16),
                jax.ShapeDtypeStruct((chan_local, 2, half_rows), jnp.float32),
            ],
            input_output_aliases={6: 0, 7: 1} if earlier else {},
            compiler_params=pltpu.CompilerParams(vmem_limit_bytes=UPDATE_LIMIT),
            name="second_update",
        )(core, spectra, model, gains_own, gains_other, flags, *earlier)
    return (
        visibilities,
        gains_new,
        jnp.transpose(beam_power, (0, 2, 1)),
    )


BLOCK = 8
VIS_BLOCK = 4
MODEL_BLOCK = 8


def chunk_shares(chan_local):
    blocks = chan_local // BLOCK
    first = blocks * 3 // 8
    return [first * BLOCK, (blocks - first) * BLOCK]


def shards(samples, window_taps, sky_model, prior_gains, beam_steering, input_flags):
    inputs, _, points, frames = samples.shape
    chan_local, _, half_rows, input_count = sky_model.shape
    frame_count = frames * lax.axis_size("tm")
    owners = lax.axis_size("chan") * lax.axis_size("tm")
    fits = (
        ITERS == 2
        and 2 * inputs == LANES
        and points % LANES == 0
        and frames == SUBLANES
        and window_taps.shape[0] == NEXT_ROWS
        and lax.axis_size("beam") == 2
        and chan_local % (8 * BLOCK) == 0
        and half_rows % LANES == 0
        and frame_count & (frame_count - 1) == 0
        and chan_local * owners & (chan_local * owners - 1) == 0
        and half_rows % (4 * LANES // 2) == 0
        and beam_steering.shape[1] % LANES == 0
    )
    form = chunk_shards if fits else general_shards
    return form(samples, window_taps, sky_model, prior_gains, beam_steering, input_flags)


def solution(mesh):
    return jax.shard_map(
        shards,
        mesh=mesh,
        in_specs=(
            P(("group", "chan", "beam"), None, None, "tm"),
            P(),
            P(("group", "chan", "tm"), None, "beam", None),
            P(("group", "chan", "tm"), None, None),
            P(None, ("group", "beam")),
            P(("group", "chan", "tm"), None),
        ),
        out_specs=(
            P(("group", "chan", "tm"), None, "beam", None),
            P(("group", "chan", "tm"), None, "beam"),
            P(("group", "chan", "tm"), "beam", None),
        ),
        check_vma=False,
    )
```

time: 106 us -> 88.1 us (0.83)
  Pallas kernels: 77.7 us -> 65.9 us
  local copies, waits for them, and re-layouts: 8.56 us -> 0.02 us
  starting transfers between devices: 14.1 us -> 17.9 us
    unnamed x18 -> x6, local copies, waits for them, and re-layouts: 7.51 us -> 0.02 us
    pallas_call x6 -> x7, Pallas kernels: 25.2 us -> 21.2 us  [the longest x2 8.95 us: formed_beams(): pl.pallas_call(functools.partial(beams_kernel, step, reach, base), in_spe...]
    ppermute x0 -> x1, starting transfers between devices: none -> 3.94 us  [from_behind(): return lax.ppermute(block, axis, route)]
    pallas_call x2, Pallas kernels: 18.7 us -> 14.8 us  [chunk_shards(): pl.pallas_call(functools.partial(first_kernel, times, base), in_specs=[sm...]
    pallas_call x2, Pallas kernels: 25.3 us -> 22.8 us  [chunk_shards(): pl.pallas_call(functools.partial(second_kernel, base), grid=(share // blo...]
    ppermute x2, waiting for transfers between devices: 2.28 us -> 0.01 us  [chunk_shards(): other = lax.ppermute(own, 'beam', swap)]
    all_to_all x2, waiting for transfers between devices: 0.02 us -> 1.6 us  [chunk_shards(): own = lax.all_to_all(sent[chunk], ('chan', 'tm'), 0, 0, tiled=True)]
    ppermute x0 -> x1, waiting for transfers between devices: none -> 1.5 us  [from_behind(): return lax.ppermute(block, axis, route)]
  transfers between devices with their start and end apart: 6 -> 7, of which waited for: 2 -> 2; matrix products, arithmetic and copies ran while one was open for 0% -> 0% of each run, Pallas kernels for 44% -> 41%
where the time goes in v3:
time: 88.1 us; the launch traced here: 87.7 us
  Pallas kernels  65.9 us (75%)
  starting transfers between devices  17.9 us (20%)
  waiting for transfers between devices  3.11 us (4%)
    pallas_call x2, Pallas kernels, chunk_shards(): pl.pallas_call(functools.partial(second_kernel, base), grid=(share // blo...  22.8 us
    pallas_call x2, Pallas kernels, chunk_shards(): pl.pallas_call(functools.partial(first_kernel, times, base), in_specs=[sm...  14.8 us
    all_to_all x2, starting transfers between devices, chunk_shards(): own = lax.all_to_all(sent[chunk], ('chan', 'tm'), 0, 0, tiled=True)  12.8 us
    pallas_call x2, Pallas kernels, formed_beams(): pl.pallas_call(functools.partial(beams_kernel, step, reach, base), in_spe...  8.95 us
    pallas_call x1, Pallas kernels, filtered(): pl.pallas_call(functools.partial(filter_kernel, owners), out_shape=[pltpu...  7.11 us
    pallas_call x2, Pallas kernels, chunk_shards(): pl.pallas_call(functools.partial(model_kernel, base), in_specs=[anywhere,...  4.43 us
    ppermute x1, starting transfers between devices, from_behind(): return lax.ppermute(block, axis, route)  3.94 us
    pallas_call x1, Pallas kernels, more(): pl.pallas_call(functools.partial(filter_more_kernel, owners, start), out_...  3.83 us
  transfers between devices with their start and end apart: 7, of which 2 were waited for; matrix products, arithmetic and copies ran while one was open for 0% of the time, Pallas kernels for 41%

profile of v3, /device:TPU:0, one launch (start us, length us, event | category | flops | bytes accessed | tf_op | source)
XLA Modules:
  0.0 87.7 jit_solution(15625741777266244998)
XLA Ops:
  0.6 7.1 %filter.1 = (bf16[1408,2048]{1,0:T(8,128)(2,1)}, bf16[8,264,128]{2,1,0:T(8,128)(2,1)}) custom-call(bf16[64,2,8,1024]{3,2,1,0:T(8,128)(2,1)} %bitcast.6, f32[4,1024]{1,0:T(4,128)} %taps_hbm.1, bf16[512,2048]{1,0:T(8,128)(2,1)} %constant.30.clone.table_hbm), custom_call_target="tpu_custom_call" | custom-call | tf_op jit(solution)/shard_map/filter/pallas_call | solution.py:399
  7.8 7.3 %all-to-all-start.1 = ((bf16[8,264,128]{2,1,0:T(8,128)(2,1)}), bf16[8,264,128]{2,1,0:T(8,128)(2,1)S(1)}, u32[]{:S(2)}, u32[]{:S(2)}) async-start(bf16[8,264,128]{2,1,0:T(8,128)(2,1)} %get-tuple-element.28), calls=%async_computation.1 | async-start | bytes 1081344 | tf_op jit(solution)/shard_map/all_to_all | solution.py:831
  15.0 2.7 %spill.1 = bf16[3,320,128]{2,1,0:T(8,128)(2,1)S(1)} custom-call(bf16[1408,2048]{1,0:T(8,128)(2,1)} %get-tuple-element.27.windowed_hbm, bf16[512,2048]{1,0:T(8,128)(2,1)} %constant.30.clone.table_hbm), custom_call_target="tpu_custom_call" | custom-call | tf_op jit(solution)/shard_map/spill/pallas_call | solution.py:423
  17.7 3.9 %collective-permute-start = (bf16[3,320,128]{2,1,0:T(8,128)(2,1)S(1)}, bf16[3,320,128]{2,1,0:T(8,128)(2,1)S(1)}, u32[]{:S(2)}, u32[]{:S(2)}) collective-permute-start(bf16[3,320,128]{2,1,0:T(8,128)(2,1)S(1)} %spill.1), channel_id=1, source_target_pairs={{0,2},{1,3},{4,6},{5,7},{8,10},{9,11},{12,14},{13,15},{16,18},{17,... | collective-permute-start | bytes 737288 | tf_op jit(solution)/shard_map/ppermute | solution.py:23
  21.7 3.8 %filter_more.1.turned_ref = f32[2560,128]{1,0:T(8,128)S(1)} custom-call(bf16[1408,2048]{1,0:T(8,128)(2,1)} %get-tuple-element.27.windowed_hbm, bf16[512,2048]{1,0:T(8,128)(2,1)} %constant.30.clone.table_hbm), custom_call_target="tpu_custom_call" | custom-call | tf_op jit(solution)/shard_map/filter_more/pallas_call | solution.py:437
  25.5 1.5 %collective-permute-done.added_ref = bf16[3,320,128]{2,1,0:T(8,128)(2,1)S(1)} collective-permute-done((bf16[3,320,128]{2,1,0:T(8,128)(2,1)S(1)}, bf16[3,320,128]{2,1,0:T(8,128)(2,1)S(1)}, u32[]{:S(2)}, u32[]{:S(2)}) %collective-permute-start) | collective-permute-done | bytes 245792 | tf_op jit(solution)/shard_map/ppermute | solution.py:23
  27.0 1.3 %added.1 = bf16[8,320,128]{2,1,0:T(8,128)(2,1)} custom-call(f32[2560,128]{1,0:T(8,128)S(1)} %filter_more.1.turned_ref, bf16[3,320,128]{2,1,0:T(8,128)(2,1)S(1)} %collective-permute-done.added_ref), custom_call_target="tpu_custom_call" | custom-call | tf_op jit(solution)/shard_map/added/pallas_call | solution.py:450
  28.3 1.6 %all-to-all-done.1.own_hbm.own_ref = bf16[8,264,128]{2,1,0:T(8,128)(2,1)S(1)} async-done(((bf16[8,264,128]{2,1,0:T(8,128)(2,1)}), bf16[8,264,128]{2,1,0:T(8,128)(2,1)S(1)}, u32[]{:S(2)}, u32[]{:S(2)}) %all-to-all-start.1) | async-done | bytes 540704 | tf_op jit(solution)/shard_map/all_to_all | solution.py:831
  29.9 5.5 %all-to-all-start = ((bf16[8,320,128]{2,1,0:T(8,128)(2,1)}), bf16[8,320,128]{2,1,0:T(8,128)(2,1)S(1)}, u32[]{:S(2)}, u32[]{:S(2)}) async-start(bf16[8,320,128]{2,1,0:T(8,128)(2,1)} %added.1), calls=%async_computation | async-start | bytes 1310720 | tf_op jit(solution)/shard_map/all_to_all | solution.py:831
  35.4 0.0 copy-start.1
  35.4 0.1 collective-permute-start.1
  35.5 2.2 %model.2.here_ref = bf16[24,2,256,512]{3,2,1,0:T(8,128)(2,1)S(1)} custom-call(bf16[8,264,128]{2,1,0:T(8,128)(2,1)S(1)} %all-to-all-done.1.own_hbm.own_ref, bf16[64,2,256,512]{3,2,1,0:T(8,128)(2,1)} %model_hbm.7), custom_call_target="tpu_custom_call" | custom-call | tf_op jit(solution)/shard_map/model/pallas_call | solution.py:837
  37.7 0.0 copy-start.2
  37.7 5.6 %first_update.2 = (bf16[24,32,512]{2,1,0:T(8,128)(2,1)S(1)}, f32[24,2,256]{2,1,0:T(2,128)S(1)}, bf16[24,2,256,512]{3,2,1,0:T(8,128)(2,1)S(1)}) custom-call(s32[1]{0:T(128)} %bitcast.1.core_ref, bf16[8,264,128]{2,1,0:T(8,128)(2,1)S(1)} %all-to-all-done.1.own_hbm.own_ref, ...), custom_call_target="tpu_custom_call", output_to_operand_aliasing={{2}: (6, {})} | custom-call | tf_op jit(solution)/shard_map/first_update/pallas_call | solution.py:848
  43.4 0.5 collective-permute-start.2
  43.9 3.5 %beams.2.refs_0_ = f32[64,16,256]{2,1,0:T(8,128)} custom-call(s32[1]{0:T(128)} %bitcast.2.centre_ref, bf16[24,32,512]{2,1,0:T(8,128)(2,1)S(1)} %get-tuple-element.31.spectra_ref, f32[64,2,512]{2,1,0:T(2,128)S(1)} %copy-done.1, s32[64,512]{1,0:T(8,128)S(1)} %copy-done, s32[2,256]{1,0:T(2,128)S(1)} %copy-done.2), custom_call_target="tpu_custom_call" | custom-call | tf_op jit(solution)/shard_map/beams/pallas_call | solution.py:782
  47.4 0.0 collective-permute-done.2.other_ref
  47.4 8.8 %second_update.2 = (bf16[64,2,256,512]{3,2,1,0:T(8,128)(2,1)}, f32[64,2,256]{2,1,0:T(2,128)}) custom-call(s32[1]{0:T(128)} %bitcast.1.core_ref, bf16[24,32,512]{2,1,0:T(8,128)(2,1)S(1)} %get-tuple-element.31.spectra_ref, bf16[24,2,256,512]{3,2,1,0:T(8,128)(2,1)S(1)} %get-tuple-element.32.model_ref, f32[24,2,256]{2,1,0:T(2,128)S(1)} %get-tuple-element.33.own_ref, ...), custom_call_target="tpu_custom_call" | custom-call | tf_op jit(solution)/shard_map/second_update/pallas_call | solution.py:875
  56.3 0.1 collective-permute-start.3
  56.3 2.2 %model.3.here_ref = bf16[40,2,256,512]{3,2,1,0:T(8,128)(2,1)S(1)} custom-call(bf16[8,320,128]{2,1,0:T(8,128)(2,1)S(1)} %all-to-all-done.own_hbm.own_ref, bf16[64,2,256,512]{3,2,1,0:T(8,128)(2,1)} %model_hbm.7), custom_call_target="tpu_custom_call" | custom-call | tf_op jit(solution)/shard_map/model/pallas_call | solution.py:837
  58.5 9.2 %first_update.3 = (bf16[40,32,512]{2,1,0:T(8,128)(2,1)S(1)}, f32[40,2,256]{2,1,0:T(2,128)S(1)}, bf16[40,2,256,512]{3,2,1,0:T(8,128)(2,1)S(1)}) custom-call(s32[1]{0:T(128)} %bitcast.1.core_ref, bf16[8,320,128]{2,1,0:T(8,128)(2,1)S(1)} %all-to-all-done.own_hbm.own_ref, ...), custom_call_target="tpu_custom_call", output_to_operand_aliasing={{2}: (6, {})} | custom-call | tf_op jit(solution)/shard_map/first_update/pallas_call | solution.py:848
  67.8 0.5 collective-permute-start.4
  68.3 5.4 %beams.3 = f32[64,16,256]{2,1,0:T(8,128)} custom-call(s32[1]{0:T(128)} %bitcast.3.centre_ref, bf16[40,32,512]{2,1,0:T(8,128)(2,1)S(1)} %get-tuple-element.38.spectra_ref, f32[64,2,512]{2,1,0:T(2,128)S(1)} %copy-done.1, s32[64,512]{1,0:T(8,128)S(1)} %copy-done, s32[2,256]{1,0:T(2,128)S(1)} %copy-done.2, ...), custom_call_target="tpu_custom_call", output_to_operand_aliasing={{}: (5, {})} | custom-call | tf_op jit(solution)/shard_map/beams/pallas_call | solution.py:782
  73.7 14.0 %second_update.3 = (bf16[64,2,256,512]{3,2,1,0:T(8,128)(2,1)}, f32[64,2,256]{2,1,0:T(2,128)}) custom-call(s32[1]{0:T(128)} %bitcast.1.core_ref, bf16[40,32,512]{2,1,0:T(8,128)(2,1)S(1)} %get-tuple-element.38.spectra_ref, bf16[40,2,256,512]{3,2,1,0:T(8,128)(2,1)S(1)} %get-tuple-element.39.model_ref, ...), custom_call_target="tpu_custom_call", output_to_operand_aliasing={{0}: (6, {}), {1}: (7, {})} | custom-call | tf_op jit(solution)/shard_map/second_update/pallas_call | solution.py:875
  (8 shorter events, 0.0 us)
Async XLA Ops:
  7.8 22.1 %all-to-all-start.1 = ((bf16[8,264,128]{2,1,0:T(8,128)(2,1)}), bf16[8,264,128]{2,1,0:T(8,128)(2,1)S(1)}, u32[]{:S(2)}, u32[]{:S(2)}) async-start(bf16[8,264,128]{2,1,0:T(8,128)(2,1)} %get-tuple-element.28), calls=%async_computation.1 | async-start | bytes 1081344 | tf_op jit(solution)/shard_map/all_to_all | solution.py:831
  17.7 9.3 %collective-permute-start = (bf16[3,320,128]{2,1,0:T(8,128)(2,1)S(1)}, bf16[3,320,128]{2,1,0:T(8,128)(2,1)S(1)}, u32[]{:S(2)}, u32[]{:S(2)}) collective-permute-start(bf16[3,320,128]{2,1,0:T(8,128)(2,1)S(1)} %spill.1), channel_id=1, source_target_pairs={{0,2},{1,3},{4,6},{5,7},{8,10},{9,11},{12,14},{13,15},{16,18},{17,... | collective-permute-start | bytes 737288 | tf_op jit(solution)/shard_map/ppermute | solution.py:23
  29.9 26.4 %all-to-all-start = ((bf16[8,320,128]{2,1,0:T(8,128)(2,1)}), bf16[8,320,128]{2,1,0:T(8,128)(2,1)S(1)}, u32[]{:S(2)}, u32[]{:S(2)}) async-start(bf16[8,320,128]{2,1,0:T(8,128)(2,1)} %added.1), calls=%async_computation | async-start | bytes 1310720 | tf_op jit(solution)/shard_map/all_to_all | solution.py:831
  35.4 2.4 %copy-start = (s32[64,512]{1,0:T(8,128)S(1)}, s32[64,512]{1,0:T(8,128)}, u32[]{:S(2)}) copy-start(s32[64,512]{1,0:T(8,128)} %flags_ref.5) | copy-start | bytes 393220
  35.4 2.4 %copy-start.1 = (f32[64,2,512]{2,1,0:T(2,128)S(1)}, f32[64,2,512]{2,1,0:T(2,128)}, u32[]{:S(2)}) copy-start(f32[64,2,512]{2,1,0:T(2,128)} %gains_ref.3) | copy-start | bytes 786436
  35.4 2.3 %collective-permute-start.1 = (bf16[8,264,128]{2,1,0:T(8,128)(2,1)S(1)}, bf16[8,264,128]{2,1,0:T(8,128)(2,1)S(1)}, u32[]{:S(2)}, u32[]{:S(2)}) collective-permute-start(bf16[8,264,128]{2,1,0:T(8,128)(2,1)S(1)} %all-to-all-done.1.own_hbm.own_ref), channel_id=1, source_target_pairs={{0,1},{1,0},{2,3},{3,2},{4,5},{5,4},{6,7},{7,6},{8,9},{9,8},{10,11... | collective-permute-start | bytes 1622024 | tf_op jit(solution)/shard_map/ppermute | solution.py:835
  37.7 6.2 %copy-start.2 = (s32[2,256]{1,0:T(2,128)S(1)}, s32[2,256]{1,0:T(2,128)}, u32[]{:S(2)}) copy-start(s32[2,256]{1,0:T(2,128)} %steering_ref.1) | copy-start | bytes 6148
  43.4 4.1 %collective-permute-start.2 = (f32[24,2,256]{2,1,0:T(2,128)S(1)}, f32[24,2,256]{2,1,0:T(2,128)S(1)}, u32[]{:S(2)}, u32[]{:S(2)}) collective-permute-start(f32[24,2,256]{2,1,0:T(2,128)S(1)} %get-tuple-element.33.own_ref), channel_id=1, source_target_pairs={{0,1},{1,0},{2,3},{3,2},{4,5},{5,4},{6,7},{7,6},{8,9},{9,8},{10,11... | collective-permute-start | bytes 147464 | tf_op jit(solution)/shard_map/ppermute | solution.py:866
  56.3 2.3 %collective-permute-start.3 = (bf16[8,320,128]{2,1,0:T(8,128)(2,1)S(1)}, bf16[8,320,128]{2,1,0:T(8,128)(2,1)S(1)}, u32[]{:S(2)}, u32[]{:S(2)}) collective-permute-start(bf16[8,320,128]{2,1,0:T(8,128)(2,1)S(1)} %all-to-all-done.own_hbm.own_ref), channel_id=1, source_target_pairs={{0,1},{1,0},{2,3},{3,2},{4,5},{5,4},{6,7},{7,6},{8,9},{9,8},{10,11... | collective-permute-start | bytes 1966088 | tf_op jit(solution)/shard_map/ppermute | solution.py:835
  67.8 6.0 %collective-permute-start.4 = (f32[40,2,256]{2,1,0:T(2,128)S(1)}, f32[40,2,256]{2,1,0:T(2,128)S(1)}, u32[]{:S(2)}, u32[]{:S(2)}) collective-permute-start(f32[40,2,256]{2,1,0:T(2,128)S(1)} %get-tuple-element.40.own_ref), channel_id=1, source_target_pairs={{0,1},{1,0},{2,3},{3,2},{4,5},{5,4},{6,7},{7,6},{8,9},{9,8},{10,11... | collective-permute-start | bytes 245768 | tf_op jit(solution)/shard_map/ppermute | solution.py:866

commit v4 on v3

--- a/solution.py
+++ b/solution.py
@@ -504,13 +504,16 @@
     return jnp.where(core == 0, values[:, :half], values[:, half:])
 
 
-def model_kernel(base, own_hbm, model_hbm, model_ref, sem):
+def model_kernel(
+    base, step, reach, own_hbm, model_hbm, centre_ref, steering_ref, model_ref, table_ref, sem
+):
     del own_hbm
     count = min(MODEL_BLOCK, model_ref.shape[0])
     copy = pltpu.make_async_copy(
         model_hbm.at[pl.ds(base, count)], model_ref.at[pl.ds(0, count)], sem
     )
     copy.start()
+    steering_tables(centre_ref[0], steering_ref, table_ref, step, reach)
     copy.wait()
 
 
@@ -537,7 +540,7 @@
 
     groups = share // VIS_BLOCK
     there = min(MODEL_BLOCK, share) // VIS_BLOCK
-    ahead = 4
+    ahead = 3
     for i in range(there, min(there + ahead, groups)):
         copy(i).start()
     if nexts:
@@ -639,46 +642,90 @@
 def second_kernel(
     base, core_ref, spectra_ref, model_ref, own_ref, other_ref, flags_ref, *refs
 ):
-    visibilities_ref, updated_ref = refs[-2:]
+    visibilities_hbm, updated_hbm, ready_ref, updated_ref, sems, sem = refs[-6:]
     core = core_ref[0]
-    count = visibilities_ref.shape[0]
-    start = pl.program_id(0) * count
-    for c in range(count):
-        here = start + c
-        spectra = spectra_ref[here]
-        half = spectra.shape[0] // 2
-        values = spectra.astype(jnp.float32)
-        real = values[:half]
-        imag = values[half:]
-        own_real = own_half(real, core)
-        own_imag = own_half(imag, core)
-        paired = (jnp.concatenate([own_real, own_imag], axis=0) / half).astype(jnp.bfloat16)
-        rotated = (jnp.concatenate([own_imag, -own_real], axis=0) / half).astype(jnp.bfloat16)
-        visibilities_ref[c, 0] = mxu(paired, spectra, TN).astype(jnp.bfloat16)
-        visibilities_ref[c, 1] = mxu(rotated, spectra, TN).astype(jnp.bfloat16)
-        own = own_ref[here]
-        other = other_ref[here]
-        first = jnp.where(core == 0, own, other)
-        second = jnp.where(core == 0, other, own)
-        gains = jnp.concatenate([first, second], axis=1)
-        turned_real, turned_imag, power = gain_terms(real, imag, gains, flags_ref[pl.ds(base + here, 1), :])
-        model_real = model_ref[here, 0]
-        model_imag = model_ref[here, 1]
-        updated_ref[c] = updated_gains(
-            (own_real, own_imag),
-            (turned_real, turned_imag),
-            model_real,
-            model_imag,
-            denominators(power, model_real, model_imag),
-            own,
+    share = spectra_ref.shape[0]
+    slots, count = ready_ref.shape[:2]
+    pieces = sems.shape[1]
+    size = count // pieces
+    steps = share // count
+
+    def copy(i, slot, piece):
+        return pltpu.make_async_copy(
+            ready_ref.at[slot, pl.ds(piece * size, size)],
+            visibilities_hbm.at[pl.ds(base + i * count + piece * size, size)],
+            sems.at[slot, piece],
         )
+
+    def step(i, carry):
+        slot = lax.rem(i, slots)
+
+        @pl.when(i >= slots)
+        def _():
+            for piece in range(pieces):
+                copy(i - slots, slot, piece).wait()
+
+        for c in range(count):
+            here = i * count + c
+            spectra = spectra_ref[here]
+            half = spectra.shape[0] // 2
+            values = spectra.astype(jnp.float32)
+            real = values[:half]
+            imag = values[half:]
+            own_real = own_half(real, core)
+            own_imag = own_half(imag, core)
+            paired = (jnp.concatenate([own_real, own_imag], axis=0) / half).astype(jnp.bfloat16)
+            rotated = (jnp.concatenate([own_imag, -own_real], axis=0) / half).astype(jnp.bfloat16)
+            ready_ref[slot, c, 0] = mxu(paired, spectra, TN).astype(jnp.bfloat16)
+            ready_ref[slot, c, 1] = mxu(rotated, spectra, TN).astype(jnp.bfloat16)
+            if c % size == size - 1:
+                copy(i, slot, c // size).start()
+            own = own_ref[here]
+            other = other_ref[here]
+            first = jnp.where(core == 0, own, other)
+            second = jnp.where(core == 0, other, own)
+            gains = jnp.concatenate([first, second], axis=1)
+            flags = flags_ref[pl.ds(base + here, 1), :]
+            turned_real, turned_imag, power = gain_terms(real, imag, gains, flags)
+            model_real = model_ref[here, 0]
+            model_imag = model_ref[here, 1]
+            updated_ref[here] = updated_gains(
+                (own_real, own_imag),
+                (turned_real, turned_imag),
+                model_real,
+                model_imag,
+                denominators(power, model_real, model_imag),
+                own,
+            )
+        return carry
+
+    lax.fori_loop(0, steps, step, 0)
+    last = pltpu.make_async_copy(updated_ref, updated_hbm.at[pl.ds(base, share)], sem)
+    last.start()
+    for i in range(max(0, steps - slots), steps):
+        for piece in range(pieces):
+            copy(i, i % slots, piece).wait()
+    last.wait()
 
 
 def series_length(reach):
     terms = 1
-    while reach**terms / math.factorial(terms) >= 2.0**-22:
+    while 2.0 * (0.5 * reach) ** terms / math.factorial(terms) >= 2.0**-22:
         terms += 1
     return terms
+
+
+def bessel(order, x, reach):
+    count = 1
+    while (0.5 * reach) ** (2 * count) / math.factorial(count) ** 2 >= 2.0**-26:
+        count += 1
+    square = x * x * -0.25
+    total = jnp.full_like(x, 1.0 / (math.factorial(count - 1) * math.factorial(count - 1 + order)))
+    for m in reversed(range(count - 1)):
+        total = total * square + 1.0 / (math.factorial(m) * math.factorial(m + order))
+    for _ in range(order):
+        total = total * (0.5 * x)
+    return total
 
 
 def turns(count, period):
@@ -712,7 +759,6 @@
             phase_index = (steering_ref[0:1, :] * (column * 64) + steering_ref[1:2, :] * within) & 255
             cosine, sine_part = turns(phase_index * centre, round(4.0 * math.pi / step))
             offset = (phase_index - 128).astype(jnp.float32) * (reach * step)
-            factor = None
             at = column * quarter + first
             rows = slice(at, at + shape[0])
             lower = slice(inputs + at, inputs + at + shape[0])
@@ -723,10 +769,9 @@
                     (-cosine, -sine_part),
                     (sine_part, -cosine),
                 )[term % 4]
-                if term:
-                    factor = offset if factor is None else factor * offset / term
-                    real = factor * real
-                    imag = factor * imag
+                factor = bessel(term, offset, 128 * reach * step) * (2.0 if term else 1.0)
+                real = factor * real
+                imag = factor * imag
                 real = real.astype(jnp.bfloat16)
                 imag = imag.astype(jnp.bfloat16)
                 table_ref[term, rows, :beams] = real
@@ -735,9 +780,8 @@
                 table_ref[term, lower, beams:] = real
 
 
-def beams_kernel(step, reach, base, centre_ref, spectra_ref, gains_ref, flags_ref, steering_ref, *refs):
-    power_hbm, power_ref, left_ref, table_ref, sem = refs[-5:]
-    steering_tables(centre_ref[0], steering_ref, table_ref, step, reach)
+def beams_kernel(base, spectra_ref, gains_ref, flags_ref, table_ref, *refs):
+    power_hbm, power_ref, left_ref, sem = refs[-4:]
     count, doubled, inputs = spectra_ref.shape
     frames = doubled // 2
     scale = 1.0 / math.sqrt(inputs)
@@ -755,7 +799,7 @@
         lit_imag = real * gain_imag + imag * gain_real
         rows = slice(c * frames, (c + 1) * frames)
         for term in range(terms):
-            power = ((c - middle) / max(middle, 0.5)) ** term
+            power = math.cos(term * math.acos((c - middle) / max(middle, 0.5)))
             left_ref[term, rows, :inputs] = (lit_real * power).astype(jnp.bfloat16)
             left_ref[term, rows, inputs:] = (lit_imag * power).astype(jnp.bfloat16)
     total = mxu(left_ref[0], table_ref[0], NN)
@@ -770,31 +814,27 @@
     copy.wait()
 
 
-def formed_beams(chunk, gains, flags, steering, step, earlier):
-    base, centre, spectra = chunk
+def formed_beams(chunk, gains, flags, earlier):
+    base, table, spectra = chunk
     share, doubled, input_count = spectra.shape
     frame_count = doubled // 2
-    beams = steering.shape[1]
+    beams = table.shape[2] // 2
     earlier = [] if earlier is None else [earlier]
-    reach = max(0.5 * (share - 1), 0.5)
-    terms = series_length(128 * reach * step)
     vmem = pl.BlockSpec(memory_space=pltpu.VMEM)
     return pl.pallas_call(
-        functools.partial(beams_kernel, step, reach, base),
-        in_specs=[pl.BlockSpec(memory_space=pltpu.SMEM)] + [vmem] * 4
-        + [pl.BlockSpec(memory_space=pl.ANY)] * len(earlier),
+        functools.partial(beams_kernel, base),
+        in_specs=[vmem] * 4 + [pl.BlockSpec(memory_space=pl.ANY)] * len(earlier),
         out_specs=pl.BlockSpec(memory_space=pl.ANY),
         out_shape=jax.ShapeDtypeStruct((gains.shape[0], frame_count, beams), jnp.float32),
-        input_output_aliases={5: 0} if earlier else {},
+        input_output_aliases={4: 0} if earlier else {},
         scratch_shapes=[
             pltpu.VMEM((share, frame_count, beams), jnp.float32),
-            pltpu.VMEM((terms, share * frame_count, 2 * input_count), jnp.bfloat16),
-            pltpu.VMEM((terms, 2 * input_count, 2 * beams), jnp.bfloat16),
+            pltpu.VMEM((table.shape[0], share * frame_count, 2 * input_count), jnp.bfloat16),
             pltpu.SemaphoreType.DMA,
         ],
         compiler_params=pltpu.CompilerParams(vmem_limit_bytes=UPDATE_LIMIT),
         name="beams",
-    )(centre, spectra, gains, flags, steering, *earlier)
+    )(spectra, gains, flags, table, *earlier)
 
 
 def chunk_shards(samples, window_taps, sky_model, prior_gains, beam_steering, input_flags):
@@ -830,19 +870,24 @@
     for chunk, (base, share) in enumerate(zip(bases, shares)):
         own = lax.all_to_all(sent[chunk], ("chan", "tm"), 0, 0, tiled=True)
         if before is not None:
-            beam_power = formed_beams(before, gains, flags, steering, step, beam_power)
+            beam_power = formed_beams(before, gains, flags, beam_power)
             own, gains_new, beam_power = lax.optimization_barrier((own, gains_new, beam_power))
         other = lax.ppermute(own, "beam", swap)
         model_shape = (share, *sky_model.shape[1:])
-        model = pl.pallas_call(
-            functools.partial(model_kernel, base),
-            in_specs=[anywhere, anywhere],
-            out_specs=vmem,
-            out_shape=pltpu.VMEM(model_shape, sky_model.dtype),
+        reach = max(0.5 * (share - 1), 0.5)
+        table_shape = (series_length(128 * reach * step), 2 * input_count, 2 * beams)
+        model, table = pl.pallas_call(
+            functools.partial(model_kernel, base, step, reach),
+            in_specs=[anywhere, anywhere, smem, vmem],
+            out_specs=[vmem, vmem],
+            out_shape=[
+                pltpu.VMEM(model_shape, sky_model.dtype),
+                jax.ShapeDtypeStruct(table_shape, jnp.bfloat16),
+            ],
             scratch_shapes=[pltpu.SemaphoreType.DMA],
             compiler_params=pltpu.CompilerParams(vmem_limit_bytes=UPDATE_LIMIT),
             name="model",
-        )(own, sky_model)
+        )(own, sky_model, centres[chunk], steering)
         model = pltpu.with_memory_space_constraint(model, pltpu.VMEM)
         half_shape = jax.ShapeDtypeStruct((share, 2, half_rows), jnp.float32)
         spectra, gains_own, model = pl.pallas_call(
@@ -864,25 +909,23 @@
         )(core, own, other, sky_model, gains, flags, model)
         model = pltpu.with_memory_space_constraint(model, pltpu.VMEM)
         gains_other = lax.ppermute(gains_own, "beam", swap)
-        before = (base, centres[chunk], spectra)
+        before = (base, table, spectra)
         if chunk == len(shares) - 1:
-            beam_power = formed_beams(before, gains, flags, steering, step, beam_power)
+            beam_power = formed_beams(before, gains, flags, beam_power)
         earlier = [] if visibilities is None else [visibilities, gains_new]
-        block = VIS_BLOCK
-        block_spec = pl.BlockSpec(
-            (block, 2, half_rows, input_count), lambda i, at=base // block: (at + i, 0, 0, 0)
-        )
         visibilities, gains_new = pl.pallas_call(
             functools.partial(second_kernel, base),
-            grid=(share // block,),
-            in_specs=[smem, vmem, vmem, vmem, vmem, vmem] + [anywhere] * len(earlier),
-            out_specs=[
-                block_spec,
-                pl.BlockSpec((block, 2, half_rows), lambda i, at=base // block: (at + i, 0, 0)),
+            in_specs=[smem] + [vmem] * 5 + [anywhere] * len(earlier),
+            out_specs=[anywhere, anywhere],
+            out_shape=[
+                jax.ShapeDtypeStruct(sky_model.shape, jnp.bfloat16),
+                jax.ShapeDtypeStruct((chan_local, 2, half_rows), jnp.float32),
             ],
-            out_shape=[
-                jax.ShapeDtypeStruct((chan_local, 2, half_rows, input_count), jnp.bfloat16),
-                jax.ShapeDtypeStruct((chan_local, 2, half_rows), jnp.float32),
+            scratch_shapes=[
+                pltpu.VMEM((2, BLOCK, 2, half_rows, input_count), jnp.bfloat16),
+                pltpu.VMEM((share, 2, half_rows), jnp.float32),
+                pltpu.SemaphoreType.DMA((2, 4)),
+                pltpu.SemaphoreType.DMA,
             ],
             input_output_aliases={6: 0, 7: 1} if earlier else {},
             compiler_params=pltpu.CompilerParams(vmem_limit_bytes=UPDATE_LIMIT),

time: 88.1 us -> 83.7 us (0.950)
  Pallas kernels: 65.9 us -> 61.3 us
    pallas_call x6, Pallas kernels: 36.2 us -> 31.6 us  [the longest x2 20.8 us: chunk_shards(): pl.pallas_call(functools.partial(second_kernel, base), in_specs=[smem] +...]
  transfers between devices with their start and end apart: 7 -> 7, of which waited for: 2 -> 2; matrix products, arithmetic and copies ran while one was open for 0% -> 0% of each run, Pallas kernels for 41% -> 39%
where the time goes in v4:
time: 83.7 us; the launch traced here: 83.3 us
  Pallas kernels  61.3 us (73%)
  starting transfers between devices  17.9 us (21%)
  waiting for transfers between devices  3.12 us (4%)
  between operations  1.01 us (1%)
    pallas_call x2, Pallas kernels, chunk_shards(): pl.pallas_call(functools.partial(second_kernel, base), in_specs=[smem] +...  20.8 us
    pallas_call x2, Pallas kernels, chunk_shards(): pl.pallas_call(functools.partial(first_kernel, times, base), in_specs=[sm...  14.8 us
    all_to_all x2, starting transfers between devices, chunk_shards(): own = lax.all_to_all(sent[chunk], ('chan', 'tm'), 0, 0, tiled=True)  12.7 us
    pallas_call x1, Pallas kernels, filtered(): pl.pallas_call(functools.partial(filter_kernel, owners), out_shape=[pltpu...  7.11 us
    pallas_call x2, Pallas kernels, formed_beams(): pl.pallas_call(functools.partial(beams_kernel, base), in_specs=[vmem] * 4...  6.37 us
    pallas_call x2, Pallas kernels, chunk_shards(): pl.pallas_call(functools.partial(model_kernel, base, step, reach), in_spe...  4.43 us
    ppermute x1, starting transfers between devices, from_behind(): return lax.ppermute(block, axis, route)  3.94 us
    pallas_call x1, Pallas kernels, more(): pl.pallas_call(functools.partial(filter_more_kernel, owners, start), out_...  3.83 us
  transfers between devices with their start and end apart: 7, of which 2 were waited for; matrix products, arithmetic and copies ran while one was open for 0% of the time, Pallas kernels for 39%

profile of v4, /device:TPU:0, one launch (start us, length us, event | category | flops | bytes accessed | tf_op | source)
XLA Modules:
  0.0 83.3 jit_solution(86498440063306721)
XLA Ops:
  0.7 7.1 %filter.1 = (bf16[1408,2048]{1,0:T(8,128)(2,1)}, bf16[8,264,128]{2,1,0:T(8,128)(2,1)}) custom-call(bf16[64,2,8,1024]{3,2,1,0:T(8,128)(2,1)} %bitcast.6, f32[4,1024]{1,0:T(4,128)} %taps_hbm.1, bf16[512,2048]{1,0:T(8,128)(2,1)} %constant.30.clone.table_hbm), custom_call_target="tpu_custom_call" | custom-call | tf_op jit(solution)/shard_map/filter/pallas_call | solution.py:399
  7.8 7.3 %all-to-all-start.1 = ((bf16[8,264,128]{2,1,0:T(8,128)(2,1)}), bf16[8,264,128]{2,1,0:T(8,128)(2,1)S(1)}, u32[]{:S(2)}, u32[]{:S(2)}) async-start(bf16[8,264,128]{2,1,0:T(8,128)(2,1)} %get-tuple-element.32), calls=%async_computation.1 | async-start | bytes 1081344 | tf_op jit(solution)/shard_map/all_to_all | solution.py:871
  15.0 2.7 %spill.1 = bf16[3,320,128]{2,1,0:T(8,128)(2,1)S(1)} custom-call(bf16[1408,2048]{1,0:T(8,128)(2,1)} %get-tuple-element.31.windowed_hbm, bf16[512,2048]{1,0:T(8,128)(2,1)} %constant.30.clone.table_hbm), custom_call_target="tpu_custom_call" | custom-call | tf_op jit(solution)/shard_map/spill/pallas_call | solution.py:423
  17.7 3.9 %collective-permute-start = (bf16[3,320,128]{2,1,0:T(8,128)(2,1)S(1)}, bf16[3,320,128]{2,1,0:T(8,128)(2,1)S(1)}, u32[]{:S(2)}, u32[]{:S(2)}) collective-permute-start(bf16[3,320,128]{2,1,0:T(8,128)(2,1)S(1)} %spill.1), channel_id=1, source_target_pairs={{0,2},{1,3},{4,6},{5,7},{8,10},{9,11},{12,14},{13,15},{16,18},{17,... | collective-permute-start | bytes 737288 | tf_op jit(solution)/shard_map/ppermute | solution.py:23
  21.7 3.8 %filter_more.1.turned_ref = f32[2560,128]{1,0:T(8,128)S(1)} custom-call(bf16[1408,2048]{1,0:T(8,128)(2,1)} %get-tuple-element.31.windowed_hbm, bf16[512,2048]{1,0:T(8,128)(2,1)} %constant.30.clone.table_hbm), custom_call_target="tpu_custom_call" | custom-call | tf_op jit(solution)/shard_map/filter_more/pallas_call | solution.py:437
  25.5 1.5 %collective-permute-done.added_ref = bf16[3,320,128]{2,1,0:T(8,128)(2,1)S(1)} collective-permute-done((bf16[3,320,128]{2,1,0:T(8,128)(2,1)S(1)}, bf16[3,320,128]{2,1,0:T(8,128)(2,1)S(1)}, u32[]{:S(2)}, u32[]{:S(2)}) %collective-permute-start) | collective-permute-done | bytes 245792 | tf_op jit(solution)/shard_map/ppermute | solution.py:23
  27.0 1.3 %added.1 = bf16[8,320,128]{2,1,0:T(8,128)(2,1)} custom-call(f32[2560,128]{1,0:T(8,128)S(1)} %filter_more.1.turned_ref, bf16[3,320,128]{2,1,0:T(8,128)(2,1)S(1)} %collective-permute-done.added_ref), custom_call_target="tpu_custom_call" | custom-call | tf_op jit(solution)/shard_map/added/pallas_call | solution.py:450
  28.3 1.6 %all-to-all-done.1.own_hbm.own_ref = bf16[8,264,128]{2,1,0:T(8,128)(2,1)S(1)} async-done(((bf16[8,264,128]{2,1,0:T(8,128)(2,1)}), bf16[8,264,128]{2,1,0:T(8,128)(2,1)S(1)}, u32[]{:S(2)}, u32[]{:S(2)}) %all-to-all-start.1) | async-done | bytes 540704 | tf_op jit(solution)/shard_map/all_to_all | solution.py:871
  29.9 5.5 %all-to-all-start = ((bf16[8,320,128]{2,1,0:T(8,128)(2,1)}), bf16[8,320,128]{2,1,0:T(8,128)(2,1)S(1)}, u32[]{:S(2)}, u32[]{:S(2)}) async-start(bf16[8,320,128]{2,1,0:T(8,128)(2,1)} %added.1), calls=%async_computation | async-start | bytes 1310720 | tf_op jit(solution)/shard_map/all_to_all | solution.py:871
  35.4 0.0 copy-start.1
  35.4 0.1 collective-permute-start.1
  35.5 2.2 %model.2 = (bf16[24,2,256,512]{3,2,1,0:T(8,128)(2,1)S(1)}, bf16[4,1024,512]{2,1,0:T(8,128)(2,1)S(1)}) custom-call(bf16[8,264,128]{2,1,0:T(8,128)(2,1)S(1)} %all-to-all-done.1.own_hbm.own_ref, bf16[64,2,256,512]{3,2,1,0:T(8,128)(2,1)} %model_hbm.7, s32[1]{0:T(128)} %bitcast.2.centre_ref, s32[2,256]{1,0:T(2,128)S(1)} %copy-done.2), custom_call_target="tpu_custom_call" | custom-call | tf_op jit(solution)/shard_map/model/pallas_call | solution.py:879
  37.7 5.6 %first_update.2 = (bf16[24,32,512]{2,1,0:T(8,128)(2,1)S(1)}, f32[24,2,256]{2,1,0:T(2,128)S(1)}, bf16[24,2,256,512]{3,2,1,0:T(8,128)(2,1)S(1)}) custom-call(s32[1]{0:T(128)} %bitcast.1.core_ref, bf16[8,264,128]{2,1,0:T(8,128)(2,1)S(1)} %all-to-all-done.1.own_hbm.own_ref, ...), custom_call_target="tpu_custom_call", output_to_operand_aliasing={{2}: (6, {})} | custom-call | tf_op jit(solution)/shard_map/first_update/pallas_call | solution.py:893
  43.4 0.5 collective-permute-start.2
  43.9 2.6 %beams.2.refs_0_ = f32[64,16,256]{2,1,0:T(8,128)} custom-call(bf16[24,32,512]{2,1,0:T(8,128)(2,1)S(1)} %get-tuple-element.38.spectra_ref, f32[64,2,512]{2,1,0:T(2,128)S(1)} %copy-done.1, s32[64,512]{1,0:T(8,128)S(1)} %copy-done, bf16[4,1024,512]{2,1,0:T(8,128)(2,1)S(1)} %get-tuple-element.42.table_ref), custom_call_target="tpu_custom_call" | custom-call | tf_op jit(solution)/shard_map/beams/pallas_call | solution.py:824
  46.5 8.0 %second_update.2 = (bf16[64,2,256,512]{3,2,1,0:T(8,128)(2,1)}, f32[64,2,256]{2,1,0:T(2,128)}) custom-call(s32[1]{0:T(128)} %bitcast.1.core_ref, bf16[24,32,512]{2,1,0:T(8,128)(2,1)S(1)} %get-tuple-element.38.spectra_ref, bf16[24,2,256,512]{3,2,1,0:T(8,128)(2,1)S(1)} %get-tuple-element.39.model_ref, f32[24,2,256]{2,1,0:T(2,128)S(1)} %get-tuple-element.40.own_ref, ...), custom_call_target="tpu_custom_call" | custom-call | tf_op jit(solution)/shard_map/second_update/pallas_call | solution.py:916
  54.5 0.0 all-to-all-done.own_hbm.own_ref
  54.5 0.1 collective-permute-start.3
  54.6 2.2 %model.3 = (bf16[40,2,256,512]{3,2,1,0:T(8,128)(2,1)S(1)}, bf16[4,1024,512]{2,1,0:T(8,128)(2,1)S(1)}) custom-call(bf16[8,320,128]{2,1,0:T(8,128)(2,1)S(1)} %all-to-all-done.own_hbm.own_ref, bf16[64,2,256,512]{3,2,1,0:T(8,128)(2,1)} %model_hbm.7, s32[1]{0:T(128)} %bitcast.3.centre_ref, s32[2,256]{1,0:T(2,128)S(1)} %copy-done.2), custom_call_target="tpu_custom_call" | custom-call | tf_op jit(solution)/shard_map/model/pallas_call | solution.py:879
  56.9 9.2 %first_update.3 = (bf16[40,32,512]{2,1,0:T(8,128)(2,1)S(1)}, f32[40,2,256]{2,1,0:T(2,128)S(1)}, bf16[40,2,256,512]{3,2,1,0:T(8,128)(2,1)S(1)}) custom-call(s32[1]{0:T(128)} %bitcast.1.core_ref, bf16[8,320,128]{2,1,0:T(8,128)(2,1)S(1)} %all-to-all-done.own_hbm.own_ref, ...), custom_call_target="tpu_custom_call", output_to_operand_aliasing={{2}: (6, {})} | custom-call | tf_op jit(solution)/shard_map/first_update/pallas_call | solution.py:893
  66.1 0.5 collective-permute-start.4
  66.6 3.8 %beams.3 = f32[64,16,256]{2,1,0:T(8,128)} custom-call(bf16[40,32,512]{2,1,0:T(8,128)(2,1)S(1)} %get-tuple-element.46.spectra_ref, f32[64,2,512]{2,1,0:T(2,128)S(1)} %copy-done.1, s32[64,512]{1,0:T(8,128)S(1)} %copy-done, bf16[4,1024,512]{2,1,0:T(8,128)(2,1)S(1)} %get-tuple-element.53.table_ref, ...), custom_call_target="tpu_custom_call", output_to_operand_aliasing={{}: (4, {})} | custom-call | tf_op jit(solution)/shard_map/beams/pallas_call | solution.py:824
  70.4 0.0 collective-permute-done.4.other_ref
  70.4 12.8 %second_update.3 = (bf16[64,2,256,512]{3,2,1,0:T(8,128)(2,1)}, f32[64,2,256]{2,1,0:T(2,128)}) custom-call(s32[1]{0:T(128)} %bitcast.1.core_ref, bf16[40,32,512]{2,1,0:T(8,128)(2,1)S(1)} %get-tuple-element.46.spectra_ref, bf16[40,2,256,512]{3,2,1,0:T(8,128)(2,1)S(1)} %get-tuple-element.47.model_ref, ...), custom_call_target="tpu_custom_call", output_to_operand_aliasing={{0}: (6, {}), {1}: (7, {})} | custom-call | tf_op jit(solution)/shard_map/second_update/pallas_call | solution.py:916
  (8 shorter events, 0.0 us)
Async XLA Ops:
  0.6 34.8 %copy-start.2 = (s32[2,256]{1,0:T(2,128)S(1)}, s32[2,256]{1,0:T(2,128)}, u32[]{:S(2)}) copy-start(s32[2,256]{1,0:T(2,128)} %steering_ref.1) | copy-start | bytes 6148
  7.8 22.1 %all-to-all-start.1 = ((bf16[8,264,128]{2,1,0:T(8,128)(2,1)}), bf16[8,264,128]{2,1,0:T(8,128)(2,1)S(1)}, u32[]{:S(2)}, u32[]{:S(2)}) async-start(bf16[8,264,128]{2,1,0:T(8,128)(2,1)} %get-tuple-element.32), calls=%async_computation.1 | async-start | bytes 1081344 | tf_op jit(solution)/shard_map/all_to_all | solution.py:871
  17.7 9.3 %collective-permute-start = (bf16[3,320,128]{2,1,0:T(8,128)(2,1)S(1)}, bf16[3,320,128]{2,1,0:T(8,128)(2,1)S(1)}, u32[]{:S(2)}, u32[]{:S(2)}) collective-permute-start(bf16[3,320,128]{2,1,0:T(8,128)(2,1)S(1)} %spill.1), channel_id=1, source_target_pairs={{0,2},{1,3},{4,6},{5,7},{8,10},{9,11},{12,14},{13,15},{16,18},{17,... | collective-permute-start | bytes 737288 | tf_op jit(solution)/shard_map/ppermute | solution.py:23
  29.9 24.6 %all-to-all-start = ((bf16[8,320,128]{2,1,0:T(8,128)(2,1)}), bf16[8,320,128]{2,1,0:T(8,128)(2,1)S(1)}, u32[]{:S(2)}, u32[]{:S(2)}) async-start(bf16[8,320,128]{2,1,0:T(8,128)(2,1)} %added.1), calls=%async_computation | async-start | bytes 1310720 | tf_op jit(solution)/shard_map/all_to_all | solution.py:871
  35.4 2.4 %copy-start = (s32[64,512]{1,0:T(8,128)S(1)}, s32[64,512]{1,0:T(8,128)}, u32[]{:S(2)}) copy-start(s32[64,512]{1,0:T(8,128)} %flags_ref.5) | copy-start | bytes 393220
  35.4 2.4 %copy-start.1 = (f32[64,2,512]{2,1,0:T(2,128)S(1)}, f32[64,2,512]{2,1,0:T(2,128)}, u32[]{:S(2)}) copy-start(f32[64,2,512]{2,1,0:T(2,128)} %gains_ref.3) | copy-start | bytes 786436
  35.4 2.3 %collective-permute-start.1 = (bf16[8,264,128]{2,1,0:T(8,128)(2,1)S(1)}, bf16[8,264,128]{2,1,0:T(8,128)(2,1)S(1)}, u32[]{:S(2)}, u32[]{:S(2)}) collective-permute-start(bf16[8,264,128]{2,1,0:T(8,128)(2,1)S(1)} %all-to-all-done.1.own_hbm.own_ref), channel_id=1, source_target_pairs={{0,1},{1,0},{2,3},{3,2},{4,5},{5,4},{6,7},{7,6},{8,9},{9,8},{10,11... | collective-permute-start | bytes 1622024 | tf_op jit(solution)/shard_map/ppermute | solution.py:875
  43.4 3.1 %collective-permute-start.2 = (f32[24,2,256]{2,1,0:T(2,128)S(1)}, f32[24,2,256]{2,1,0:T(2,128)S(1)}, u32[]{:S(2)}, u32[]{:S(2)}) collective-permute-start(f32[24,2,256]{2,1,0:T(2,128)S(1)} %get-tuple-element.40.own_ref), channel_id=1, source_target_pairs={{0,1},{1,0},{2,3},{3,2},{4,5},{5,4},{6,7},{7,6},{8,9},{9,8},{10,11... | collective-permute-start | bytes 147464 | tf_op jit(solution)/shard_map/ppermute | solution.py:911
  54.5 2.3 %collective-permute-start.3 = (bf16[8,320,128]{2,1,0:T(8,128)(2,1)S(1)}, bf16[8,320,128]{2,1,0:T(8,128)(2,1)S(1)}, u32[]{:S(2)}, u32[]{:S(2)}) collective-permute-start(bf16[8,320,128]{2,1,0:T(8,128)(2,1)S(1)} %all-to-all-done.own_hbm.own_ref), channel_id=1, source_target_pairs={{0,1},{1,0},{2,3},{3,2},{4,5},{5,4},{6,7},{7,6},{8,9},{9,8},{10,11... | collective-permute-start | bytes 1966088 | tf_op jit(solution)/shard_map/ppermute | solution.py:875
  66.1 4.3 %collective-permute-start.4 = (f32[40,2,256]{2,1,0:T(2,128)S(1)}, f32[40,2,256]{2,1,0:T(2,128)S(1)}, u32[]{:S(2)}, u32[]{:S(2)}) collective-permute-start(f32[40,2,256]{2,1,0:T(2,128)S(1)} %get-tuple-element.48.own_ref), channel_id=1, source_target_pairs={{0,1},{1,0},{2,3},{3,2},{4,5},{5,4},{6,7},{7,6},{8,9},{9,8},{10,11... | collective-permute-start | bytes 245768 | tf_op jit(solution)/shard_map/ppermute | solution.py:911

commit v5 on v4

--- a/solution.py
+++ b/solution.py
@@ -246,11 +246,12 @@
     windowed_ref,
     turned_ref,
     sems,
+    keep_sems,
 ):
     inputs, _, frames, points = x_ref.shape
     taps = taps_ref.shape[0]
     width = 2 * inputs
-    pieces = sems.shape[0] - 3
+    pieces = sems.shape[0] - 2
     group = inputs // pieces
     table_copy = pltpu.make_async_copy(
         table_hbm.at[pl.ds(0, table_ref.shape[0])], table_ref, sems.at[pieces]
@@ -261,7 +262,7 @@
         )
         for i in range(pieces)
     ]
-    taps_copy = pltpu.make_async_copy(taps_hbm, taps_ref, sems.at[pieces + 2])
+    taps_copy = pltpu.make_async_copy(taps_hbm, taps_ref, sems.at[pieces + 1])
     taps_copy.start()
     for copy in copies:
         copy.start()
@@ -277,9 +278,15 @@
 
     for i, copy in enumerate(copies):
         copy.wait()
-        lax.fori_loop(i * group, (i + 1) * group, spread, 0, unroll=4)
+        lax.fori_loop(i * group, (i + 1) * group, spread, 0, unroll=8)
 
     table_copy.start()
+
+    def keep(piece, half):
+        here = pl.ds(pl.multiple_of(half * points + piece * LANES, LANES), LANES)
+        return pltpu.make_async_copy(
+            windowed_ref.at[:, here], windowed_hbm.at[:, here], keep_sems.at[half, piece]
+        )
 
     def window(piece, carry):
         lanes = pl.ds(pl.multiple_of(piece * LANES, LANES), LANES)
@@ -313,11 +320,11 @@
                     else:
                         windowed_ref[rows, upper] = total
                         windowed_ref[swapped, lanes] = total
+        keep(piece, 0).start()
+        keep(piece, 1).start()
         return carry
 
-    lax.fori_loop(0, points // LANES, window, 0)
-    keep = pltpu.make_async_copy(windowed_ref, windowed_hbm, sems.at[pieces + 1])
-    keep.start()
+    lax.fori_loop(0, points // LANES, window, 0, unroll=2)
     table_copy.wait()
     transformed(owners, frames, table_ref[...], windowed_ref, turned_ref)
     share = table_ref.shape[0] // owners
@@ -331,7 +338,9 @@
         out_ref[owner, main : main + extra, :] = turned_ref[first : first + extra, :].astype(
             jnp.bfloat16
         )
-    keep.wait()
+    for piece in range(points // LANES):
+        keep(piece, 0).wait()
+        keep(piece, 1).wait()
 
 
 def rows_copies(source, target, sems, first=0):
@@ -411,7 +420,8 @@
             pltpu.VMEM((2, pieces, inputs * frames, LANES), jnp.float32),
             pltpu.VMEM(windowed_shape, jnp.bfloat16),
             pltpu.VMEM((rows * (frames + taps - 1), width), jnp.float32),
-            pltpu.SemaphoreType.DMA((7,)),
+            pltpu.SemaphoreType.DMA((6,)),
+            pltpu.SemaphoreType.DMA((2, pieces)),
         ],
         compiler_params=pltpu.CompilerParams(vmem_limit_bytes=32 * MIB),
         name="filter",
@@ -484,17 +494,29 @@
     return mxu(jnp.ones((SUBLANES, LANES), jnp.bfloat16), folded, NT)[0:1] + epsilon
 
 
-def updated_gains(own, turned, model_real, model_imag, denom, older):
-    real, imag = turned
-    straight = jnp.concatenate([real, imag], axis=0).astype(jnp.bfloat16)
-    crossed = jnp.concatenate([-imag, real], axis=0).astype(jnp.bfloat16)
-    modelled = mxu(straight, model_real, NT) + mxu(crossed, model_imag, NT)
+def put_turned(turned_ref, at, real, imag, gains, flags):
+    turned_real, turned_imag, power = gain_terms(real, imag, gains, flags)
     frames = real.shape[0]
-    modelled_real = modelled[:frames]
-    modelled_imag = modelled[frames:]
+    turned_real = turned_real.astype(jnp.bfloat16)
+    turned_imag = turned_imag.astype(jnp.bfloat16)
+    turned_ref[at, 0, :frames] = turned_real
+    turned_ref[at, 0, frames:] = turned_imag
+    turned_ref[at, 1, :frames] = -turned_imag
+    turned_ref[at, 1, frames:] = turned_real
+    return power
+
+
+def modelled(turned_ref, at, model_real, model_imag):
+    return mxu(turned_ref[at, 0], model_real, NT) + mxu(turned_ref[at, 1], model_imag, NT)
+
+
+def updated_gains(own, products, denom, older):
     own_real, own_imag = own
-    numer_real = jnp.sum(own_real * modelled_real + own_imag * modelled_imag, axis=0, keepdims=True)
-    numer_imag = jnp.sum(own_imag * modelled_real - own_real * modelled_imag, axis=0, keepdims=True)
+    frames = own_real.shape[0]
+    real = products[:frames]
+    imag = products[frames:]
+    numer_real = jnp.sum(own_real * real + own_imag * imag, axis=0, keepdims=True)
+    numer_imag = jnp.sum(own_imag * real - own_real * imag, axis=0, keepdims=True)
     numer = jnp.concatenate([numer_real, numer_imag], axis=0) / frames
     return damping * older + (1.0 - damping) * (numer / denom)
 
@@ -521,7 +543,7 @@
     times, base, core_ref, own_ref, other_ref, model_hbm, gains_ref, flags_ref, here_ref, *refs
 ):
     del here_ref
-    spectra_ref, updated_ref, model_ref, next_ref, sems = refs
+    spectra_ref, updated_ref, model_ref, next_ref, turned_ref, products_ref, power_ref, denom_ref, sems = refs
     core = core_ref[0]
     share = spectra_ref.shape[0]
     sources, rows, width = own_ref.shape
@@ -608,24 +630,29 @@
                 def _():
                     copy(group + ahead).start()
 
-        for c in range(count):
-            here = i * count + c
+        channels = [i * count + c for c in range(count)]
+
+        def parts(here):
             values = spectra_ref[here].astype(jnp.float32)
             half = values.shape[0] // 2
-            real = values[:half]
-            imag = values[half:]
-            gains = gains_ref[base + here]
+            return values[:half], values[half:]
+
+        for c, here in enumerate(channels):
+            real, imag = parts(here)
             flags = flags_ref[pl.ds(base + here, 1), :]
+            power_ref[c] = put_turned(turned_ref, c, real, imag, gains_ref[base + here], flags)
+        for c, here in enumerate(channels):
             model_real = model_ref[here, 0]
             model_imag = model_ref[here, 1]
-            turned_real, turned_imag, power = gain_terms(real, imag, gains, flags)
+            products_ref[c] = modelled(turned_ref, c, model_real, model_imag)
+            denom_ref[c] = denominators(power_ref[c], model_real, model_imag)
+        for c, here in enumerate(channels):
+            real, imag = parts(here)
             updated_ref[here] = updated_gains(
                 (own_half(real, core), own_half(imag, core)),
-                (turned_real, turned_imag),
-                model_real,
-                model_imag,
-                denominators(power, model_real, model_imag),
-                own_half(gains, core),
+                products_ref[c],
+                denom_ref[c],
+                own_half(gains_ref[base + here], core),
             )
 
     def step(i, carry):
@@ -642,7 +669,8 @@
 def second_kernel(
     base, core_ref, spectra_ref, model_ref, own_ref, other_ref, flags_ref, *refs
 ):
-    visibilities_hbm, updated_hbm, ready_ref, updated_ref, sems, sem = refs[-6:]
+    visibilities_hbm, updated_hbm, ready_ref, updated_ref = refs[-10:-6]
+    turned_ref, products_ref, power_ref, denom_ref, sems, sem = refs[-6:]
     core = core_ref[0]
     share = spectra_ref.shape[0]
     slots, count = ready_ref.shape[:2]
@@ -665,37 +693,45 @@
             for piece in range(pieces):
                 copy(i - slots, slot, piece).wait()
 
-        for c in range(count):
-            here = i * count + c
-            spectra = spectra_ref[here]
-            half = spectra.shape[0] // 2
-            values = spectra.astype(jnp.float32)
-            real = values[:half]
-            imag = values[half:]
-            own_real = own_half(real, core)
-            own_imag = own_half(imag, core)
-            paired = (jnp.concatenate([own_real, own_imag], axis=0) / half).astype(jnp.bfloat16)
-            rotated = (jnp.concatenate([own_imag, -own_real], axis=0) / half).astype(jnp.bfloat16)
-            ready_ref[slot, c, 0] = mxu(paired, spectra, TN).astype(jnp.bfloat16)
-            ready_ref[slot, c, 1] = mxu(rotated, spectra, TN).astype(jnp.bfloat16)
-            if c % size == size - 1:
-                copy(i, slot, c // size).start()
+        channels = [i * count + c for c in range(count)]
+
+        def parts(here):
+            values = spectra_ref[here].astype(jnp.float32)
+            half = values.shape[0] // 2
+            return values[:half], values[half:]
+
+        for c, here in enumerate(channels):
+            real, imag = parts(here)
             own = own_ref[here]
             other = other_ref[here]
             first = jnp.where(core == 0, own, other)
             second = jnp.where(core == 0, other, own)
             gains = jnp.concatenate([first, second], axis=1)
             flags = flags_ref[pl.ds(base + here, 1), :]
-            turned_real, turned_imag, power = gain_terms(real, imag, gains, flags)
+            power_ref[c] = put_turned(turned_ref, c, real, imag, gains, flags)
+        for c, here in enumerate(channels):
+            real, imag = parts(here)
+            frames = real.shape[0]
+            own_real = own_half(real, core)
+            own_imag = own_half(imag, core)
+            paired = jnp.concatenate([own_real, own_imag], axis=0) / frames
+            rotated = jnp.concatenate([own_imag, -own_real], axis=0) / frames
+            spectra = spectra_ref[here]
+            ready_ref[slot, c, 0] = mxu(paired.astype(jnp.bfloat16), spectra, TN).astype(jnp.bfloat16)
+            ready_ref[slot, c, 1] = mxu(rotated.astype(jnp.bfloat16), spectra, TN).astype(jnp.bfloat16)
+            if c % size == size - 1:
+                copy(i, slot, c // size).start()
             model_real = model_ref[here, 0]
             model_imag = model_ref[here, 1]
+            products_ref[c] = modelled(turned_ref, c, model_real, model_imag)
+            denom_ref[c] = denominators(power_ref[c], model_real, model_imag)
+        for c, here in enumerate(channels):
+            real, imag = parts(here)
             updated_ref[here] = updated_gains(
-                (own_real, own_imag),
-                (turned_real, turned_imag),
-                model_real,
-                model_imag,
-                denominators(power, model_real, model_imag),
-                own,
+                (own_half(real, core), own_half(imag, core)),
+                products_ref[c],
+                denom_ref[c],
+                own_ref[here],
             )
         return carry
 
@@ -902,6 +938,10 @@
             input_output_aliases={6: 2},
             scratch_shapes=[
                 pltpu.VMEM((2, owners, max(own.shape[1] - share * frames, SUBLANES), own.shape[2]), jnp.float32),
+                pltpu.VMEM((BLOCK, 2, 2 * frame_count, input_count), jnp.bfloat16),
+                pltpu.VMEM((BLOCK, 2 * frame_count, half_rows), jnp.float32),
+                pltpu.VMEM((BLOCK, 1, input_count), jnp.float32),
+                pltpu.VMEM((BLOCK, 1, half_rows), jnp.float32),
                 pltpu.SemaphoreType.DMA((share // VIS_BLOCK,)),
             ],
             compiler_params=pltpu.CompilerParams(vmem_limit_bytes=UPDATE_LIMIT),
@@ -924,6 +964,10 @@
             scratch_shapes=[
                 pltpu.VMEM((2, BLOCK, 2, half_rows, input_count), jnp.bfloat16),
                 pltpu.VMEM((share, 2, half_rows), jnp.float32),
+                pltpu.VMEM((BLOCK, 2, 2 * frame_count, input_count), jnp.bfloat16),
+                pltpu.VMEM((BLOCK, 2 * frame_count, half_rows), jnp.float32),
+                pltpu.VMEM((BLOCK, 1, input_count), jnp.float32),
+                pltpu.VMEM((BLOCK, 1, half_rows), jnp.float32),
                 pltpu.SemaphoreType.DMA((2, 4)),
                 pltpu.SemaphoreType.DMA,
             ],

time: 83.7 us -> 82.1 us (0.981)
  Pallas kernels: 61.3 us -> 59.6 us
    pallas_call x2, Pallas kernels: 14.8 us -> 13.9 us  [chunk_shards(): pl.pallas_call(functools.partial(first_kernel, times, base), in_specs=[sm...]
where the time goes in v5:
time: 82.1 us; the launch traced here: 81.6 us
  Pallas kernels  59.6 us (73%)
  starting transfers between devices  17.9 us (22%)
  waiting for transfers between devices  3.13 us (4%)
  between operations  1.01 us (1%)
    pallas_call x2, Pallas kernels, chunk_shards(): pl.pallas_call(functools.partial(second_kernel, base), in_specs=[smem] +...  20.3 us
    pallas_call x2, Pallas kernels, chunk_shards(): pl.pallas_call(functools.partial(first_kernel, times, base), in_specs=[sm...  13.9 us
    all_to_all x2, starting transfers between devices, chunk_shards(): own = lax.all_to_all(sent[chunk], ('chan', 'tm'), 0, 0, tiled=True)  12.7 us
    pallas_call x1, Pallas kernels, filtered(): pl.pallas_call(functools.partial(filter_kernel, owners), out_shape=[pltpu...  6.75 us
    pallas_call x2, Pallas kernels, formed_beams(): pl.pallas_call(functools.partial(beams_kernel, base), in_specs=[vmem] * 4...  6.37 us
    pallas_call x2, Pallas kernels, chunk_shards(): pl.pallas_call(functools.partial(model_kernel, base, step, reach), in_spe...  4.43 us
    ppermute x1, starting transfers between devices, from_behind(): return lax.ppermute(block, axis, route)  3.94 us
    pallas_call x1, Pallas kernels, more(): pl.pallas_call(functools.partial(filter_more_kernel, owners, start), out_...  3.83 us
  transfers between devices with their start and end apart: 7, of which 2 were waited for; matrix products, arithmetic and copies ran while one was open for 0% of the time, Pallas kernels for 39%

profile of v5, /device:TPU:0, one launch (start us, length us, event | category | flops | bytes accessed | tf_op | source)
XLA Modules:
  0.0 81.6 jit_solution(3633696502937215231)
XLA Ops:
  0.7 6.7 %filter.1 = (bf16[1408,2048]{1,0:T(8,128)(2,1)}, bf16[8,264,128]{2,1,0:T(8,128)(2,1)}) custom-call(bf16[64,2,8,1024]{3,2,1,0:T(8,128)(2,1)} %bitcast.6, f32[4,1024]{1,0:T(4,128)} %taps_hbm.1, bf16[512,2048]{1,0:T(8,128)(2,1)} %constant.30.clone.table_hbm), custom_call_target="tpu_custom_call" | custom-call | tf_op jit(solution)/shard_map/filter/pallas_call | solution.py:408
  7.4 7.3 %all-to-all-start.1 = ((bf16[8,264,128]{2,1,0:T(8,128)(2,1)}), bf16[8,264,128]{2,1,0:T(8,128)(2,1)S(1)}, u32[]{:S(2)}, u32[]{:S(2)}) async-start(bf16[8,264,128]{2,1,0:T(8,128)(2,1)} %get-tuple-element.32), calls=%async_computation.1 | async-start | bytes 1081344 | tf_op jit(solution)/shard_map/all_to_all | solution.py:907
  14.7 2.7 %spill.1 = bf16[3,320,128]{2,1,0:T(8,128)(2,1)S(1)} custom-call(bf16[1408,2048]{1,0:T(8,128)(2,1)} %get-tuple-element.31.windowed_hbm, bf16[512,2048]{1,0:T(8,128)(2,1)} %constant.30.clone.table_hbm), custom_call_target="tpu_custom_call" | custom-call | tf_op jit(solution)/shard_map/spill/pallas_call | solution.py:433
  17.4 3.9 %collective-permute-start = (bf16[3,320,128]{2,1,0:T(8,128)(2,1)S(1)}, bf16[3,320,128]{2,1,0:T(8,128)(2,1)S(1)}, u32[]{:S(2)}, u32[]{:S(2)}) collective-permute-start(bf16[3,320,128]{2,1,0:T(8,128)(2,1)S(1)} %spill.1), channel_id=1, source_target_pairs={{0,2},{1,3},{4,6},{5,7},{8,10},{9,11},{12,14},{13,15},{16,18},{17,... | collective-permute-start | bytes 737288 | tf_op jit(solution)/shard_map/ppermute | solution.py:23
  21.3 3.8 %filter_more.1.turned_ref = f32[2560,128]{1,0:T(8,128)S(1)} custom-call(bf16[1408,2048]{1,0:T(8,128)(2,1)} %get-tuple-element.31.windowed_hbm, bf16[512,2048]{1,0:T(8,128)(2,1)} %constant.30.clone.table_hbm), custom_call_target="tpu_custom_call" | custom-call | tf_op jit(solution)/shard_map/filter_more/pallas_call | solution.py:447
  25.1 1.5 %collective-permute-done.added_ref = bf16[3,320,128]{2,1,0:T(8,128)(2,1)S(1)} collective-permute-done((bf16[3,320,128]{2,1,0:T(8,128)(2,1)S(1)}, bf16[3,320,128]{2,1,0:T(8,128)(2,1)S(1)}, u32[]{:S(2)}, u32[]{:S(2)}) %collective-permute-start) | collective-permute-done | bytes 245792 | tf_op jit(solution)/shard_map/ppermute | solution.py:23
  26.6 1.3 %added.1 = bf16[8,320,128]{2,1,0:T(8,128)(2,1)} custom-call(f32[2560,128]{1,0:T(8,128)S(1)} %filter_more.1.turned_ref, bf16[3,320,128]{2,1,0:T(8,128)(2,1)S(1)} %collective-permute-done.added_ref), custom_call_target="tpu_custom_call" | custom-call | tf_op jit(solution)/shard_map/added/pallas_call | solution.py:460
  27.9 1.6 %all-to-all-done.1.own_hbm.own_ref = bf16[8,264,128]{2,1,0:T(8,128)(2,1)S(1)} async-done(((bf16[8,264,128]{2,1,0:T(8,128)(2,1)}), bf16[8,264,128]{2,1,0:T(8,128)(2,1)S(1)}, u32[]{:S(2)}, u32[]{:S(2)}) %all-to-all-start.1) | async-done | bytes 540704 | tf_op jit(solution)/shard_map/all_to_all | solution.py:907
  29.5 5.5 %all-to-all-start = ((bf16[8,320,128]{2,1,0:T(8,128)(2,1)}), bf16[8,320,128]{2,1,0:T(8,128)(2,1)S(1)}, u32[]{:S(2)}, u32[]{:S(2)}) async-start(bf16[8,320,128]{2,1,0:T(8,128)(2,1)} %added.1), calls=%async_computation | async-start | bytes 1310720 | tf_op jit(solution)/shard_map/all_to_all | solution.py:907
  35.0 0.0 copy-start.1
  35.0 0.1 collective-permute-start.1
  35.1 2.2 %model.2 = (bf16[24,2,256,512]{3,2,1,0:T(8,128)(2,1)S(1)}, bf16[4,1024,512]{2,1,0:T(8,128)(2,1)S(1)}) custom-call(bf16[8,264,128]{2,1,0:T(8,128)(2,1)S(1)} %all-to-all-done.1.own_hbm.own_ref, bf16[64,2,256,512]{3,2,1,0:T(8,128)(2,1)} %model_hbm.7, s32[1]{0:T(128)} %bitcast.2.centre_ref, s32[2,256]{1,0:T(2,128)S(1)} %copy-done.2), custom_call_target="tpu_custom_call" | custom-call | tf_op jit(solution)/shard_map/model/pallas_call | solution.py:915
  37.4 5.3 %first_update.2 = (bf16[24,32,512]{2,1,0:T(8,128)(2,1)S(1)}, f32[24,2,256]{2,1,0:T(2,128)S(1)}, bf16[24,2,256,512]{3,2,1,0:T(8,128)(2,1)S(1)}) custom-call(s32[1]{0:T(128)} %bitcast.1.core_ref, bf16[8,264,128]{2,1,0:T(8,128)(2,1)S(1)} %all-to-all-done.1.own_hbm.own_ref, ...), custom_call_target="tpu_custom_call", output_to_operand_aliasing={{2}: (6, {})} | custom-call | tf_op jit(solution)/shard_map/first_update/pallas_call | solution.py:929
  42.6 0.5 collective-permute-start.2
  43.2 2.6 %beams.2.refs_0_ = f32[64,16,256]{2,1,0:T(8,128)} custom-call(bf16[24,32,512]{2,1,0:T(8,128)(2,1)S(1)} %get-tuple-element.38.spectra_ref, f32[64,2,512]{2,1,0:T(2,128)S(1)} %copy-done.1, s32[64,512]{1,0:T(8,128)S(1)} %copy-done, bf16[4,1024,512]{2,1,0:T(8,128)(2,1)S(1)} %get-tuple-element.42.table_ref), custom_call_target="tpu_custom_call" | custom-call | tf_op jit(solution)/shard_map/beams/pallas_call | solution.py:860
  45.8 0.0 collective-permute-done.2.other_ref
  45.8 7.9 %second_update.2 = (bf16[64,2,256,512]{3,2,1,0:T(8,128)(2,1)}, f32[64,2,256]{2,1,0:T(2,128)}) custom-call(s32[1]{0:T(128)} %bitcast.1.core_ref, bf16[24,32,512]{2,1,0:T(8,128)(2,1)S(1)} %get-tuple-element.38.spectra_ref, bf16[24,2,256,512]{3,2,1,0:T(8,128)(2,1)S(1)} %get-tuple-element.39.model_ref, f32[24,2,256]{2,1,0:T(2,128)S(1)} %get-tuple-element.40.own_ref, ...), custom_call_target="tpu_custom_call" | custom-call | tf_op jit(solution)/shard_map/second_update/pallas_call | solution.py:956
  53.6 0.0 all-to-all-done.own_hbm.own_ref
  53.7 0.1 collective-permute-start.3
  53.8 2.2 %model.3 = (bf16[40,2,256,512]{3,2,1,0:T(8,128)(2,1)S(1)}, bf16[4,1024,512]{2,1,0:T(8,128)(2,1)S(1)}) custom-call(bf16[8,320,128]{2,1,0:T(8,128)(2,1)S(1)} %all-to-all-done.own_hbm.own_ref, bf16[64,2,256,512]{3,2,1,0:T(8,128)(2,1)} %model_hbm.7, s32[1]{0:T(128)} %bitcast.3.centre_ref, s32[2,256]{1,0:T(2,128)S(1)} %copy-done.2), custom_call_target="tpu_custom_call" | custom-call | tf_op jit(solution)/shard_map/model/pallas_call | solution.py:915
  56.0 8.7 %first_update.3 = (bf16[40,32,512]{2,1,0:T(8,128)(2,1)S(1)}, f32[40,2,256]{2,1,0:T(2,128)S(1)}, bf16[40,2,256,512]{3,2,1,0:T(8,128)(2,1)S(1)}) custom-call(s32[1]{0:T(128)} %bitcast.1.core_ref, bf16[8,320,128]{2,1,0:T(8,128)(2,1)S(1)} %all-to-all-done.own_hbm.own_ref, ...), custom_call_target="tpu_custom_call", output_to_operand_aliasing={{2}: (6, {})} | custom-call | tf_op jit(solution)/shard_map/first_update/pallas_call | solution.py:929
  64.7 0.5 collective-permute-start.4
  65.2 3.8 %beams.3 = f32[64,16,256]{2,1,0:T(8,128)} custom-call(bf16[40,32,512]{2,1,0:T(8,128)(2,1)S(1)} %get-tuple-element.46.spectra_ref, f32[64,2,512]{2,1,0:T(2,128)S(1)} %copy-done.1, s32[64,512]{1,0:T(8,128)S(1)} %copy-done, bf16[4,1024,512]{2,1,0:T(8,128)(2,1)S(1)} %get-tuple-element.53.table_ref, ...), custom_call_target="tpu_custom_call", output_to_operand_aliasing={{}: (4, {})} | custom-call | tf_op jit(solution)/shard_map/beams/pallas_call | solution.py:860
  69.0 12.4 %second_update.3 = (bf16[64,2,256,512]{3,2,1,0:T(8,128)(2,1)}, f32[64,2,256]{2,1,0:T(2,128)}) custom-call(s32[1]{0:T(128)} %bitcast.1.core_ref, bf16[40,32,512]{2,1,0:T(8,128)(2,1)S(1)} %get-tuple-element.46.spectra_ref, bf16[40,2,256,512]{3,2,1,0:T(8,128)(2,1)S(1)} %get-tuple-element.47.model_ref, ...), custom_call_target="tpu_custom_call", output_to_operand_aliasing={{0}: (6, {}), {1}: (7, {})} | custom-call | tf_op jit(solution)/shard_map/second_update/pallas_call | solution.py:956
  (8 shorter events, 0.0 us)
Async XLA Ops:
  0.6 34.5 %copy-start.2 = (s32[2,256]{1,0:T(2,128)S(1)}, s32[2,256]{1,0:T(2,128)}, u32[]{:S(2)}) copy-start(s32[2,256]{1,0:T(2,128)} %steering_ref.1) | copy-start | bytes 6148
  7.4 22.1 %all-to-all-start.1 = ((bf16[8,264,128]{2,1,0:T(8,128)(2,1)}), bf16[8,264,128]{2,1,0:T(8,128)(2,1)S(1)}, u32[]{:S(2)}, u32[]{:S(2)}) async-start(bf16[8,264,128]{2,1,0:T(8,128)(2,1)} %get-tuple-element.32), calls=%async_computation.1 | async-start | bytes 1081344 | tf_op jit(solution)/shard_map/all_to_all | solution.py:907
  17.4 9.3 %collective-permute-start = (bf16[3,320,128]{2,1,0:T(8,128)(2,1)S(1)}, bf16[3,320,128]{2,1,0:T(8,128)(2,1)S(1)}, u32[]{:S(2)}, u32[]{:S(2)}) collective-permute-start(bf16[3,320,128]{2,1,0:T(8,128)(2,1)S(1)} %spill.1), channel_id=1, source_target_pairs={{0,2},{1,3},{4,6},{5,7},{8,10},{9,11},{12,14},{13,15},{16,18},{17,... | collective-permute-start | bytes 737288 | tf_op jit(solution)/shard_map/ppermute | solution.py:23
  29.5 24.1 %all-to-all-start = ((bf16[8,320,128]{2,1,0:T(8,128)(2,1)}), bf16[8,320,128]{2,1,0:T(8,128)(2,1)S(1)}, u32[]{:S(2)}, u32[]{:S(2)}) async-start(bf16[8,320,128]{2,1,0:T(8,128)(2,1)} %added.1), calls=%async_computation | async-start | bytes 1310720 | tf_op jit(solution)/shard_map/all_to_all | solution.py:907
  35.0 2.4 %copy-start = (s32[64,512]{1,0:T(8,128)S(1)}, s32[64,512]{1,0:T(8,128)}, u32[]{:S(2)}) copy-start(s32[64,512]{1,0:T(8,128)} %flags_ref.5) | copy-start | bytes 393220
  35.0 2.4 %copy-start.1 = (f32[64,2,512]{2,1,0:T(2,128)S(1)}, f32[64,2,512]{2,1,0:T(2,128)}, u32[]{:S(2)}) copy-start(f32[64,2,512]{2,1,0:T(2,128)} %gains_ref.3) | copy-start | bytes 786436
  35.0 2.3 %collective-permute-start.1 = (bf16[8,264,128]{2,1,0:T(8,128)(2,1)S(1)}, bf16[8,264,128]{2,1,0:T(8,128)(2,1)S(1)}, u32[]{:S(2)}, u32[]{:S(2)}) collective-permute-start(bf16[8,264,128]{2,1,0:T(8,128)(2,1)S(1)} %all-to-all-done.1.own_hbm.own_ref), channel_id=1, source_target_pairs={{0,1},{1,0},{2,3},{3,2},{4,5},{5,4},{6,7},{7,6},{8,9},{9,8},{10,11... | collective-permute-start | bytes 1622024 | tf_op jit(solution)/shard_map/ppermute | solution.py:911
  42.6 3.1 %collective-permute-start.2 = (f32[24,2,256]{2,1,0:T(2,128)S(1)}, f32[24,2,256]{2,1,0:T(2,128)S(1)}, u32[]{:S(2)}, u32[]{:S(2)}) collective-permute-start(f32[24,2,256]{2,1,0:T(2,128)S(1)} %get-tuple-element.40.own_ref), channel_id=1, source_target_pairs={{0,1},{1,0},{2,3},{3,2},{4,5},{5,4},{6,7},{7,6},{8,9},{9,8},{10,11... | collective-permute-start | bytes 147464 | tf_op jit(solution)/shard_map/ppermute | solution.py:951
  53.7 2.3 %collective-permute-start.3 = (bf16[8,320,128]{2,1,0:T(8,128)(2,1)S(1)}, bf16[8,320,128]{2,1,0:T(8,128)(2,1)S(1)}, u32[]{:S(2)}, u32[]{:S(2)}) collective-permute-start(bf16[8,320,128]{2,1,0:T(8,128)(2,1)S(1)} %all-to-all-done.own_hbm.own_ref), channel_id=1, source_target_pairs={{0,1},{1,0},{2,3},{3,2},{4,5},{5,4},{6,7},{7,6},{8,9},{9,8},{10,11... | collective-permute-start | bytes 1966088 | tf_op jit(solution)/shard_map/ppermute | solution.py:911
  64.7 4.3 %collective-permute-start.4 = (f32[40,2,256]{2,1,0:T(2,128)S(1)}, f32[40,2,256]{2,1,0:T(2,128)S(1)}, u32[]{:S(2)}, u32[]{:S(2)}) collective-permute-start(f32[40,2,256]{2,1,0:T(2,128)S(1)} %get-tuple-element.48.own_ref), channel_id=1, source_target_pairs={{0,1},{1,0},{2,3},{3,2},{4,5},{5,4},{6,7},{7,6},{8,9},{9,8},{10,11... | collective-permute-start | bytes 245768 | tf_op jit(solution)/shard_map/ppermute | solution.py:951

commit v6 on v5

--- a/solution.py
+++ b/solution.py
@@ -667,9 +667,9 @@
 
 
 def second_kernel(
-    base, core_ref, spectra_ref, model_ref, own_ref, other_ref, flags_ref, *refs
+    base, core_ref, spectra_ref, model_ref, own_ref, other_ref, flags_ref, beams_ref, *refs
 ):
-    visibilities_hbm, updated_hbm, ready_ref, updated_ref = refs[-10:-6]
+    visibilities_hbm, updated_hbm, beams_hbm, ready_ref, updated_ref = refs[-11:-6]
     turned_ref, products_ref, power_ref, denom_ref, sems, sem = refs[-6:]
     core = core_ref[0]
     share = spectra_ref.shape[0]
@@ -677,6 +677,8 @@
     pieces = sems.shape[1]
     size = count // pieces
     steps = share // count
+    beams_copy = pltpu.make_async_copy(beams_ref, beams_hbm.at[pl.ds(base, share)], sem.at[0])
+    beams_copy.start()
 
     def copy(i, slot, piece):
         return pltpu.make_async_copy(
@@ -736,12 +738,13 @@
         return carry
 
     lax.fori_loop(0, steps, step, 0)
-    last = pltpu.make_async_copy(updated_ref, updated_hbm.at[pl.ds(base, share)], sem)
+    last = pltpu.make_async_copy(updated_ref, updated_hbm.at[pl.ds(base, share)], sem.at[1])
     last.start()
     for i in range(max(0, steps - slots), steps):
         for piece in range(pieces):
             copy(i, i % slots, piece).wait()
     last.wait()
+    beams_copy.wait()
 
 
 def series_length(reach):
@@ -817,7 +820,7 @@
 
 
 def beams_kernel(base, spectra_ref, gains_ref, flags_ref, table_ref, *refs):
-    power_hbm, power_ref, left_ref, sem = refs[-4:]
+    power_ref, left_ref = refs
     count, doubled, inputs = spectra_ref.shape
     frames = doubled // 2
     scale = 1.0 / math.sqrt(inputs)
@@ -845,32 +848,23 @@
     real = total[:, :beams]
     imag = total[:, beams:]
     power_ref[...] = (real * real + imag * imag).reshape(count, frames, beams)
-    copy = pltpu.make_async_copy(power_ref, power_hbm.at[pl.ds(base, count)], sem)
-    copy.start()
-    copy.wait()
-
-
-def formed_beams(chunk, gains, flags, earlier):
-    base, table, spectra = chunk
+
+
+def formed_beams(base, spectra, table, gains, flags):
     share, doubled, input_count = spectra.shape
     frame_count = doubled // 2
-    beams = table.shape[2] // 2
-    earlier = [] if earlier is None else [earlier]
     vmem = pl.BlockSpec(memory_space=pltpu.VMEM)
     return pl.pallas_call(
         functools.partial(beams_kernel, base),
-        in_specs=[vmem] * 4 + [pl.BlockSpec(memory_space=pl.ANY)] * len(earlier),
-        out_specs=pl.BlockSpec(memory_space=pl.ANY),
-        out_shape=jax.ShapeDtypeStruct((gains.shape[0], frame_count, beams), jnp.float32),
-        input_output_aliases={4: 0} if earlier else {},
+        in_specs=[vmem] * 4,
+        out_specs=vmem,
+        out_shape=jax.ShapeDtypeStruct((share, frame_count, table.shape[2] // 2), jnp.float32),
         scratch_shapes=[
-            pltpu.VMEM((share, frame_count, beams), jnp.float32),
             pltpu.VMEM((table.shape[0], share * frame_count, 2 * input_count), jnp.bfloat16),
-            pltpu.SemaphoreType.DMA,
         ],
         compiler_params=pltpu.CompilerParams(vmem_limit_bytes=UPDATE_LIMIT),
         name="beams",
-    )(spectra, gains, flags, table, *earlier)
+    )(spectra, gains, flags, table)
 
 
 def chunk_shards(samples, window_taps, sky_model, prior_gains, beam_steering, input_flags):
@@ -902,12 +896,10 @@
     visibilities = None
     beam_power = None
     gains_new = None
-    before = None
     for chunk, (base, share) in enumerate(zip(bases, shares)):
         own = lax.all_to_all(sent[chunk], ("chan", "tm"), 0, 0, tiled=True)
-        if before is not None:
-            beam_power = formed_beams(before, gains, flags, beam_power)
-            own, gains_new, beam_power = lax.optimization_barrier((own, gains_new, beam_power))
+        if gains_new is not None:
+            own, gains_new = lax.optimization_barrier((own, gains_new))
         other = lax.ppermute(own, "beam", swap)
         model_shape = (share, *sky_model.shape[1:])
         reach = max(0.5 * (share - 1), 0.5)
@@ -949,17 +941,16 @@
         )(core, own, other, sky_model, gains, flags, model)
         model = pltpu.with_memory_space_constraint(model, pltpu.VMEM)
         gains_other = lax.ppermute(gains_own, "beam", swap)
-        before = (base, table, spectra)
-        if chunk == len(shares) - 1:
-            beam_power = formed_beams(before, gains, flags, beam_power)
-        earlier = [] if visibilities is None else [visibilities, gains_new]
-        visibilities, gains_new = pl.pallas_call(
+        powers = formed_beams(base, spectra, table, gains, flags)
+        earlier = [] if visibilities is None else [visibilities, gains_new, beam_power]
+        visibilities, gains_new, beam_power = pl.pallas_call(
             functools.partial(second_kernel, base),
-            in_specs=[smem] + [vmem] * 5 + [anywhere] * len(earlier),
-            out_specs=[anywhere, anywhere],
+            in_specs=[smem] + [vmem] * 6 + [anywhere] * len(earlier),
+            out_specs=[anywhere] * 3,
             out_shape=[
                 jax.ShapeDtypeStruct(sky_model.shape, jnp.bfloat16),
                 jax.ShapeDtypeStruct((chan_local, 2, half_rows), jnp.float32),
+                jax.ShapeDtypeStruct((chan_local, frame_count, beams), jnp.float32),
             ],
             scratch_shapes=[
                 pltpu.VMEM((2, BLOCK, 2, half_rows, input_count), jnp.bfloat16),
@@ -969,12 +960,12 @@
                 pltpu.VMEM((BLOCK, 1, input_count), jnp.float32),
                 pltpu.VMEM((BLOCK, 1, half_rows), jnp.float32),
                 pltpu.SemaphoreType.DMA((2, 4)),
-                pltpu.SemaphoreType.DMA,
+                pltpu.SemaphoreType.DMA((2,)),
             ],
-            input_output_aliases={6: 0, 7: 1} if earlier else {},
+            input_output_aliases={7: 0, 8: 1, 9: 2} if earlier else {},
             compiler_params=pltpu.CompilerParams(vmem_limit_bytes=UPDATE_LIMIT),
             name="second_update",
-        )(core, spectra, model, gains_own, gains_other, flags, *earlier)
+        )(core, spectra, model, gains_own, gains_other, flags, powers, *earlier)
     return (
         visibilities,
         gains_new,

time: 82.1 us -> 80.5 us (0.981)
  Pallas kernels: 59.6 us -> 58 us
    pallas_call x2, Pallas kernels: 6.37 us -> 4.74 us  [formed_beams(): pl.pallas_call(functools.partial(beams_kernel, base), in_specs=[vmem] * 4...]
  transfers between devices with their start and end apart: 7 -> 7, of which waited for: 2 -> 2; matrix products, arithmetic and copies ran while one was open for 0% -> 0% of each run, Pallas kernels for 39% -> 38%
where the time goes in v6:
time: 80.5 us; the launch traced here: 80 us
  Pallas kernels  58 us (72%)
  starting transfers between devices  17.9 us (22%)
  waiting for transfers between devices  3.13 us (4%)
  between operations  1.01 us (1%)
    pallas_call x2, Pallas kernels, chunk_shards(): pl.pallas_call(functools.partial(second_kernel, base), in_specs=[smem] +...  20.4 us
    pallas_call x2, Pallas kernels, chunk_shards(): pl.pallas_call(functools.partial(first_kernel, times, base), in_specs=[sm...  13.9 us
    all_to_all x2, starting transfers between devices, chunk_shards(): own = lax.all_to_all(sent[chunk], ('chan', 'tm'), 0, 0, tiled=True)  12.7 us
    pallas_call x1, Pallas kernels, filtered(): pl.pallas_call(functools.partial(filter_kernel, owners), out_shape=[pltpu...  6.75 us
    pallas_call x2, Pallas kernels, formed_beams(): pl.pallas_call(functools.partial(beams_kernel, base), in_specs=[vmem] * 4...  4.74 us
    pallas_call x2, Pallas kernels, chunk_shards(): pl.pallas_call(functools.partial(model_kernel, base, step, reach), in_spe...  4.43 us
    ppermute x1, starting transfers between devices, from_behind(): return lax.ppermute(block, axis, route)  3.94 us
    pallas_call x1, Pallas kernels, more(): pl.pallas_call(functools.partial(filter_more_kernel, owners, start), out_...  3.83 us
  transfers between devices with their start and end apart: 7, of which 2 were waited for; matrix products, arithmetic and copies ran while one was open for 0% of the time, Pallas kernels for 38%

profile of v6, /device:TPU:0, one launch (start us, length us, event | category | flops | bytes accessed | tf_op | source)
XLA Modules:
  0.0 80.0 jit_solution(15345404878890801001)
XLA Ops:
  0.7 6.7 %filter.1 = (bf16[1408,2048]{1,0:T(8,128)(2,1)}, bf16[8,264,128]{2,1,0:T(8,128)(2,1)}) custom-call(bf16[64,2,8,1024]{3,2,1,0:T(8,128)(2,1)} %bitcast.5, f32[4,1024]{1,0:T(4,128)} %taps_hbm.1, bf16[512,2048]{1,0:T(8,128)(2,1)} %constant.30.clone.table_hbm), custom_call_target="tpu_custom_call" | custom-call | tf_op jit(solution)/shard_map/filter/pallas_call | solution.py:408
  7.4 7.3 %all-to-all-start.1 = ((bf16[8,264,128]{2,1,0:T(8,128)(2,1)}), bf16[8,264,128]{2,1,0:T(8,128)(2,1)S(1)}, u32[]{:S(2)}, u32[]{:S(2)}) async-start(bf16[8,264,128]{2,1,0:T(8,128)(2,1)} %get-tuple-element.33), calls=%async_computation.1 | async-start | bytes 1081344 | tf_op jit(solution)/shard_map/all_to_all | solution.py:900
  14.7 2.7 %spill.1 = bf16[3,320,128]{2,1,0:T(8,128)(2,1)S(1)} custom-call(bf16[1408,2048]{1,0:T(8,128)(2,1)} %get-tuple-element.32.windowed_hbm, bf16[512,2048]{1,0:T(8,128)(2,1)} %constant.30.clone.table_hbm), custom_call_target="tpu_custom_call" | custom-call | tf_op jit(solution)/shard_map/spill/pallas_call | solution.py:433
  17.4 3.9 %collective-permute-start = (bf16[3,320,128]{2,1,0:T(8,128)(2,1)S(1)}, bf16[3,320,128]{2,1,0:T(8,128)(2,1)S(1)}, u32[]{:S(2)}, u32[]{:S(2)}) collective-permute-start(bf16[3,320,128]{2,1,0:T(8,128)(2,1)S(1)} %spill.1), channel_id=1, source_target_pairs={{0,2},{1,3},{4,6},{5,7},{8,10},{9,11},{12,14},{13,15},{16,18},{17,... | collective-permute-start | bytes 737288 | tf_op jit(solution)/shard_map/ppermute | solution.py:23
  21.3 3.8 %filter_more.1.turned_ref = f32[2560,128]{1,0:T(8,128)S(1)} custom-call(bf16[1408,2048]{1,0:T(8,128)(2,1)} %get-tuple-element.32.windowed_hbm, bf16[512,2048]{1,0:T(8,128)(2,1)} %constant.30.clone.table_hbm), custom_call_target="tpu_custom_call" | custom-call | tf_op jit(solution)/shard_map/filter_more/pallas_call | solution.py:447
  25.1 1.5 %collective-permute-done.added_ref = bf16[3,320,128]{2,1,0:T(8,128)(2,1)S(1)} collective-permute-done((bf16[3,320,128]{2,1,0:T(8,128)(2,1)S(1)}, bf16[3,320,128]{2,1,0:T(8,128)(2,1)S(1)}, u32[]{:S(2)}, u32[]{:S(2)}) %collective-permute-start) | collective-permute-done | bytes 245792 | tf_op jit(solution)/shard_map/ppermute | solution.py:23
  26.6 1.3 %added.1 = bf16[8,320,128]{2,1,0:T(8,128)(2,1)} custom-call(f32[2560,128]{1,0:T(8,128)S(1)} %filter_more.1.turned_ref, bf16[3,320,128]{2,1,0:T(8,128)(2,1)S(1)} %collective-permute-done.added_ref), custom_call_target="tpu_custom_call" | custom-call | tf_op jit(solution)/shard_map/added/pallas_call | solution.py:460
  27.9 1.6 %all-to-all-done.1.own_hbm.own_ref = bf16[8,264,128]{2,1,0:T(8,128)(2,1)S(1)} async-done(((bf16[8,264,128]{2,1,0:T(8,128)(2,1)}), bf16[8,264,128]{2,1,0:T(8,128)(2,1)S(1)}, u32[]{:S(2)}, u32[]{:S(2)}) %all-to-all-start.1) | async-done | bytes 540704 | tf_op jit(solution)/shard_map/all_to_all | solution.py:900
  29.5 5.5 %all-to-all-start = ((bf16[8,320,128]{2,1,0:T(8,128)(2,1)}), bf16[8,320,128]{2,1,0:T(8,128)(2,1)S(1)}, u32[]{:S(2)}, u32[]{:S(2)}) async-start(bf16[8,320,128]{2,1,0:T(8,128)(2,1)} %added.1), calls=%async_computation | async-start | bytes 1310720 | tf_op jit(solution)/shard_map/all_to_all | solution.py:900
  35.0 0.0 copy-start.1
  35.0 0.1 collective-permute-start.1
  35.1 2.2 %model.2 = (bf16[24,2,256,512]{3,2,1,0:T(8,128)(2,1)S(1)}, bf16[4,1024,512]{2,1,0:T(8,128)(2,1)S(1)}) custom-call(bf16[8,264,128]{2,1,0:T(8,128)(2,1)S(1)} %all-to-all-done.1.own_hbm.own_ref, bf16[64,2,256,512]{3,2,1,0:T(8,128)(2,1)} %model_hbm.7, s32[1]{0:T(128)} %bitcast.2.centre_ref, s32[2,256]{1,0:T(2,128)S(1)} %copy-done.2), custom_call_target="tpu_custom_call" | custom-call | tf_op jit(solution)/shard_map/model/pallas_call | solution.py:907
  37.4 5.3 %first_update.2 = (bf16[24,32,512]{2,1,0:T(8,128)(2,1)S(1)}, f32[24,2,256]{2,1,0:T(2,128)S(1)}, bf16[24,2,256,512]{3,2,1,0:T(8,128)(2,1)S(1)}) custom-call(s32[1]{0:T(128)} %bitcast.1.core_ref, bf16[8,264,128]{2,1,0:T(8,128)(2,1)S(1)} %all-to-all-done.1.own_hbm.own_ref, ...), custom_call_target="tpu_custom_call", output_to_operand_aliasing={{2}: (6, {})} | custom-call | tf_op jit(solution)/shard_map/first_update/pallas_call | solution.py:921
  42.6 0.5 collective-permute-start.2
  43.2 1.8 %beams.2.beams_ref = f32[24,16,256]{2,1,0:T(8,128)S(1)} custom-call(bf16[24,32,512]{2,1,0:T(8,128)(2,1)S(1)} %get-tuple-element.39.spectra_ref, f32[64,2,512]{2,1,0:T(2,128)S(1)} %copy-done.1, s32[64,512]{1,0:T(8,128)S(1)} %copy-done, bf16[4,1024,512]{2,1,0:T(8,128)(2,1)S(1)} %get-tuple-element.42.table_ref), custom_call_target="tpu_custom_call" | custom-call | tf_op jit(solution)/shard_map/beams/pallas_call | solution.py:857
  45.0 0.0 collective-permute-done.2.other_ref
  45.0 7.9 %second_update.2 = (bf16[64,2,256,512]{3,2,1,0:T(8,128)(2,1)}, f32[64,2,256]{2,1,0:T(2,128)}, f32[64,16,256]{2,1,0:T(8,128)}) custom-call(s32[1]{0:T(128)} %bitcast.1.core_ref, bf16[24,32,512]{2,1,0:T(8,128)(2,1)S(1)} %get-tuple-element.39.spectra_ref, bf16[24,2,256,512]{3,2,1,0:T(8,128)(2,1)S(1)} %get-tuple-element.40.model_ref, ...), custom_call_target="tpu_custom_call" | custom-call | tf_op jit(solution)/shard_map/second_update/pallas_call | solution.py:946
  52.9 0.0 all-to-all-done.own_hbm.own_ref
  52.9 0.1 collective-permute-start.3
  53.0 2.2 %model.3 = (bf16[40,2,256,512]{3,2,1,0:T(8,128)(2,1)S(1)}, bf16[4,1024,512]{2,1,0:T(8,128)(2,1)S(1)}) custom-call(bf16[8,320,128]{2,1,0:T(8,128)(2,1)S(1)} %all-to-all-done.own_hbm.own_ref, bf16[64,2,256,512]{3,2,1,0:T(8,128)(2,1)} %model_hbm.7, s32[1]{0:T(128)} %bitcast.3.centre_ref, s32[2,256]{1,0:T(2,128)S(1)} %copy-done.2), custom_call_target="tpu_custom_call" | custom-call | tf_op jit(solution)/shard_map/model/pallas_call | solution.py:907
  55.2 8.7 %first_update.3 = (bf16[40,32,512]{2,1,0:T(8,128)(2,1)S(1)}, f32[40,2,256]{2,1,0:T(2,128)S(1)}, bf16[40,2,256,512]{3,2,1,0:T(8,128)(2,1)S(1)}) custom-call(s32[1]{0:T(128)} %bitcast.1.core_ref, bf16[8,320,128]{2,1,0:T(8,128)(2,1)S(1)} %all-to-all-done.own_hbm.own_ref, ...), custom_call_target="tpu_custom_call", output_to_operand_aliasing={{2}: (6, {})} | custom-call | tf_op jit(solution)/shard_map/first_update/pallas_call | solution.py:921
  63.9 0.5 collective-permute-start.4
  64.5 2.9 %beams.3.beams_ref = f32[40,16,256]{2,1,0:T(8,128)S(1)} custom-call(bf16[40,32,512]{2,1,0:T(8,128)(2,1)S(1)} %get-tuple-element.47.spectra_ref, f32[64,2,512]{2,1,0:T(2,128)S(1)} %copy-done.1, s32[64,512]{1,0:T(8,128)S(1)} %copy-done, bf16[4,1024,512]{2,1,0:T(8,128)(2,1)S(1)} %get-tuple-element.50.table_ref), custom_call_target="tpu_custom_call" | custom-call | tf_op jit(solution)/shard_map/beams/pallas_call | solution.py:857
  67.4 12.5 %second_update.3 = (bf16[64,2,256,512]{3,2,1,0:T(8,128)(2,1)}, f32[64,2,256]{2,1,0:T(2,128)}, f32[64,16,256]{2,1,0:T(8,128)}) custom-call(s32[1]{0:T(128)} %bitcast.1.core_ref, bf16[40,32,512]{2,1,0:T(8,128)(2,1)S(1)} %get-tuple-element.47.spectra_ref, ...), custom_call_target="tpu_custom_call", output_to_operand_aliasing={{0}: (7, {}), {1}: (8, {}), {2}: (9, {})} | custom-call | tf_op jit(solution)/shard_map/second_update/pallas_call | solution.py:946
  (8 shorter events, 0.0 us)
Async XLA Ops:
  0.6 34.5 %copy-start.2 = (s32[2,256]{1,0:T(2,128)S(1)}, s32[2,256]{1,0:T(2,128)}, u32[]{:S(2)}) copy-start(s32[2,256]{1,0:T(2,128)} %steering_ref.1) | copy-start | bytes 6148
  7.4 22.1 %all-to-all-start.1 = ((bf16[8,264,128]{2,1,0:T(8,128)(2,1)}), bf16[8,264,128]{2,1,0:T(8,128)(2,1)S(1)}, u32[]{:S(2)}, u32[]{:S(2)}) async-start(bf16[8,264,128]{2,1,0:T(8,128)(2,1)} %get-tuple-element.33), calls=%async_computation.1 | async-start | bytes 1081344 | tf_op jit(solution)/shard_map/all_to_all | solution.py:900
  17.4 9.3 %collective-permute-start = (bf16[3,320,128]{2,1,0:T(8,128)(2,1)S(1)}, bf16[3,320,128]{2,1,0:T(8,128)(2,1)S(1)}, u32[]{:S(2)}, u32[]{:S(2)}) collective-permute-start(bf16[3,320,128]{2,1,0:T(8,128)(2,1)S(1)} %spill.1), channel_id=1, source_target_pairs={{0,2},{1,3},{4,6},{5,7},{8,10},{9,11},{12,14},{13,15},{16,18},{17,... | collective-permute-start | bytes 737288 | tf_op jit(solution)/shard_map/ppermute | solution.py:23
  29.5 23.4 %all-to-all-start = ((bf16[8,320,128]{2,1,0:T(8,128)(2,1)}), bf16[8,320,128]{2,1,0:T(8,128)(2,1)S(1)}, u32[]{:S(2)}, u32[]{:S(2)}) async-start(bf16[8,320,128]{2,1,0:T(8,128)(2,1)} %added.1), calls=%async_computation | async-start | bytes 1310720 | tf_op jit(solution)/shard_map/all_to_all | solution.py:900
  35.0 2.4 %copy-start = (s32[64,512]{1,0:T(8,128)S(1)}, s32[64,512]{1,0:T(8,128)}, u32[]{:S(2)}) copy-start(s32[64,512]{1,0:T(8,128)} %flags_ref.5) | copy-start | bytes 393220
  35.0 2.4 %copy-start.1 = (f32[64,2,512]{2,1,0:T(2,128)S(1)}, f32[64,2,512]{2,1,0:T(2,128)}, u32[]{:S(2)}) copy-start(f32[64,2,512]{2,1,0:T(2,128)} %gains_ref.3) | copy-start | bytes 786436
  35.0 2.3 %collective-permute-start.1 = (bf16[8,264,128]{2,1,0:T(8,128)(2,1)S(1)}, bf16[8,264,128]{2,1,0:T(8,128)(2,1)S(1)}, u32[]{:S(2)}, u32[]{:S(2)}) collective-permute-start(bf16[8,264,128]{2,1,0:T(8,128)(2,1)S(1)} %all-to-all-done.1.own_hbm.own_ref), channel_id=1, source_target_pairs={{0,1},{1,0},{2,3},{3,2},{4,5},{5,4},{6,7},{7,6},{8,9},{9,8},{10,11... | collective-permute-start | bytes 1622024 | tf_op jit(solution)/shard_map/ppermute | solution.py:903
  42.6 2.4 %collective-permute-start.2 = (f32[24,2,256]{2,1,0:T(2,128)S(1)}, f32[24,2,256]{2,1,0:T(2,128)S(1)}, u32[]{:S(2)}, u32[]{:S(2)}) collective-permute-start(f32[24,2,256]{2,1,0:T(2,128)S(1)} %get-tuple-element.41.own_ref), channel_id=1, source_target_pairs={{0,1},{1,0},{2,3},{3,2},{4,5},{5,4},{6,7},{7,6},{8,9},{9,8},{10,11... | collective-permute-start | bytes 147464 | tf_op jit(solution)/shard_map/ppermute | solution.py:943
  52.9 2.3 %collective-permute-start.3 = (bf16[8,320,128]{2,1,0:T(8,128)(2,1)S(1)}, bf16[8,320,128]{2,1,0:T(8,128)(2,1)S(1)}, u32[]{:S(2)}, u32[]{:S(2)}) collective-permute-start(bf16[8,320,128]{2,1,0:T(8,128)(2,1)S(1)} %all-to-all-done.own_hbm.own_ref), channel_id=1, source_target_pairs={{0,1},{1,0},{2,3},{3,2},{4,5},{5,4},{6,7},{7,6},{8,9},{9,8},{10,11... | collective-permute-start | bytes 1966088 | tf_op jit(solution)/shard_map/ppermute | solution.py:903
  63.9 3.4 %collective-permute-start.4 = (f32[40,2,256]{2,1,0:T(2,128)S(1)}, f32[40,2,256]{2,1,0:T(2,128)S(1)}, u32[]{:S(2)}, u32[]{:S(2)}) collective-permute-start(f32[40,2,256]{2,1,0:T(2,128)S(1)} %get-tuple-element.49.own_ref), channel_id=1, source_target_pairs={{0,1},{1,0},{2,3},{3,2},{4,5},{5,4},{6,7},{7,6},{8,9},{9,8},{10,11... | collective-permute-start | bytes 245768 | tf_op jit(solution)/shard_map/ppermute | solution.py:943
